TPU v7x, 32 devices: a whole 2x2x4 slice. The times are simulated.
32 devices in a mesh: section: 2 (over x), dp: 16 (over z, y, core).
Axes of the slice: x: 2, y: 2, z: 4, core: 2. Of those that a mesh axis runs over, the one named last changes fastest.
Arguments:
- entering_tokens: bfloat16 [4, 16, 256, 384], P(None, 'dp'), may hold values from -6 to 6
- output_sensitivity: bfloat16 [4, 16, 256, 384], P(None, 'dp'), may hold values from -6 to 6
- picture_tile_extents: int32 [4, 16, 2], P(None, 'dp'), may hold values from 8 to 16
- pointwise_enlarge: bfloat16 [384, 1536], replicated, may hold values from -0.3125 to 0.3125
- enlarge_bias: float32 [1536], replicated, may hold values from -3 to 3
- channelwise_kernel: float32 [9, 1536], replicated, may hold values from -2 to 2
- channelwise_conv_bias: float32 [1536], replicated, may hold values from -3 to 3
- pointwise_contract: bfloat16 [1536, 384], replicated, may hold values from -0.15625 to 0.15625
- convblock_scale: float32 [384], replicated, may hold values from 0.1 to 1.9
- convblock_offset: float32 [384], replicated, may hold values from -3 to 3
- attend_scale: float32 [384], replicated, may hold values from 0.1 to 1.9
- attend_offset: float32 [384], replicated, may hold values from -3 to 3
- query_key_proj: bfloat16 [384, 1152], replicated, may hold values from -0.3125 to 0.3125
- heads_output_proj: bfloat16 [384, 384], replicated, may hold values from -3.5 to 3.5
- heads_output_bias: float32 [384], replicated, may hold values from -3 to 3
- feedforward_scale: float32 [384], replicated, may hold values from 0.1 to 1.9
- feedforward_offset: float32 [384], replicated, may hold values from -3 to 3
- feedforward_enlarge: bfloat16 [384, 1536], replicated, may hold values from -0.3125 to 0.3125
- feedforward_enlarge_bias: float32 [1536], replicated, may hold values from -3 to 3
- feedforward_contract: bfloat16 [1536, 384], replicated, may hold values from -0.15625 to 0.15625
- contract_bias: float32 [384], replicated, may hold values from -3 to 3
Outputs:
- section_ends: bfloat16 [2, 4, 16, 256, 384], P('section', None, 'dp')
- root_means: float32 [2, 4, 16], P('section', None, 'dp')
- expander_grad: float32 [384, 1536], replicated
- upshift_grad: float32 [1536], replicated
- depthwise_grad: float32 [9, 1536], replicated
- depthshift_grad: float32 [1536], replicated
- projector_grad: float32 [1536, 384], replicated
- postgain_grad: float32 [384], replicated
- postshift_grad: float32 [384], replicated
- pregain_grad: float32 [384], replicated
- preshift_grad: float32 [384], replicated
- attention_grad: float32 [384, 1152], replicated
- mixing_grad: float32 [384, 384], replicated
- mixshift_grad: float32 [384], replicated
- midgain_grad: float32 [384], replicated
- midshift_grad: float32 [384], replicated
- widener_grad: float32 [384, 1536], replicated
- wideshift_grad: float32 [1536], replicated
- narrower_grad: float32 [1536, 384], replicated
- narrowshift_grad: float32 [384], replicated
Inputs may be any that keep to these rules, and one draw needn't show every extreme that they name: Image (m, i) occupies the slots of the first picture_tile_extents[m, i, 0] rows and first picture_tile_extents[m, i, 1] columns of its 16 x 16 grid.
All inputs are finite; a program needn't handle non-finite values.
Results may differ from a plain program's by a relative error of at most 0.015.
Values may be sent and summed in bfloat16 or wider, within the bound.
No kernel may reach another device: no remote copies, remote signals or barrier semaphores. Data moves between devices by JAX's collectives and lax.ppermute only.
A program may use at most 256 MiB of HBM per device.

v0:
```python
import functools
import math

import jax
import jax.numpy as jnp
from jax import lax
from jax.experimental import pallas as pl
from jax.experimental.pallas import tpu as pltpu
from jax.sharding import PartitionSpec as P

HEADS = 6
SIDE = 16
SLOTS = SIDE * SIDE
EPSILON = 1e-05
BLOCKED = -1000000000.0
LANES = 128
BLOCK = 256
FIXED = 4
SQUARE = 4
ROW = 4
PIECE = 144
HEIGHT = 48
ACROSS = PIECE // HEIGHT
SWAPPED = (0, 2, 1, 3)
BF16 = jnp.bfloat16
F32 = jnp.float32


def dot_nn(left, right):
    return jnp.dot(left, right, preferred_element_type=F32)


def dot_nt(left, right):
    return lax.dot_general(left, right, (((1,), (1,)), ((), ())), preferred_element_type=F32)


def dot_tn(left, right):
    return lax.dot_general(left, right, (((0,), (0,)), ((), ())), preferred_element_type=F32)


def norm_parts(values):
    centered = values - jnp.mean(values, axis=-1, keepdims=True)
    inverse = lax.rsqrt(jnp.mean(centered * centered, axis=-1, keepdims=True) + EPSILON)
    return centered * inverse, inverse


def norm_reverse(upstream, scaled, inverse, gain):
    lifted = upstream * gain
    return inverse * (
        lifted
        - jnp.mean(lifted, axis=-1, keepdims=True)
        - scaled * jnp.mean(lifted * scaled, axis=-1, keepdims=True)
    )


def across(vector):
    return vector[...].reshape(1, -1)


def own_share(tokens, numbers, rows):
    share = rows // (tokens.shape[1] * tokens.shape[2])
    return tokens[pl.ds(numbers[0, 0] * share, share)].reshape(rows, tokens.shape[3])


def total_rows(values):
    return jnp.sum(values, axis=0, keepdims=True)


def extent(numbers, image, local, side):
    micros, images = numbers.shape[1] - FIXED, numbers.shape[0] // 2
    first = numbers[0, 0] * (micros // 2) if local else 0
    return numbers[image % images * 2 + side, FIXED + first + image // images]


def valid_column(numbers, image):
    slot = lax.broadcasted_iota(jnp.int32, (SLOTS, 1), 0)
    height, width = (extent(numbers, image, True, side) for side in range(2))
    inside = (slot // SIDE < height) & (slot % SIDE < width)
    return inside.astype(F32)


def valid_rows(numbers, images):
    return jnp.concatenate([valid_column(numbers, image) for image in range(images)], axis=0)


def column_shifts(row, first_column, last_column):
    before = jnp.where(first_column, 0.0, pltpu.roll(row, 1, 0))
    after = jnp.where(last_column, 0.0, pltpu.roll(row, SIDE - 1, 0))
    return before, after


def conv_ahead_kernel(
    numbers, tokens, enlarge, enlarge_bias, taps, taps_bias, contract, gain, shift,
    sent, expanded, slope, active, projected, grid_cells,
):
    rows = sent.shape[0]
    images = rows // SLOTS
    width = sent.shape[1]
    channels = enlarge.shape[1]
    local_in = own_share(tokens, numbers, rows)
    valid = valid_rows(numbers, images)
    column = lax.broadcasted_iota(jnp.int32, (SIDE, BLOCK), 0)
    first_column, last_column = column == 0, column == SIDE - 1
    total = jnp.zeros((rows, width), F32)
    for start in range(0, channels, BLOCK):
        part = slice(start, start + BLOCK)
        cells = (dot_nn(local_in, enlarge[:, part]) + enlarge_bias[part].reshape(1, -1)) * valid
        grid_cells[...] = cells
        expanded[:, part] = cells.astype(BF16)
        kernel = [taps[tap : tap + 1, part] for tap in range(9)]
        bias = taps_bias[part].reshape(1, -1)
        for image in range(images):
            base = image * SLOTS
            above = here = None
            for line in range(SIDE + 1):
                if line < SIDE:
                    row = grid_cells[base + line * SIDE : base + (line + 1) * SIDE, :]
                    before, after = column_shifts(row, first_column, last_column)
                    sums = [
                        before * kernel[3 * a] + row * kernel[3 * a + 1] + after * kernel[3 * a + 2]
                        for a in range(3)
                    ]
                if line > 0:
                    convolved = above + sums[2] if line < SIDE else above
                    gate = jax.nn.sigmoid(convolved)
                    lit = convolved * gate
                    place = slice(base + (line - 1) * SIDE, base + line * SIDE)
                    active[place, part] = lit.astype(BF16)
                    slope[place, part] = (gate + lit * (1.0 - gate)).astype(BF16)
                if line < SIDE:
                    above = (here if line > 0 else bias) + sums[1]
                    here = bias + sums[0]
        total = total + dot_nn(active[:, part], contract[part, :])
    projected[...] = total
    scaled, _ = norm_parts(total)
    sent[...] = (local_in.astype(F32) + scaled * across(gain) + across(shift)).astype(BF16)


def head_lanes(width):
    return lax.broadcasted_iota(jnp.int32, (1, width), 1)


def attend_ahead_kernel(
    numbers, sent, gain, shift, mixing_in, mixing_out, mixing_bias,
    qkv, weights, context, middle,
):
    rows, width = sent.shape
    images = rows // SLOTS
    head = width // HEADS
    factor = 1.0 / math.sqrt(head)
    entering = sent[...].astype(F32)
    scaled, _ = norm_parts(entering)
    normed = (scaled * across(gain) + across(shift)).astype(BF16)
    for start in range(0, 3 * width, width):
        part = slice(start, start + width)
        qkv[:, part] = dot_nn(normed, mixing_in[:, part]).astype(BF16)
    pair = 2 * head
    lane = head_lanes(pair)
    for image in range(images):
        valid = valid_column(numbers, image) > 0.5
        place = slice(image * SLOTS, (image + 1) * SLOTS)
        for couple in range(HEADS // 2):
            at = couple * pair
            queries = qkv[place, at : at + pair]
            keys = qkv[place, width + at : width + at + pair]
            values = qkv[place, 2 * width + at : 2 * width + at + pair]
            gathered = []
            for side in range(2):
                own = (lane >= side * head) & (lane < (side + 1) * head)
                scores = dot_nt(jnp.where(own, keys, jnp.zeros_like(keys)), queries) * factor
                scores = jnp.where(valid, scores, BLOCKED)
                powers = jnp.exp(scores - jnp.max(scores, axis=0, keepdims=True))
                soft = powers * (1.0 / jnp.sum(powers, axis=0, keepdims=True))
                low = soft.astype(BF16)
                weights[image * HEADS + couple * 2 + side] = low
                gathered.append(dot_tn(low, values))
            context[place, at : at + pair] = jnp.where(lane < head, *gathered).astype(BF16)
    middle[...] = entering + dot_nn(context[...], mixing_out[...]) + across(mixing_bias)


def place_tall(pieces, grad, first_row, offset):
    for low in range(first_row, first_row + grad.shape[0], 16):
        piece, inside = low // HEIGHT, low % HEIGHT
        core, square, row = piece // (SQUARE * ROW), piece // ROW % SQUARE, piece % ROW
        for lane in range(ACROSS):
            at = offset + lane * HEIGHT + inside
            pieces[core, square, row, at : at + 16, :] = grad[
                low - first_row : low - first_row + 16, lane * LANES : (lane + 1) * LANES
            ]


def place_wide(pieces, grad, first_lane, offset, first_row=0):
    for block in range(grad.shape[0] // HEIGHT):
        for lane in range(grad.shape[1] // LANES):
            row, inside = (first_lane + lane) // ACROSS, (first_lane + lane) % ACROSS
            at = offset + inside * HEIGHT
            pieces[block // SQUARE, block % SQUARE, row - first_row, at : at + HEIGHT, :] = grad[
                block * HEIGHT : (block + 1) * HEIGHT, lane * LANES : (lane + 1) * LANES
            ]


def square_at(numbers, core, step):
    return numbers[0, 2] ^ jnp.where(core == 0, step, SWAPPED[step])


def row_at(numbers, step):
    return step % 2 * 2 + (numbers[0, 3] % 2 ^ step // 2)


def hand_out(numbers, pieces, keep, send):
    for target, core in ((keep, numbers[0, 1]), (send, 1 - numbers[0, 1])):
        for step in range(SQUARE):
            square = square_at(numbers, core, step)
            for along in range(ROW):
                target[step * ROW + along] = pieces[core, square, row_at(numbers, along)]


def mlp_kernel(
    numbers, middle, sensitivity, gain, shift, enlarge, enlarge_bias, contract, contract_bias,
    output, grad_middle, keep, send, small, wide_small, blocks,
):
    rows, width = middle.shape
    images = rows // SLOTS
    hidden_width = enlarge.shape[1]
    valid = valid_rows(numbers, images)
    center = middle[...]
    scaled, inverse = norm_parts(center)
    hidden = (scaled * across(gain) + across(shift)).astype(BF16)
    grad_out = own_share(sensitivity, numbers, rows).astype(F32) * valid
    out_low = grad_out.astype(BF16)
    total = jnp.zeros((rows, width), F32)
    grad_hidden = jnp.zeros((rows, width), F32)
    for start in range(0, hidden_width, BLOCK):
        part = slice(start, start + BLOCK)
        widened = dot_nn(hidden, enlarge[:, part]) + enlarge_bias[part].reshape(1, -1)
        normal_cdf = 0.5 * (1.0 + lax.erf(widened * (1.0 / math.sqrt(2.0))))
        normal_pdf = jnp.exp(-0.5 * widened * widened) * (1.0 / math.sqrt(2.0 * math.pi))
        activated = (widened * normal_cdf).astype(BF16)
        total = total + dot_nn(activated, contract[part, :])
        grad_wide = dot_nt(out_low, contract[part, :]) * (normal_cdf + widened * normal_pdf)
        wide_small[:, part] = total_rows(grad_wide)
        wide_low = grad_wide.astype(BF16)
        place_tall(blocks, dot_tn(activated, out_low).astype(BF16), start, 0)
        place_wide(blocks, dot_tn(hidden, wide_low).astype(BF16), start // LANES, PIECE)
        grad_hidden = grad_hidden + dot_nt(wide_low, enlarge[:, part])
    output[...] = ((center + total + across(contract_bias)) * valid).astype(BF16)
    gradient = grad_out + norm_reverse(grad_hidden, scaled, inverse, across(gain))
    grad_middle[...] = gradient
    small[0:1, :] = total_rows(grad_out)
    small[1:2, :] = total_rows(grad_hidden * scaled)
    small[2:3, :] = total_rows(grad_hidden)
    small[3:4, :] = total_rows(gradient)
    hand_out(numbers, blocks, keep, send)


def heads_back_kernel(
    grad_middle, qkv, weights, mixing_out, grad_qkv,
):
    rows, width = grad_middle.shape
    images = rows // SLOTS
    head = width // HEADS
    factor = 1.0 / math.sqrt(head)
    grad_context = dot_nt(grad_middle[...].astype(BF16), mixing_out[...]).astype(BF16)
    pair = 2 * head
    lane = head_lanes(pair)
    for image in range(images):
        place = slice(image * SLOTS, (image + 1) * SLOTS)
        for couple in range(HEADS // 2):
            at = couple * pair
            queries = qkv[place, at : at + pair]
            keys = qkv[place, width + at : width + at + pair]
            values = qkv[place, 2 * width + at : 2 * width + at + pair]
            upstream = grad_context[place, at : at + pair]
            parts = []
            for side in range(2):
                own = (lane >= side * head) & (lane < (side + 1) * head)
                low = weights[image * HEADS + couple * 2 + side]
                soft = low.astype(F32)
                grad_values = dot_nn(low, upstream)
                lifted = soft * dot_nt(jnp.where(own, values, jnp.zeros_like(values)), upstream)
                scores_low = (lifted - soft * jnp.sum(lifted, axis=0, keepdims=True)).astype(BF16)
                parts.append(
                    (
                        dot_tn(scores_low, keys) * factor,
                        dot_nn(scores_low, queries) * factor,
                        grad_values,
                    )
                )
            for which in range(3):
                merged = jnp.where(lane < head, parts[0][which], parts[1][which])
                grad_qkv[place, which * width + at : which * width + at + pair] = merged.astype(
                    BF16
                )


def sent_back_kernel(
    numbers, sent, grad_middle, grad_qkv, context, projected, active, gain, shift, mixing_in,
    conv_gain, grad_sent, proj_low, keep, send, small, blocks,
):
    rows, width = sent.shape
    gradient = grad_middle[...]
    entering = sent[...].astype(F32)
    scaled, inverse = norm_parts(entering)
    normed = (scaled * across(gain) + across(shift)).astype(BF16)
    lifted = jnp.zeros((rows, width), F32)
    for which in range(3):
        part = slice(which * width, (which + 1) * width)
        piece = grad_qkv[:, part]
        place_wide(blocks, dot_tn(normed, piece).astype(BF16), which * width // LANES, 0)
        lifted = lifted + dot_nt(piece, mixing_in[:, part])
    mixing = dot_tn(context[...], gradient.astype(BF16)).astype(BF16)
    place_wide(blocks, mixing, 3 * width // LANES, 0)
    grad_low = (gradient + norm_reverse(lifted, scaled, inverse, across(gain))).astype(BF16)
    grad_sent[...] = grad_low
    small[0:1, :] = total_rows(lifted * scaled)
    small[1:2, :] = total_rows(lifted)
    incoming = grad_low.astype(F32)
    scaled, inverse = norm_parts(projected[...])
    low = norm_reverse(incoming, scaled, inverse, across(conv_gain)).astype(BF16)
    proj_low[...] = low
    small[2:3, :] = total_rows(incoming * scaled)
    small[3:4, :] = total_rows(incoming)
    for start in range(0, active.shape[1], BLOCK):
        part = slice(start, start + BLOCK)
        place_tall(blocks, dot_tn(active[:, part], low).astype(BF16), start, PIECE)
    hand_out(numbers, blocks, keep, send)


def conv_part(
    numbers, local_in, proj_low, expanded, slope, enlarge, taps, contract, wide_small, grad_cells,
    blocks, total, first, last, first_row=0,
):
    rows = local_in.shape[0]
    images = rows // SLOTS
    valid = valid_rows(numbers, images)
    column = lax.broadcasted_iota(jnp.int32, (SIDE, LANES), 0)
    first_column, last_column = column == 0, column == SIDE - 1
    for start in range(first, last, BLOCK):
        part = slice(start, start + BLOCK)
        grad_conv = dot_nt(proj_low, contract[part, :]) * slope[:, part].astype(F32)
        wide_small[9:10, part] = total_rows(grad_conv)
        grad_cells[...] = grad_conv
        pieces = []
        for lanes in range(0, BLOCK, LANES):
            chans = slice(start + lanes, start + lanes + LANES)
            kernel = [taps[tap : tap + 1, chans] for tap in range(9)]
            sums = [jnp.zeros((SIDE, LANES), F32) for _ in range(9)]
            outcome = []
            for image in range(images):
                base = image * SLOTS
                shifted = {}
                for line in range(SIDE):
                    for ahead in (line, line + 1):
                        if ahead < SIDE and ahead not in shifted:
                            row = grad_cells[
                                base + ahead * SIDE : base + (ahead + 1) * SIDE,
                                lanes : lanes + LANES,
                            ]
                            before, after = column_shifts(row, first_column, last_column)
                            shifted[ahead] = (after, row, before)
                    place = slice(base + line * SIDE, base + (line + 1) * SIDE)
                    cells = expanded[place, chans].astype(F32)
                    grid = jnp.zeros((SIDE, LANES), F32)
                    for a in range(3):
                        if 0 <= line + 1 - a < SIDE:
                            for b in range(3):
                                moved = shifted[line + 1 - a][b]
                                sums[3 * a + b] = sums[3 * a + b] + cells * moved
                                grid = grid + moved * kernel[3 * a + b]
                    outcome.append(grid)
            for tap in range(9):
                wide_small[tap : tap + 1, chans] = total_rows(sums[tap])
            pieces.append(jnp.concatenate(outcome, axis=0) * valid)
        grad_expanded = jnp.concatenate(pieces, axis=1)
        wide_small[10:11, part] = total_rows(grad_expanded)
        expanded_low = grad_expanded.astype(BF16)
        place_wide(
            blocks, dot_tn(local_in, expanded_low).astype(BF16), start // LANES, 0, first_row
        )
        total = total + dot_nt(expanded_low, enlarge[:, part])
    return total


def conv_back_kernel(
    numbers, tokens, grad_sent, proj_low, expanded, slope, enlarge, taps, contract,
    total, early, early_wide, grad_cells,
):
    rows, width = grad_sent.shape
    total[...] = conv_part(
        numbers, own_share(tokens, numbers, rows), proj_low[...], expanded, slope, enlarge, taps,
        contract, early_wide, grad_cells, early, grad_sent[...].astype(F32), 0,
        enlarge.shape[1] // 2,
    )


def small_rows(small, wide):
    mlp, sent = small
    mlp_wide, conv_wide = wide
    found = []
    for source, rows in ((mlp, 4), (sent, 4), (mlp_wide, 1), (conv_wide, 11)):
        for row in range(rows):
            for at in range(0, source.shape[1], LANES):
                found.append((source, row, at))
    return found


def conv_end_kernel(
    numbers, tokens, total, proj_low, expanded, slope, enlarge, taps, contract, early, early_wide,
    mlp_small, sent_small, mlp_wide, output, own, give, keep, send, pieces, conv_wide, grad_cells,
    short,
):
    rows, width = total.shape
    channels = enlarge.shape[1]
    half = channels // 2
    conv_wide[:, 0:half] = early_wide[:, 0:half]
    pieces[:, :, 0 : ROW // 2, 0:PIECE, :] = early[...]
    gradient = conv_part(
        numbers, own_share(tokens, numbers, rows), proj_low[...], expanded, slope, enlarge, taps,
        contract, conv_wide, grad_cells, pieces, total[...], half, channels,
    ).astype(BF16)
    first = numbers[0, 0] == 0
    own[...] = jnp.where(first, gradient, output[...])
    give[...] = jnp.where(first, output[...], gradient)
    short[...] = jnp.zeros_like(short)
    places = small_rows((mlp_small, sent_small), (mlp_wide, conv_wide))
    for number, (source, row, at) in enumerate(places):
        piece, inside = number // 8, number % 8
        short[piece, inside : inside + 1, :] = source[row : row + 1, at : at + LANES]
    for piece in range(2 * SQUARE * ROW):
        value = short[piece]
        high = value.astype(BF16).astype(F32)
        pair = jnp.concatenate([high, value - high], axis=0).astype(BF16)
        core, square, row = piece // (SQUARE * ROW), piece // ROW % SQUARE, piece % ROW
        pieces[core, square, row, PIECE : PIECE + 16, :] = pair
    hand_out(numbers, pieces, keep, send)


def summed(parts, short):
    total = parts[0].astype(F32)
    for part in parts[1:]:
        total = total + part.astype(F32)
    if not short:
        return total.astype(BF16)
    main = total.shape[0] - short
    value = total[main : main + 8] + total[main + 8 : main + 16]
    high = value.astype(BF16).astype(F32)
    return jnp.concatenate([total[:main], high, value - high], axis=0).astype(BF16)


def halve_kernel(short, keep, arrived, kept, send):
    half = kept.shape[0]
    for step in range(half):
        kept[step] = summed((keep[step], arrived[step]), short)
        send[step] = summed((keep[half + step], arrived[half + step]), short)


def sum_kernel(short, keep, arrived, out):
    for step in range(out.shape[0]):
        out[step] = summed((keep[step], arrived[step]), short)


def join_kernel(short, own, arrived, out):
    half = own.shape[0]
    out[0:half] = own[...]
    out[half:] = arrived[...]


def pieces_of(numbers, parts):
    half = SQUARE * ROW // 2
    for side in range(2):
        core = numbers[0, 1] if side == 0 else 1 - numbers[0, 1]
        for step in range(2 * half):
            square = square_at(numbers, core, step // ROW)
            yield core * SQUARE + square, row_at(numbers, step % ROW), parts[2 * side + step // half], step % half


def write_tall(target, block, row, part, step, offset):
    at = pl.multiple_of((block * ROW + row) * HEIGHT, 16)
    for lane in range(ACROSS):
        low = offset + lane * HEIGHT
        target[pl.ds(at, HEIGHT), lane * LANES : (lane + 1) * LANES] = part[
            step, low : low + HEIGHT, :
        ].astype(F32)


def write_wide(target, block, row, part, step, offset):
    at = pl.multiple_of(block * HEIGHT, 16)
    for lane in range(ACROSS):
        low = offset + lane * HEIGHT
        column = pl.multiple_of((row * ACROSS + lane) * LANES, LANES)
        target[pl.ds(at, HEIGHT), pl.ds(column, LANES)] = part[step, low : low + HEIGHT, :].astype(
            F32
        )


def mlp_end_kernel(numbers, *refs):
    narrower, widener = refs[4:]
    for block, row, part, step in pieces_of(numbers, refs):
        write_tall(narrower, block, row, part, step, 0)
        write_wide(widener, block, row, part, step, PIECE)


def sent_end_kernel(numbers, *refs):
    attention, mixing, projector, joint = refs[4:]
    for block, row, part, step in pieces_of(numbers, refs):
        write_wide(joint, block, row, part, step, 0)
        write_tall(projector, block, row, part, step, PIECE)
    attention[...] = joint[:, : attention.shape[1]]
    mixing[...] = joint[:, attention.shape[1] :]


def conv_all_kernel(numbers, *refs):
    expander, shorts, short = refs[4], refs[5:-1], refs[-1]
    for block, row, part, step in pieces_of(numbers, refs):
        write_wide(expander, block, row, part, step, 0)
        pair = part[step, PIECE : PIECE + 16, :].astype(F32)
        short[pl.ds(pl.multiple_of((block * ROW + row) * 8, 8), 8), :] = pair[0:8] + pair[8:16]
    (upshift, depthwise, depthshift, postgain, postshift, pregain, preshift, mixshift, midgain,
     midshift, wideshift, narrowshift) = shorts
    lanes = narrowshift.shape[0] // LANES
    wide_lanes = upshift.shape[0] // LANES
    number = 0
    for target in (narrowshift, midgain, midshift, mixshift, pregain, preshift, postgain, postshift):
        for lane in range(lanes):
            target[lane * LANES : (lane + 1) * LANES] = short[number, :]
            number += 1
    for target in (wideshift,) + (depthwise,) * 9 + (depthshift, upshift):
        for lane in range(wide_lanes):
            value = short[number : number + 1, :]
            if target is depthwise:
                tap = number // wide_lanes - 3
                target[tap : tap + 1, lane * LANES : (lane + 1) * LANES] = value
            else:
                target[lane * LANES : (lane + 1) * LANES] = value.reshape(LANES)
            number += 1


def ends_kernel(numbers, own, arrived, ends, means):
    share = ends.shape[0] // 2
    local, slots, width = ends.shape[1:]
    first = numbers[0, 0]
    ends[pl.ds(first * share, share)] = own[...].reshape(share, local, slots, width)
    ends[pl.ds((1 - first) * share, share)] = arrived[...].reshape(share, local, slots, width)
    for micro in range(ends.shape[0]):
        for image in range(local):
            value = ends[micro, image].astype(F32)
            square = jnp.sum(value * value, axis=0, keepdims=True)
            number = micro * local + image
            filled = extent(numbers, number, False, 0) * extent(numbers, number, False, 1) * width
            mean = jnp.sum(square, axis=1, keepdims=True) / filled.astype(F32)
            means[0, micro : micro + 1, image : image + 1] = jnp.sqrt(mean)


WHOLE = pl.BlockSpec(memory_space=pltpu.VMEM)
ANYWHERE = pl.BlockSpec(memory_space=pl.ANY)
COST = 30
BOTH = ("section", "dp")


def shape(dims, kind):
    return jax.ShapeDtypeStruct(dims, kind)


class Calls:
    def __init__(self, numbers):
        self.numbers = numbers
        self.last = None

    def __call__(self, kernel, name, ins, outs, scratch=(), plain=False, mb=8, us=0):
        count = len(ins)
        after = () if self.last is None else (self.last,)

        def body(numbers, *refs):
            refs = refs[:count] + refs[count + len(after) :]
            return kernel(*refs) if plain else kernel(numbers, *refs)

        result = pl.pallas_call(
            body,
            out_shape=outs,
            in_specs=[pl.BlockSpec(memory_space=pltpu.SMEM)]
            + [WHOLE] * count
            + [ANYWHERE] * len(after),
            out_specs=[WHOLE] * len(outs),
            scratch_shapes=list(scratch),
            cost_estimate=pl.CostEstimate(flops=1 + int(us * 1e9), bytes_accessed=1, transcendentals=0),
            compiler_params=pltpu.CompilerParams(vmem_limit_bytes=mb * 1024 * 1024),
            name=name,
        )(self.numbers, *ins, *after)
        self.last = result[0]
        return result


def swapped(value, digit, step=1):
    sections, members = (lax.axis_size(axis) for axis in BOTH)
    pairs = []
    for section in range(sections):
        for member in range(members):
            if digit == "first" or digit == "second":
                along = (digit == "first") == (member % 2 == 0)
                other = (section ^ along) * members + (member ^ (0 if along else 2))
            elif digit == "near":
                other = section * members + (member ^ 4)
            else:
                other = section * members + (member ^ (step * digit))
            pairs.append((section * members + member, other))
    return lax.ppermute(value, BOTH, pairs)


class Group:
    def __init__(self, name, calls, keep, send, short=0):
        self.name, self.calls, self.keep, self.short = name, calls, keep, short
        self.rows = keep.shape[1]
        self.arrived = swapped(send, 1)

    def call(self, kernel, what, ins, outs):
        return self.calls(
            functools.partial(kernel, self.short), f"{self.name}_{what}", ins,
            [shape(dims + (self.rows, LANES), BF16) for dims in outs], plain=True, us=COST,
        )

    def halve(self, digit):
        half = (self.keep.shape[0] // 2,)
        self.keep, send = self.call(halve_kernel, digit, (self.keep, self.arrived), [half] * 2)
        self.arrived = swapped(send, digit)

    def first(self):
        self.halve("first")

    def second(self):
        self.halve("second")

    def near(self):
        self.halve("near")

    def add(self, what, digit, step):
        (self.keep,) = self.call(sum_kernel, what, (self.keep, self.arrived), [self.keep.shape[:1]])
        self.arrived = swapped(self.keep, digit, step)

    def far(self):
        self.add("far", 4, 2)
        stride = 4 * ROW
        while stride < lax.axis_size("dp"):
            self.add(f"over_{stride}", stride, 1)
            stride *= 2

    def total(self):
        self.add("total", 4, 1)

    def join(self, what, digit):
        dims = (2 * self.keep.shape[0],)
        (self.keep,) = self.call(join_kernel, what, (self.keep, self.arrived), [dims])
        self.arrived = swapped(self.keep, digit)

    def join_row(self):
        self.join("join_row", "second")

    def join_square(self):
        self.join("join", "first")
        self.near_half = swapped(self.keep, 1)

    def join_cores(self):
        self.blocks = [self.keep, self.arrived, self.near_half, swapped(self.arrived, 1)]


def shards(
    entering_tokens,
    output_sensitivity,
    picture_tile_extents,
    pointwise_enlarge,
    enlarge_bias,
    channelwise_kernel,
    channelwise_conv_bias,
    pointwise_contract,
    convblock_scale,
    convblock_offset,
    attend_scale,
    attend_offset,
    query_key_proj,
    heads_output_proj,
    heads_output_bias,
    feedforward_scale,
    feedforward_offset,
    feedforward_enlarge,
    feedforward_enlarge_bias,
    feedforward_contract,
    contract_bias,
):
    micro_count, local_images, slots, width = entering_tokens.shape
    channels = pointwise_enlarge.shape[1]
    section, member = lax.axis_index("section"), lax.axis_index("dp")
    share = micro_count // 2
    images = share * local_images
    rows = images * slots
    fixed = jnp.stack(
        [section, member % 2, section * 2 + member // 2 % 2, member // 4 % ROW]
    ).astype(jnp.int32)
    extents = jnp.transpose(picture_tile_extents, (1, 2, 0)).reshape(-1, micro_count)
    numbers = jnp.concatenate(
        [jnp.broadcast_to(fixed, (2 * local_images, FIXED)), extents], axis=1
    )

    call = Calls(numbers)
    sent, expanded, slope, active, projected = call(
        conv_ahead_kernel, "conv_ahead",
        (entering_tokens, pointwise_enlarge, enlarge_bias, channelwise_kernel,
         channelwise_conv_bias, pointwise_contract, convblock_scale, convblock_offset),
        (shape((rows, width), BF16), shape((rows, channels), BF16), shape((rows, channels), BF16),
         shape((rows, channels), BF16), shape((rows, width), F32)),
        [pltpu.VMEM((rows, BLOCK), F32)], mb=20,
    )
    qkv, weights, context, middle = call(
        attend_ahead_kernel, "attend_ahead",
        (sent, attend_scale, attend_offset, query_key_proj, heads_output_proj, heads_output_bias),
        (shape((rows, 3 * width), BF16), shape((images * HEADS, slots, slots), BF16),
         shape((rows, width), BF16), shape((rows, width), F32)), mb=16,
    )
    halves = [shape((SQUARE * ROW, 2 * PIECE, LANES), BF16)] * 2
    whole = [pltpu.VMEM((2, SQUARE, ROW, 2 * PIECE, LANES), BF16)]
    output, grad_middle, keep, send, mlp_small, mlp_wide = call(
        mlp_kernel, "mlp",
        (middle, output_sensitivity, feedforward_scale, feedforward_offset, feedforward_enlarge,
         feedforward_enlarge_bias, feedforward_contract, contract_bias),
        [shape((rows, width), BF16), shape((rows, width), F32)] + halves
        + [shape((8, width), F32), shape((1, channels), F32)],
        whole, mb=24,
    )
    mlp = Group("mlp", call, keep, send)
    (grad_qkv,) = call(
        heads_back_kernel, "heads_back", (grad_middle, qkv, weights, heads_output_proj),
        [shape((rows, 3 * width), BF16)], plain=True, mb=16,
    )
    mlp.first()
    grad_sent, proj_low, keep, send, sent_small = call(
        sent_back_kernel, "sent_back",
        (sent, grad_middle, grad_qkv, context, projected, active, attend_scale, attend_offset,
         query_key_proj, convblock_scale),
        [shape((rows, width), BF16), shape((rows, width), BF16)] + halves
        + [shape((8, width), F32)],
        whole, mb=24,
    )
    inner = Group("inner", call, keep, send)
    early_pieces = shape((2, SQUARE, ROW // 2, PIECE, LANES), BF16)
    total, early, early_wide = call(
        conv_back_kernel, "conv_back",
        (entering_tokens, grad_sent, proj_low, expanded, slope, pointwise_enlarge,
         channelwise_kernel, pointwise_contract),
        [shape((rows, width), F32), early_pieces, shape((16, channels), F32)],
        [pltpu.VMEM((rows, BLOCK), F32)], mb=20,
    )
    mlp.second()
    inner.first()
    halves = [shape((SQUARE * ROW, PIECE + 16, LANES), BF16)] * 2
    own, give, keep, send = call(
        conv_end_kernel, "conv_end",
        (entering_tokens, total, proj_low, expanded, slope, pointwise_enlarge, channelwise_kernel,
         pointwise_contract, early, early_wide, mlp_small, sent_small, mlp_wide, output),
        [shape((rows, width), BF16)] * 2 + halves,
        [pltpu.VMEM((2, SQUARE, ROW, PIECE + 16, LANES), BF16), pltpu.VMEM((16, channels), F32),
         pltpu.VMEM((rows, BLOCK), F32), pltpu.VMEM((2 * SQUARE * ROW, 8, LANES), F32)],
        mb=20,
    )
    conv = Group("conv", call, keep, send, 16)
    mlp.near()
    inner.second()
    conv.first()
    mlp.far()
    inner.near()
    conv.second()
    mlp.total()
    inner.far()
    conv.near()
    arrived = lax.ppermute(give, "section", [(0, 1), (1, 0)])
    mlp.join_row()
    conv.far()
    inner.total()
    mlp.join_square()
    ends, means = call(
        ends_kernel, "ends", (own, arrived),
        [shape(entering_tokens.shape, BF16), shape((1, micro_count, local_images), F32)],
    )
    conv.total()
    inner.join_row()
    conv.join_row()
    mlp.join_cores()
    inner.join_square()

    line, wide_line = shape((width,), F32), shape((channels,), F32)
    tall, wide = shape((channels, width), F32), shape((width, channels), F32)
    narrower, widener = call(mlp_end_kernel, "mlp_end", mlp.blocks, [tall, wide], mb=12)
    conv.join_square()
    inner.join_cores()
    attention, mixing, projector = call(
        sent_end_kernel, "sent_end", inner.blocks,
        [shape((width, 3 * width), F32), shape((width, width), F32), tall],
        [pltpu.VMEM((width, 4 * width), F32)], mb=12,
    )
    conv.join_cores()
    (expander, upshift, depthwise, depthshift, postgain, postshift, pregain, preshift, mixshift,
     midgain, midshift, wideshift, narrowshift) = call(
        conv_all_kernel, "conv_all", conv.blocks,
        [wide, wide_line, shape((9, channels), F32), wide_line] + [line] * 7 + [wide_line, line],
        [pltpu.VMEM((2 * SQUARE * ROW * 8, LANES), F32)],
    )
    return (
        ends[None], means, expander, upshift, depthwise, depthshift, projector, postgain,
        postshift, pregain, preshift, attention, mixing, mixshift, midgain, midshift, widener,
        wideshift, narrower, narrowshift,
    )


def solution(mesh):
    tokens = P(None, "dp", None, None)
    placed = (tokens, tokens, P(None, "dp", None)) + (P(),) * 18
    return jax.shard_map(
        shards,
        mesh=mesh,
        in_specs=placed,
        out_specs=(P("section", None, "dp", None, None), P("section", None, "dp")) + (P(),) * 18,
        check_vma=False,
    )
```

profile of v0, /device:TPU:1, one launch (start us, length us, event | category | flops | bytes accessed | tf_op | source)
XLA Modules:
  0.0 127.0 jit_solution(14094829936079578839)
XLA Ops:
  1.6 1.3 copy-done
  2.8 1.3 copy-done.2
  4.1 1.1 copy-done.4
  8.9 6.2 %conv_ahead.1 = (bf16[512,384]{1,0:T(8,128)(2,1)S(1)}, bf16[512,1536]{1,0:T(8,128)(2,1)S(1)}, bf16[512,1536]{1,0:T(8,128)(2,1)S(1)}, bf16[512,1536]{1,0:T(8,128)(2,1)S(1)}, f32[512,384]{1,0:T(8,128)S(1)}) custom-call(s32[2,8]{1,0:T(2,128)S(1)} %pad_add_fusion.numbers, bf16[4,1,256,384]{3,2,1,0:T(8,128)(2,1)S(1)} %copy-done.4, bf16[384,1536]{1,0:T(8,128)(2,1)S(1)} %copy-done, ...), custom_call_target="tpu_custom_call" | custom-call | flops 1 | bytes 1 | tf_op jit(solution)/shard_map/conv_ahead/pallas_call | solution.py:577
  15.2 3.6 %attend_ahead.1 = (bf16[512,1152]{1,0:T(8,128)(2,1)S(1)}, bf16[12,256,256]{2,1,0:T(8,128)(2,1)S(1)}, bf16[512,384]{1,0:T(8,128)(2,1)S(1)}, f32[512,384]{1,0:T(8,128)S(1)}) custom-call(s32[2,8]{1,0:T(2,128)S(1)} %pad_add_fusion.numbers, bf16[512,384]{1,0:T(8,128)(2,1)S(1)} %get-tuple-element.85.refs_0_.refs_6_, f32[384]{0:T(512)S(1)} %copy-done.19, ...), custom_call_target="tpu_custom_call" | custom-call | flops 1 | bytes 1 | tf_op jit(solution)/shard_map/attend_ahead/pallas_call | solution.py:577
  18.9 6.9 %mlp.1 = (bf16[512,384]{1,0:T(8,128)(2,1)S(1)}, f32[512,384]{1,0:T(8,128)S(1)}, bf16[16,288,128]{2,1,0:T(8,128)(2,1)S(1)}, bf16[16,288,128]{2,1,0:T(8,128)(2,1)S...) custom-call(s32[2,8]{1,0:T(2,128)S(1)} %pad_add_fusion.numbers, f32[512,384]{1,0:T(8,128)S(1)} %get-tuple-element.86.refs_0_, ...), custom_call_target="tpu_custom_call" | custom-call | flops 1 | bytes 1 | tf_op jit(solution)/shard_map/mlp/pallas_call | solution.py:577
  26.0 4.5 %heads_back.1.refs_2_ = bf16[512,1152]{1,0:T(8,128)(2,1)S(1)} custom-call(s32[2,8]{1,0:T(2,128)S(1)} %pad_add_fusion.numbers, f32[512,384]{1,0:T(8,128)S(1)} %get-tuple-element.88.refs_0_.refs_1_, bf16[512,1152]{1,0:T(8,128)(2,1)S(1)} %get-tuple-element.87.refs_8_.refs_1_, bf16[12,256,256]{2,1,0:T(8,128)(2,1)S(1)} %get-tuple-element.89.refs_2_, ...), custom_call_target="tpu_custom_call" | custom-call | flops 1 | bytes 1 | tf_op jit(solution)/shard_map/heads_back/pallas_call | solution.py:577
  31.3 2.8 %collective-permute-start.2 = (bf16[8,288,128]{2,1,0:T(8,128)(2,1)S(1)}, bf16[8,288,128]{2,1,0:T(8,128)(2,1)S(1)}, u32[]{:S(2)}, u32[]{:S(2)}) collective-permute-start(bf16[8,288,128]{2,1,0:T(8,128)(2,1)S(1)} %get-tuple-element.109), channel_id=1, source_target_pairs={{0,16},{1,3},{2,18},{3,1},{4,20},{5,7},{6,22},{7,5},{8,24},{9,11},... | collective-permute-start | bytes 1769480 | tf_op jit(solution)/shard_map/ppermute | solution.py:606
  34.1 4.3 %sent_back.1 = (bf16[512,384]{1,0:T(8,128)(2,1)S(1)}, bf16[512,384]{1,0:T(8,128)(2,1)S(1)}, bf16[16,288,128]{2,1,0:T(8,128)(2,1)S(1)}, bf16[16,288,128]{2,1,0:T(8,128)(2,1)S(1)}, f32[8,384]{1,0:T(8,128)S(1)}) custom-call(s32[2,8]{1,0:T(2,128)S(1)} %pad_add_fusion.numbers, bf16[512,384]{1,0:T(8,128)(2,1)S(1)} %get-tuple-element.85.refs_0_.refs_6_, ...), custom_call_target="tpu_custom_call" | custom-call | flops 1 | bytes 1 | tf_op jit(solution)/shard_map/sent_back/pallas_call | solution.py:577
  38.8 4.8 %conv_back.1 = (f32[512,384]{1,0:T(8,128)S(1)}, bf16[2,4,2,144,128]{4,3,2,1,0:T(8,128)(2,1)S(1)}, f32[16,1536]{1,0:T(8,128)S(1)}) custom-call(s32[2,8]{1,0:T(2,128)S(1)} %pad_add_fusion.numbers, bf16[4,1,256,384]{3,2,1,0:T(8,128)(2,1)S(1)} %copy-done.5, bf16[512,384]{1,0:T(8,128)(2,1)S(1)} %get-tuple-element.97.refs_1_.refs_8_, ...), custom_call_target="tpu_custom_call" | custom-call | flops 1 | bytes 1 | tf_op jit(solution)/shard_map/conv_back/pallas_call | solution.py:577
  44.3 1.1 collective-permute-start.4
  46.8 5.5 %conv_end.1 = (bf16[512,384]{1,0:T(8,128)(2,1)S(1)}, bf16[512,384]{1,0:T(8,128)(2,1)}, bf16[16,160,128]{2,1,0:T(8,128)(2,1)S(1)}, bf16[16,160,128]{2,1,0:T(8,128)(2,1)S(1)}) custom-call(s32[2,8]{1,0:T(2,128)S(1)} %pad_add_fusion.numbers, bf16[4,1,256,384]{3,2,1,0:T(8,128)(2,1)S(1)} %copy-done.5, f32[512,384]{1,0:T(8,128)S(1)} %get-tuple-element.101.refs_2_.refs_1_, ...), custom_call_target="tpu_custom_call" | custom-call | flops 1 | bytes 1 | tf_op jit(solution)/shard_map/conv_end/pallas_call | solution.py:577
  52.9 1.4 %collective-permute-start.5 = (bf16[2,288,128]{2,1,0:T(8,128)(2,1)S(1)}, bf16[2,288,128]{2,1,0:T(8,128)(2,1)S(1)}, u32[]{:S(2)}, u32[]{:S(2)}) collective-permute-start(bf16[2,288,128]{2,1,0:T(8,128)(2,1)S(1)} %get-tuple-element.116), channel_id=1, source_target_pairs={{0,4},{1,5},{2,6},{3,7},{4,0},{5,1},{6,2},{7,3},{8,12},{9,13},{10,... | collective-permute-start | bytes 442376 | tf_op jit(solution)/shard_map/ppermute | solution.py:606
  54.3 1.2 collective-permute-start.3
  55.5 2.4 %collective-permute-start.6 = (bf16[16,160,128]{2,1,0:T(8,128)(2,1)S(1)}, bf16[16,160,128]{2,1,0:T(8,128)(2,1)S(1)}, u32[]{:S(2)}, u32[]{:S(2)}) collective-permute-start(bf16[16,160,128]{2,1,0:T(8,128)(2,1)S(1)} %get-tuple-element.118), channel_id=1, source_target_pairs={{0,1},{1,0},{2,3},{3,2},{4,5},{5,4},{6,7},{7,6},{8,9},{9,8},{10,11... | collective-permute-start | bytes 1966088 | tf_op jit(solution)/shard_map/ppermute | solution.py:606
  61.0 2.4 %collective-permute-start.8 = (bf16[2,288,128]{2,1,0:T(8,128)(2,1)S(1)}, bf16[2,288,128]{2,1,0:T(8,128)(2,1)S(1)}, u32[]{:S(2)}, u32[]{:S(2)}) collective-permute-start(bf16[2,288,128]{2,1,0:T(8,128)(2,1)S(1)} %mlp_far.1.refs_2_.refs_0_), channel_id=1, source_target_pairs={{0,8},{1,9},{2,10},{3,11},{4,12},{5,13},{6,14},{7,15},{8,0},{9,1},... | collective-permute-start | bytes 442376 | tf_op jit(solution)/shard_map/ppermute | solution.py:606
  63.4 6.3 %collective-permute-done.10.refs_1_ = bf16[4,288,128]{2,1,0:T(8,128)(2,1)S(1)} collective-permute-done((bf16[4,288,128]{2,1,0:T(8,128)(2,1)S(1)}, bf16[4,288,128]{2,1,0:T(8,128)(2,1)S(1)}, u32[]{:S(2)}, u32[]{:S(2)}) %collective-permute-start.10) | collective-permute-done | bytes 294944 | tf_op jit(solution)/shard_map/ppermute | solution.py:606
  75.1 2.3 %collective-permute-start.15 = (bf16[2,288,128]{2,1,0:T(8,128)(2,1)S(1)}, bf16[2,288,128]{2,1,0:T(8,128)(2,1)S(1)}, u32[]{:S(2)}, u32[]{:S(2)}) collective-permute-start(bf16[2,288,128]{2,1,0:T(8,128)(2,1)S(1)} %inner_far.1.refs_2_.refs_0_), channel_id=1, source_target_pairs={{0,8},{1,9},{2,10},{3,11},{4,12},{5,13},{6,14},{7,15},{8,0},{9,1},... | collective-permute-start | bytes 442376 | tf_op jit(solution)/shard_map/ppermute | solution.py:606
  80.4 2.1 %collective-permute-done.16.refs_1_ = bf16[2,160,128]{2,1,0:T(8,128)(2,1)S(1)} collective-permute-done((bf16[2,160,128]{2,1,0:T(8,128)(2,1)S(1)}, bf16[2,160,128]{2,1,0:T(8,128)(2,1)S(1)}, u32[]{:S(2)}, u32[]{:S(2)}) %collective-permute-start.16) | collective-permute-done | bytes 81952 | tf_op jit(solution)/shard_map/ppermute | solution.py:606
  83.1 2.8 %collective-permute-start.17 = (bf16[2,160,128]{2,1,0:T(8,128)(2,1)S(1)}, bf16[2,160,128]{2,1,0:T(8,128)(2,1)S(1)}, u32[]{:S(2)}, u32[]{:S(2)}) collective-permute-start(bf16[2,160,128]{2,1,0:T(8,128)(2,1)S(1)} %conv_far.1.refs_2_.refs_0_), channel_id=1, source_target_pairs={{0,8},{1,9},{2,10},{3,11},{4,12},{5,13},{6,14},{7,15},{8,0},{9,1},... | collective-permute-start | bytes 245768 | tf_op jit(solution)/shard_map/ppermute | solution.py:606
  87.7 4.6 %collective-permute-start.22 = (bf16[8,288,128]{2,1,0:T(8,128)(2,1)S(1)}, bf16[8,288,128]{2,1,0:T(8,128)(2,1)S(1)}, u32[]{:S(2)}, u32[]{:S(2)}) collective-permute-start(bf16[8,288,128]{2,1,0:T(8,128)(2,1)S(1)} %mlp_join.1.refs_2_.refs_0_), channel_id=1, source_target_pairs={{0,1},{1,0},{2,3},{3,2},{4,5},{5,4},{6,7},{7,6},{8,9},{9,8},{10,11... | collective-permute-start | bytes 1769480 | tf_op jit(solution)/shard_map/ppermute | solution.py:606
  93.2 2.0 %ends.1 = (bf16[4,1,256,384]{3,2,1,0:T(8,128)(2,1)}, f32[1,4,1]{2,1,0:T(4,128)S(1)}) custom-call(s32[2,8]{1,0:T(2,128)S(1)} %pad_add_fusion.numbers, bf16[512,384]{1,0:T(8,128)(2,1)S(1)} %get-tuple-element.112.refs_2_.refs_0_, bf16[512,384]{1,0:T(8,128)(2,1)} %collective-permute-done.3.refs_1_, bf16[8,288,128]{2,1,0:T(8,128)(2,1)S(1)} %mlp_join.1.refs_2_.refs_0_), custom_call_target="tpu_custom_call" | custom-call | flops 1 | bytes 1 | tf_op jit(solution)/shard_map/ends/pallas_call | solution.py:577
  95.2 1.1 copy-done.27
  98.6 2.6 %collective-permute-done.18.refs_1_ = bf16[2,160,128]{2,1,0:T(8,128)(2,1)S(1)} collective-permute-done((bf16[2,160,128]{2,1,0:T(8,128)(2,1)S(1)}, bf16[2,160,128]{2,1,0:T(8,128)(2,1)S(1)}, u32[]{:S(2)}, u32[]{:S(2)}) %collective-permute-start.18) | collective-permute-done | bytes 81952 | tf_op jit(solution)/shard_map/ppermute | solution.py:606
  102.6 1.1 collective-permute-start.23
  106.3 3.2 %mlp_end.1 = (f32[1536,384]{1,0:T(8,128)}, f32[384,1536]{1,0:T(8,128)}) custom-call(s32[2,8]{1,0:T(2,128)S(1)} %pad_add_fusion.numbers, bf16[8,288,128]{2,1,0:T(8,128)(2,1)S(1)} %mlp_join.1.refs_2_.refs_0_, bf16[8,288,128]{2,1,0:T(8,128)(2,1)S(1)} %collective-permute-done.21.refs_1_, bf16[8,288,128]{2,1,0:T(8,128)(2,1)S(1)} %collective-permute-done.22.refs_2_, ...), custom_call_target="tpu_custom_call" | custom-call | flops 1 | bytes 1 | tf_op jit(solution)/shard_map/mlp_end/pallas_call | solution.py:577
  109.5 1.7 %copy-done.26 = f32[1536,384]{1,0:T(8,128)S(1)} copy-done((f32[1536,384]{1,0:T(8,128)S(1)}, f32[1536,384]{1,0:T(8,128)}, u32[]{:S(2)}) %copy-start.26) | copy-done | bytes 2359320
  113.1 1.3 %collective-permute-done.28.refs_1_ = bf16[8,288,128]{2,1,0:T(8,128)(2,1)S(1)} collective-permute-done((bf16[8,288,128]{2,1,0:T(8,128)(2,1)S(1)}, bf16[8,288,128]{2,1,0:T(8,128)(2,1)S(1)}, u32[]{:S(2)}, u32[]{:S(2)}) %collective-permute-start.28) | collective-permute-done | bytes 589856 | tf_op jit(solution)/shard_map/ppermute | solution.py:606
  115.4 2.6 %collective-permute-done.25.refs_1_ = bf16[8,160,128]{2,1,0:T(8,128)(2,1)S(1)} collective-permute-done((bf16[8,160,128]{2,1,0:T(8,128)(2,1)S(1)}, bf16[8,160,128]{2,1,0:T(8,128)(2,1)S(1)}, u32[]{:S(2)}, u32[]{:S(2)}) %collective-permute-start.25) | collective-permute-done | bytes 327712 | tf_op jit(solution)/shard_map/ppermute | solution.py:606
  119.6 3.1 %sent_end.1 = (f32[384,1152]{1,0:T(8,128)}, f32[384,384]{1,0:T(8,128)}, f32[1536,384]{1,0:T(8,128)}) custom-call(s32[2,8]{1,0:T(2,128)S(1)} %pad_add_fusion.numbers, bf16[8,288,128]{2,1,0:T(8,128)(2,1)S(1)} %inner_join.1.refs_4_.refs_0_, bf16[8,288,128]{2,1,0:T(8,128)(2,1)S(1)} %collective-permute-done.28.refs_1_, ...), custom_call_target="tpu_custom_call" | custom-call | flops 1 | bytes 1 | tf_op jit(solution)/shard_map/sent_end/pallas_call | solution.py:577
  122.7 1.5 %copy-done.7 = f32[384,1152]{1,0:T(8,128)S(1)} copy-done((f32[384,1152]{1,0:T(8,128)S(1)}, f32[384,1152]{1,0:T(8,128)}, u32[]{:S(2)}) %copy-start.7) | copy-done | bytes 1769496
  124.1 2.7 %conv_all.1 = (f32[384,1536]{1,0:T(8,128)}, f32[1536]{0:T(1024)}, f32[9,1536]{1,0:T(8,128)}, f32[1536]{0:T(1024)}, f32[384]{0:T(512)}, /*index=5*/f32[384]{0:T(5...) custom-call(s32[2,8]{1,0:T(2,128)S(1)} %pad_add_fusion.numbers, ...), custom_call_target="tpu_custom_call" | custom-call | flops 1 | bytes 1 | tf_op jit(solution)/shard_map/conv_all/pallas_call | solution.py:577
  (122 shorter events, 33.9 us)
Async XLA Ops:
  8.9 10.0 %copy-start.10 = (bf16[1536,384]{1,0:T(8,128)(2,1)S(1)}, bf16[1536,384]{1,0:T(8,128)(2,1)}, u32[]{:S(2)}) copy-start(bf16[1536,384]{1,0:T(8,128)(2,1)} %refs_6_.6) | copy-start | bytes 3538948
  25.9 4.6 %collective-permute-start = (bf16[16,288,128]{2,1,0:T(8,128)(2,1)S(1)}, bf16[16,288,128]{2,1,0:T(8,128)(2,1)S(1)}, u32[]{:S(2)}, u32[]{:S(2)}) collective-permute-start(bf16[16,288,128]{2,1,0:T(8,128)(2,1)S(1)} %get-tuple-element.95), channel_id=1, source_target_pairs={{0,1},{1,0},{2,3},{3,2},{4,5},{5,4},{6,7},{7,6},{8,9},{9,8},{10,11... | collective-permute-start | bytes 3538952 | tf_op jit(solution)/shard_map/ppermute | solution.py:606
  31.3 12.3 %collective-permute-start.2 = (bf16[8,288,128]{2,1,0:T(8,128)(2,1)S(1)}, bf16[8,288,128]{2,1,0:T(8,128)(2,1)S(1)}, u32[]{:S(2)}, u32[]{:S(2)}) collective-permute-start(bf16[8,288,128]{2,1,0:T(8,128)(2,1)S(1)} %get-tuple-element.109), channel_id=1, source_target_pairs={{0,16},{1,3},{2,18},{3,1},{4,20},{5,7},{6,22},{7,5},{8,24},{9,11},... | collective-permute-start | bytes 1769480 | tf_op jit(solution)/shard_map/ppermute | solution.py:606
  38.4 6.9 %collective-permute-start.1 = (bf16[16,288,128]{2,1,0:T(8,128)(2,1)S(1)}, bf16[16,288,128]{2,1,0:T(8,128)(2,1)S(1)}, u32[]{:S(2)}, u32[]{:S(2)}) collective-permute-start(bf16[16,288,128]{2,1,0:T(8,128)(2,1)S(1)} %get-tuple-element.108), channel_id=1, source_target_pairs={{0,1},{1,0},{2,3},{3,2},{4,5},{5,4},{6,7},{7,6},{8,9},{9,8},{10,11... | collective-permute-start | bytes 3538952 | tf_op jit(solution)/shard_map/ppermute | solution.py:606
  44.3 8.0 %collective-permute-start.4 = (bf16[4,288,128]{2,1,0:T(8,128)(2,1)S(1)}, bf16[4,288,128]{2,1,0:T(8,128)(2,1)S(1)}, u32[]{:S(2)}, u32[]{:S(2)}) collective-permute-start(bf16[4,288,128]{2,1,0:T(8,128)(2,1)S(1)} %get-tuple-element.114), channel_id=1, source_target_pairs={{0,2},{1,17},{2,0},{3,19},{4,6},{5,21},{6,4},{7,23},{8,10},{9,25},... | collective-permute-start | bytes 884744 | tf_op jit(solution)/shard_map/ppermute | solution.py:606
  46.2 11.7 %collective-permute-start.7 = (bf16[8,288,128]{2,1,0:T(8,128)(2,1)S(1)}, bf16[8,288,128]{2,1,0:T(8,128)(2,1)S(1)}, u32[]{:S(2)}, u32[]{:S(2)}) collective-permute-start(bf16[8,288,128]{2,1,0:T(8,128)(2,1)S(1)} %get-tuple-element.119), channel_id=1, source_target_pairs={{0,16},{1,3},{2,18},{3,1},{4,20},{5,7},{6,22},{7,5},{8,24},{9,11},... | collective-permute-start | bytes 1769480 | tf_op jit(solution)/shard_map/ppermute | solution.py:606
  52.9 7.5 %collective-permute-start.5 = (bf16[2,288,128]{2,1,0:T(8,128)(2,1)S(1)}, bf16[2,288,128]{2,1,0:T(8,128)(2,1)S(1)}, u32[]{:S(2)}, u32[]{:S(2)}) collective-permute-start(bf16[2,288,128]{2,1,0:T(8,128)(2,1)S(1)} %get-tuple-element.116), channel_id=1, source_target_pairs={{0,4},{1,5},{2,6},{3,7},{4,0},{5,1},{6,2},{7,3},{8,12},{9,13},{10,... | collective-permute-start | bytes 442376 | tf_op jit(solution)/shard_map/ppermute | solution.py:606
  54.3 39.0 %collective-permute-start.3 = (bf16[512,384]{1,0:T(8,128)(2,1)}, bf16[512,384]{1,0:T(8,128)(2,1)}, u32[]{:S(2)}, u32[]{:S(2)}) collective-permute-start(bf16[512,384]{1,0:T(8,128)(2,1)} %get-tuple-element.113), channel_id=1, source_target_pairs={{0,16},{16,0},{1,17},{17,1},{2,18},{18,2},{3,19},{19,3},{4,20},{20... | collective-permute-start | bytes 1179656 | tf_op jit(solution)/shard_map/ppermute | solution.py:772
  55.5 4.2 %collective-permute-start.6 = (bf16[16,160,128]{2,1,0:T(8,128)(2,1)S(1)}, bf16[16,160,128]{2,1,0:T(8,128)(2,1)S(1)}, u32[]{:S(2)}, u32[]{:S(2)}) collective-permute-start(bf16[16,160,128]{2,1,0:T(8,128)(2,1)S(1)} %get-tuple-element.118), channel_id=1, source_target_pairs={{0,1},{1,0},{2,3},{3,2},{4,5},{5,4},{6,7},{7,6},{8,9},{9,8},{10,11... | collective-permute-start | bytes 1966088 | tf_op jit(solution)/shard_map/ppermute | solution.py:606
  58.6 11.2 %collective-permute-start.10 = (bf16[4,288,128]{2,1,0:T(8,128)(2,1)S(1)}, bf16[4,288,128]{2,1,0:T(8,128)(2,1)S(1)}, u32[]{:S(2)}, u32[]{:S(2)}) collective-permute-start(bf16[4,288,128]{2,1,0:T(8,128)(2,1)S(1)} %get-tuple-element.123), channel_id=1, source_target_pairs={{0,2},{1,17},{2,0},{3,19},{4,6},{5,21},{6,4},{7,23},{8,10},{9,25},... | collective-permute-start | bytes 884744 | tf_op jit(solution)/shard_map/ppermute | solution.py:606
  61.0 10.8 %collective-permute-start.8 = (bf16[2,288,128]{2,1,0:T(8,128)(2,1)S(1)}, bf16[2,288,128]{2,1,0:T(8,128)(2,1)S(1)}, u32[]{:S(2)}, u32[]{:S(2)}) collective-permute-start(bf16[2,288,128]{2,1,0:T(8,128)(2,1)S(1)} %mlp_far.1.refs_2_.refs_0_), channel_id=1, source_target_pairs={{0,8},{1,9},{2,10},{3,11},{4,12},{5,13},{6,14},{7,15},{8,0},{9,1},... | collective-permute-start | bytes 442376 | tf_op jit(solution)/shard_map/ppermute | solution.py:606
  63.3 7.8 %collective-permute-start.9 = (bf16[8,160,128]{2,1,0:T(8,128)(2,1)S(1)}, bf16[8,160,128]{2,1,0:T(8,128)(2,1)S(1)}, u32[]{:S(2)}, u32[]{:S(2)}) collective-permute-start(bf16[8,160,128]{2,1,0:T(8,128)(2,1)S(1)} %get-tuple-element.122), channel_id=1, source_target_pairs={{0,16},{1,3},{2,18},{3,1},{4,20},{5,7},{6,22},{7,5},{8,24},{9,11},... | collective-permute-start | bytes 983048 | tf_op jit(solution)/shard_map/ppermute | solution.py:606
  70.4 4.1 %collective-permute-start.13 = (bf16[2,288,128]{2,1,0:T(8,128)(2,1)S(1)}, bf16[2,288,128]{2,1,0:T(8,128)(2,1)S(1)}, u32[]{:S(2)}, u32[]{:S(2)}) collective-permute-start(bf16[2,288,128]{2,1,0:T(8,128)(2,1)S(1)} %get-tuple-element.127), channel_id=1, source_target_pairs={{0,4},{1,5},{2,6},{3,7},{4,0},{5,1},{6,2},{7,3},{8,12},{9,13},{10,... | collective-permute-start | bytes 442376 | tf_op jit(solution)/shard_map/ppermute | solution.py:606
  72.4 6.9 %collective-permute-start.11 = (bf16[2,288,128]{2,1,0:T(8,128)(2,1)S(1)}, bf16[2,288,128]{2,1,0:T(8,128)(2,1)S(1)}, u32[]{:S(2)}, u32[]{:S(2)}) collective-permute-start(bf16[2,288,128]{2,1,0:T(8,128)(2,1)S(1)} %mlp_total.1.refs_2_.refs_0_), channel_id=1, source_target_pairs={{0,4},{1,5},{2,6},{3,7},{4,0},{5,1},{6,2},{7,3},{8,12},{9,13},{10,... | collective-permute-start | bytes 442376 | tf_op jit(solution)/shard_map/ppermute | solution.py:606
  73.2 4.5 %collective-permute-start.12 = (bf16[4,160,128]{2,1,0:T(8,128)(2,1)S(1)}, bf16[4,160,128]{2,1,0:T(8,128)(2,1)S(1)}, u32[]{:S(2)}, u32[]{:S(2)}) collective-permute-start(bf16[4,160,128]{2,1,0:T(8,128)(2,1)S(1)} %get-tuple-element.126), channel_id=1, source_target_pairs={{0,2},{1,17},{2,0},{3,19},{4,6},{5,21},{6,4},{7,23},{8,10},{9,25},... | collective-permute-start | bytes 491528 | tf_op jit(solution)/shard_map/ppermute | solution.py:606
  75.1 10.8 %collective-permute-start.15 = (bf16[2,288,128]{2,1,0:T(8,128)(2,1)S(1)}, bf16[2,288,128]{2,1,0:T(8,128)(2,1)S(1)}, u32[]{:S(2)}, u32[]{:S(2)}) collective-permute-start(bf16[2,288,128]{2,1,0:T(8,128)(2,1)S(1)} %inner_far.1.refs_2_.refs_0_), channel_id=1, source_target_pairs={{0,8},{1,9},{2,10},{3,11},{4,12},{5,13},{6,14},{7,15},{8,0},{9,1},... | collective-permute-start | bytes 442376 | tf_op jit(solution)/shard_map/ppermute | solution.py:606
  78.3 4.2 %collective-permute-start.16 = (bf16[2,160,128]{2,1,0:T(8,128)(2,1)S(1)}, bf16[2,160,128]{2,1,0:T(8,128)(2,1)S(1)}, u32[]{:S(2)}, u32[]{:S(2)}) collective-permute-start(bf16[2,160,128]{2,1,0:T(8,128)(2,1)S(1)} %get-tuple-element.129), channel_id=1, source_target_pairs={{0,4},{1,5},{2,6},{3,7},{4,0},{5,1},{6,2},{7,3},{8,12},{9,13},{10,... | collective-permute-start | bytes 245768 | tf_op jit(solution)/shard_map/ppermute | solution.py:606
  79.9 7.3 %collective-permute-start.14 = (bf16[4,288,128]{2,1,0:T(8,128)(2,1)S(1)}, bf16[4,288,128]{2,1,0:T(8,128)(2,1)S(1)}, u32[]{:S(2)}, u32[]{:S(2)}) collective-permute-start(bf16[4,288,128]{2,1,0:T(8,128)(2,1)S(1)} %mlp_join_row.1.refs_2_.refs_0_), channel_id=1, source_target_pairs={{0,2},{1,17},{2,0},{3,19},{4,6},{5,21},{6,4},{7,23},{8,10},{9,25},... | collective-permute-start | bytes 884744 | tf_op jit(solution)/shard_map/ppermute | solution.py:606
  83.1 12.1 %collective-permute-start.17 = (bf16[2,160,128]{2,1,0:T(8,128)(2,1)S(1)}, bf16[2,160,128]{2,1,0:T(8,128)(2,1)S(1)}, u32[]{:S(2)}, u32[]{:S(2)}) collective-permute-start(bf16[2,160,128]{2,1,0:T(8,128)(2,1)S(1)} %conv_far.1.refs_2_.refs_0_), channel_id=1, source_target_pairs={{0,8},{1,9},{2,10},{3,11},{4,12},{5,13},{6,14},{7,15},{8,0},{9,1},... | collective-permute-start | bytes 245768 | tf_op jit(solution)/shard_map/ppermute | solution.py:606
  86.5 10.5 %collective-permute-start.19 = (bf16[2,288,128]{2,1,0:T(8,128)(2,1)S(1)}, bf16[2,288,128]{2,1,0:T(8,128)(2,1)S(1)}, u32[]{:S(2)}, u32[]{:S(2)}) collective-permute-start(bf16[2,288,128]{2,1,0:T(8,128)(2,1)S(1)} %inner_total.1.refs_2_.refs_0_), channel_id=1, source_target_pairs={{0,4},{1,5},{2,6},{3,7},{4,0},{5,1},{6,2},{7,3},{8,12},{9,13},{10,... | collective-permute-start | bytes 442376 | tf_op jit(solution)/shard_map/ppermute | solution.py:606
  87.7 18.6 %collective-permute-start.22 = (bf16[8,288,128]{2,1,0:T(8,128)(2,1)S(1)}, bf16[8,288,128]{2,1,0:T(8,128)(2,1)S(1)}, u32[]{:S(2)}, u32[]{:S(2)}) collective-permute-start(bf16[8,288,128]{2,1,0:T(8,128)(2,1)S(1)} %mlp_join.1.refs_2_.refs_0_), channel_id=1, source_target_pairs={{0,1},{1,0},{2,3},{3,2},{4,5},{5,4},{6,7},{7,6},{8,9},{9,8},{10,11... | collective-permute-start | bytes 1769480 | tf_op jit(solution)/shard_map/ppermute | solution.py:606
  92.3 10.3 %collective-permute-start.21 = (bf16[8,288,128]{2,1,0:T(8,128)(2,1)S(1)}, bf16[8,288,128]{2,1,0:T(8,128)(2,1)S(1)}, u32[]{:S(2)}, u32[]{:S(2)}) collective-permute-start(bf16[8,288,128]{2,1,0:T(8,128)(2,1)S(1)} %mlp_join.1.refs_2_.refs_0_), channel_id=1, source_target_pairs={{0,16},{1,3},{2,18},{3,1},{4,20},{5,7},{6,22},{7,5},{8,24},{9,11},... | collective-permute-start | bytes 1769480 | tf_op jit(solution)/shard_map/ppermute | solution.py:606
  96.9 4.3 %collective-permute-start.18 = (bf16[2,160,128]{2,1,0:T(8,128)(2,1)S(1)}, bf16[2,160,128]{2,1,0:T(8,128)(2,1)S(1)}, u32[]{:S(2)}, u32[]{:S(2)}) collective-permute-start(bf16[2,160,128]{2,1,0:T(8,128)(2,1)S(1)} %conv_total.1.refs_2_.refs_0_), channel_id=1, source_target_pairs={{0,4},{1,5},{2,6},{3,7},{4,0},{5,1},{6,2},{7,3},{8,12},{9,13},{10,... | collective-permute-start | bytes 245768 | tf_op jit(solution)/shard_map/ppermute | solution.py:606
  97.6 7.2 %collective-permute-start.24 = (bf16[4,288,128]{2,1,0:T(8,128)(2,1)S(1)}, bf16[4,288,128]{2,1,0:T(8,128)(2,1)S(1)}, u32[]{:S(2)}, u32[]{:S(2)}) collective-permute-start(bf16[4,288,128]{2,1,0:T(8,128)(2,1)S(1)} %inner_join_row.1.refs_2_.refs_0_), channel_id=1, source_target_pairs={{0,2},{1,17},{2,0},{3,19},{4,6},{5,21},{6,4},{7,23},{8,10},{9,25},... | collective-permute-start | bytes 884744 | tf_op jit(solution)/shard_map/ppermute | solution.py:606
  101.8 7.7 %collective-permute-start.20 = (bf16[4,160,128]{2,1,0:T(8,128)(2,1)S(1)}, bf16[4,160,128]{2,1,0:T(8,128)(2,1)S(1)}, u32[]{:S(2)}, u32[]{:S(2)}) collective-permute-start(bf16[4,160,128]{2,1,0:T(8,128)(2,1)S(1)} %conv_join_row.1.refs_2_.refs_0_), channel_id=1, source_target_pairs={{0,2},{1,17},{2,0},{3,19},{4,6},{5,21},{6,4},{7,23},{8,10},{9,25},... | collective-permute-start | bytes 491528 | tf_op jit(solution)/shard_map/ppermute | solution.py:606
  102.6 3.7 %collective-permute-start.23 = (bf16[8,288,128]{2,1,0:T(8,128)(2,1)S(1)}, bf16[8,288,128]{2,1,0:T(8,128)(2,1)S(1)}, u32[]{:S(2)}, u32[]{:S(2)}) collective-permute-start(bf16[8,288,128]{2,1,0:T(8,128)(2,1)S(1)} %collective-permute-done.21.refs_1_), channel_id=1, source_target_pairs={{0,1},{1,0},{2,3},{3,2},{4,5},{5,4},{6,7},{7,6},{8,9},{9,8},{10,11... | collective-permute-start | bytes 1769480 | tf_op jit(solution)/shard_map/ppermute | solution.py:606
  105.3 9.1 %collective-permute-start.28 = (bf16[8,288,128]{2,1,0:T(8,128)(2,1)S(1)}, bf16[8,288,128]{2,1,0:T(8,128)(2,1)S(1)}, u32[]{:S(2)}, u32[]{:S(2)}) collective-permute-start(bf16[8,288,128]{2,1,0:T(8,128)(2,1)S(1)} %inner_join.1.refs_4_.refs_0_), channel_id=1, source_target_pairs={{0,16},{1,3},{2,18},{3,1},{4,20},{5,7},{6,22},{7,5},{8,24},{9,11},... | collective-permute-start | bytes 1769480 | tf_op jit(solution)/shard_map/ppermute | solution.py:606
  111.8 6.3 %collective-permute-start.25 = (bf16[8,160,128]{2,1,0:T(8,128)(2,1)S(1)}, bf16[8,160,128]{2,1,0:T(8,128)(2,1)S(1)}, u32[]{:S(2)}, u32[]{:S(2)}) collective-permute-start(bf16[8,160,128]{2,1,0:T(8,128)(2,1)S(1)} %conv_join.1.refs_4_.refs_0_), channel_id=1, source_target_pairs={{0,16},{1,3},{2,18},{3,1},{4,20},{5,7},{6,22},{7,5},{8,24},{9,11},... | collective-permute-start | bytes 983048 | tf_op jit(solution)/shard_map/ppermute | solution.py:606
  112.4 7.2 %collective-permute-start.29 = (bf16[8,288,128]{2,1,0:T(8,128)(2,1)S(1)}, bf16[8,288,128]{2,1,0:T(8,128)(2,1)S(1)}, u32[]{:S(2)}, u32[]{:S(2)}) collective-permute-start(bf16[8,288,128]{2,1,0:T(8,128)(2,1)S(1)} %inner_join.1.refs_4_.refs_0_), channel_id=1, source_target_pairs={{0,1},{1,0},{2,3},{3,2},{4,5},{5,4},{6,7},{7,6},{8,9},{9,8},{10,11... | collective-permute-start | bytes 1769480 | tf_op jit(solution)/shard_map/ppermute | solution.py:606
  114.4 5.1 %collective-permute-start.30 = (bf16[8,288,128]{2,1,0:T(8,128)(2,1)S(1)}, bf16[8,288,128]{2,1,0:T(8,128)(2,1)S(1)}, u32[]{:S(2)}, u32[]{:S(2)}) collective-permute-start(bf16[8,288,128]{2,1,0:T(8,128)(2,1)S(1)} %collective-permute-done.28.refs_1_), channel_id=1, source_target_pairs={{0,1},{1,0},{2,3},{3,2},{4,5},{5,4},{6,7},{7,6},{8,9},{9,8},{10,11... | collective-permute-start | bytes 1769480 | tf_op jit(solution)/shard_map/ppermute | solution.py:606
  115.4 7.2 %collective-permute-start.26 = (bf16[8,160,128]{2,1,0:T(8,128)(2,1)S(1)}, bf16[8,160,128]{2,1,0:T(8,128)(2,1)S(1)}, u32[]{:S(2)}, u32[]{:S(2)}) collective-permute-start(bf16[8,160,128]{2,1,0:T(8,128)(2,1)S(1)} %conv_join.1.refs_4_.refs_0_), channel_id=1, source_target_pairs={{0,1},{1,0},{2,3},{3,2},{4,5},{5,4},{6,7},{7,6},{8,9},{9,8},{10,11... | collective-permute-start | bytes 983048 | tf_op jit(solution)/shard_map/ppermute | solution.py:606
  118.0 4.6 %collective-permute-start.27 = (bf16[8,160,128]{2,1,0:T(8,128)(2,1)S(1)}, bf16[8,160,128]{2,1,0:T(8,128)(2,1)}, u32[]{:S(2)}, u32[]{:S(2)}) collective-permute-start(bf16[8,160,128]{2,1,0:T(8,128)(2,1)S(1)} %collective-permute-done.25.refs_1_), channel_id=1, source_target_pairs={{0,1},{1,0},{2,3},{3,2},{4,5},{5,4},{6,7},{7,6},{8,9},{9,8},{10,11... | collective-permute-start | bytes 983048 | tf_op jit(solution)/shard_map/ppermute | solution.py:606
  (27 other events, 94.4 us)
where the time goes:
time: 128 us; the launch traced here: 127 us
  Pallas kernels  60 us (47%)
  starting transfers between devices  35 us (27%)
  waiting for transfers between devices  17.6 us (14%)
  local copies, waits for them, and re-layouts  12.3 us (10%)
  between operations  1.34 us (1%)
    pallas_call x32, Pallas kernels, __call__(): pl.pallas_call(body, out_shape=outs, in_specs=[pl.BlockSpec(memory_space=...  60 us
    ppermute x30, starting transfers between devices, swapped(): return lax.ppermute(value, BOTH, pairs)  33.8 us
    ppermute x30, waiting for transfers between devices, swapped(): return lax.ppermute(value, BOTH, pairs)  17.6 us
    unnamed x57, local copies, waits for them, and re-layouts  12.3 us
  transfers between devices with their start and end apart: 31, of which 9 were waited for; matrix products, arithmetic and copies ran while one was open for 0% of the time, Pallas kernels for 31%

commit v1 on v0

v1 whole, which is shorter than its diff:
```python
import functools
import math

import jax
import jax.numpy as jnp
from jax import lax
from jax.experimental import pallas as pl
from jax.experimental.pallas import tpu as pltpu
from jax.sharding import PartitionSpec as P

HEADS = 6
SIDE = 16
SLOTS = SIDE * SIDE
EPSILON = 1e-05
BLOCKED = -1000000000.0
LANES = 128
BLOCK = 256
SQUARE = 4
ROW = 4
PIECE = 144
HEIGHT = 48
ACROSS = PIECE // HEIGHT
SWAPPED = (0, 2, 1, 3)
BF16 = jnp.bfloat16
F32 = jnp.float32


def dot_nn(left, right):
    return jnp.dot(left, right, preferred_element_type=F32)


def dot_nt(left, right):
    return lax.dot_general(left, right, (((1,), (1,)), ((), ())), preferred_element_type=F32)


def dot_tn(left, right):
    return lax.dot_general(left, right, (((0,), (0,)), ((), ())), preferred_element_type=F32)


def norm_parts(values):
    centered = values - jnp.mean(values, axis=-1, keepdims=True)
    inverse = lax.rsqrt(jnp.mean(centered * centered, axis=-1, keepdims=True) + EPSILON)
    return centered * inverse, inverse


def norm_reverse(upstream, scaled, inverse, gain):
    lifted = upstream * gain
    return inverse * (
        lifted
        - jnp.mean(lifted, axis=-1, keepdims=True)
        - scaled * jnp.mean(lifted * scaled, axis=-1, keepdims=True)
    )


def across(vector):
    return vector[...].reshape(1, -1)


def own_share(tokens, rows):
    share = rows // (tokens.shape[1] * tokens.shape[2])
    return tokens[pl.ds(Here().section * share, share)].reshape(rows, tokens.shape[3])


def total_rows(values):
    return jnp.sum(values, axis=0, keepdims=True)


class Here:
    def __init__(self):
        member = lax.axis_index("dp")
        self.section = lax.axis_index("section")
        self.core = member % 2
        self.square = self.section * 2 + member // 2 % 2
        self.row = member // 4 % ROW


def own_share(tokens, rows):
    share = rows // (tokens.shape[1] * tokens.shape[2])
    return tokens[pl.ds(Here().section * share, share)].reshape(rows, tokens.shape[3])


def total_rows(values):
    return jnp.sum(values, axis=0, keepdims=True)


def own_share(tokens, rows):
    share = rows // (tokens.shape[1] * tokens.shape[2])
    return tokens[pl.ds(Here().section * share, share)].reshape(rows, tokens.shape[3])


def total_rows(values):
    return jnp.sum(values, axis=0, keepdims=True)


class Here:
    def __init__(self):
        member = lax.axis_index("dp")
        self.section = lax.axis_index("section")
        self.core = member % 2
        self.square = self.section * 2 + member // 2 % 2
        self.row = member // 4 % ROW


def own_share(tokens, rows):
    share = rows // (tokens.shape[1] * tokens.shape[2])
    return tokens[pl.ds(Here().section * share, share)].reshape(rows, tokens.shape[3])


def total_rows(values):
    return jnp.sum(values, axis=0, keepdims=True)


def extent(numbers, image, local, side):
    micros, images = numbers.shape[1] - FIXED, numbers.shape[0] // 2
    first = numbers[0, 0] * (micros // 2) if local else 0
    return numbers[image % images * 2 + side, FIXED + first + image // images]


def valid_column(numbers, image):
    slot = lax.broadcasted_iota(jnp.int32, (SLOTS, 1), 0)
    height, width = (extent(numbers, image, True, side) for side in range(2))
    inside = (slot // SIDE < height) & (slot % SIDE < width)
    return inside.astype(F32)


def valid_rows(numbers, images):
    return jnp.concatenate([valid_column(numbers, image) for image in range(images)], axis=0)


def column_shifts(row, first_column, last_column):
    before = jnp.where(first_column, 0.0, pltpu.roll(row, 1, 0))
    after = jnp.where(last_column, 0.0, pltpu.roll(row, SIDE - 1, 0))
    return before, after


def conv_ahead_kernel(
    extents, tokens, enlarge_from, enlarge_bias_from, taps_from, taps_bias_from, contract_from,
    gain_from, shift_from, sent, expanded, slope, active, projected, inside, filled,
    grid_cells, entering, enlarge, enlarge_bias, taps, taps_bias, contract, gain, shift, arrivals,
):
    rows, width = sent.shape
    images = rows // SLOTS
    channels = enlarge.shape[1]
    share = entering.shape[0]
    starts = range(0, channels, BLOCK)
    section = Here().section
    copies = [(tokens.at[pl.ds(section * share, share)], entering)]
    copies += [(enlarge_from.at[:, pl.ds(0, BLOCK)], enlarge.at[:, pl.ds(0, BLOCK)])]
    copies += [
        (enlarge_bias_from, enlarge_bias), (taps_from, taps), (taps_bias_from, taps_bias),
        (gain_from, gain), (shift_from, shift),
    ]
    early = len(copies)
    for start in starts:
        part = pl.ds(start, BLOCK)
        if start:
            copies.append((enlarge_from.at[:, part], enlarge.at[:, part]))
        copies.append((contract_from.at[part], contract.at[part]))
    copies = [
        pltpu.make_async_copy(source, target, arrivals.at[number])
        for number, (source, target) in enumerate(copies)
    ]
    for copy in copies:
        copy.start()
    micros, local = extents.shape[2], extents.shape[0]
    for image in range(micros * local):
        count = extents[image % local, 0, image // local] * extents[image % local, 1, image // local]
        filled[image : image + 1, :] = jnp.full((1, LANES), (count * width).astype(F32))
    slot = lax.broadcasted_iota(jnp.int32, (SLOTS, 1), 0)
    for image in range(images):
        height, across_it = (
            extents[image % local, side, section * share + image // local] for side in range(2)
        )
        held = (slot // SIDE < height) & (slot % SIDE < across_it)
        inside[image * SLOTS : (image + 1) * SLOTS, :] = held.astype(F32)
    for copy in copies[:early]:
        copy.wait()
    later = copies[early:]
    local_in = entering[...].reshape(rows, width)
    valid = inside[...]
    column = lax.broadcasted_iota(jnp.int32, (SIDE, BLOCK), 0)
    first_column, last_column = column == 0, column == SIDE - 1
    total = jnp.zeros((rows, width), F32)

    def cells_of(start):
        part = slice(start, start + BLOCK)
        if start:
            later[2 * (start // BLOCK) - 1].wait()
        cells = (dot_nn(local_in, enlarge[:, part]) + enlarge_bias[part].reshape(1, -1)) * valid
        grid_cells[start // BLOCK % 2] = cells
        expanded[:, part] = cells.astype(BF16)

    cells_of(0)
    for start in starts:
        part = slice(start, start + BLOCK)
        number = start // BLOCK
        if start + BLOCK < channels:
            cells_of(start + BLOCK)
        kernel = [taps[tap : tap + 1, part] for tap in range(9)]
        bias = taps_bias[part].reshape(1, -1)
        for image in range(images):
            base = image * SLOTS
            above = here = None
            for line in range(SIDE + 1):
                if line < SIDE:
                    row = grid_cells[number % 2, base + line * SIDE : base + (line + 1) * SIDE, :]
                    before, after = column_shifts(row, first_column, last_column)
                    sums = [
                        before * kernel[3 * a] + row * kernel[3 * a + 1] + after * kernel[3 * a + 2]
                        for a in range(3)
                    ]
                if line > 0:
                    convolved = above + sums[2] if line < SIDE else above
                    gate = jax.nn.sigmoid(convolved)
                    lit = convolved * gate
                    place = slice(base + (line - 1) * SIDE, base + line * SIDE)
                    active[place, part] = lit.astype(BF16)
                    slope[place, part] = (gate + lit * (1.0 - gate)).astype(BF16)
                if line < SIDE:
                    above = (here if line > 0 else bias) + sums[1]
                    here = bias + sums[0]
        later[2 * number].wait()
        total = total + dot_nn(active[:, part], contract[part, :])
    projected[...] = total
    scaled, _ = norm_parts(total)
    sent[...] = (local_in.astype(F32) + scaled * across(gain) + across(shift)).astype(BF16)


def head_lanes(width):
    return lax.broadcasted_iota(jnp.int32, (1, width), 1)


def attend_ahead_kernel(
    inside, sent, gain, shift, mixing_in, mixing_out, mixing_bias,
    qkv, weights, context, middle,
):
    rows, width = sent.shape
    images = rows // SLOTS
    head = width // HEADS
    factor = 1.0 / math.sqrt(head)
    entering = sent[...].astype(F32)
    scaled, _ = norm_parts(entering)
    normed = (scaled * across(gain) + across(shift)).astype(BF16)
    for start in range(0, 3 * width, width):
        part = slice(start, start + width)
        qkv[:, part] = dot_nn(normed, mixing_in[:, part]).astype(BF16)
    pair = 2 * head
    lane = head_lanes(pair)
    valid = [inside[image * SLOTS : (image + 1) * SLOTS, :] > 0.5 for image in range(images)]
    order = [(image, number) for image in range(images) for number in range(HEADS)]

    def where_of(image, number):
        at = number // 2 * pair
        return slice(image * SLOTS, (image + 1) * SLOTS), at

    def scores_of(image, number):
        place, at = where_of(image, number)
        low, high = number % 2 * head, (number % 2 + 1) * head
        keys = qkv[place, width + at : width + at + pair]
        own = jnp.where((lane >= low) & (lane < high), keys, jnp.zeros_like(keys))
        return dot_nt(own, qkv[place, at : at + pair])

    ahead = scores_of(*order[0])
    gathered = []
    for turn, (image, number) in enumerate(order):
        scores = ahead
        if turn + 1 < len(order):
            ahead = scores_of(*order[turn + 1])
        scores = jnp.where(valid[image], scores * factor, BLOCKED)
        powers = jnp.exp(scores - jnp.max(scores, axis=0, keepdims=True))
        low = (powers * (1.0 / jnp.sum(powers, axis=0, keepdims=True))).astype(BF16)
        weights[image * HEADS + number] = low
        place, at = where_of(image, number)
        gathered.append(dot_tn(low, qkv[place, 2 * width + at : 2 * width + at + pair]))
        if number % 2:
            context[place, at : at + pair] = jnp.where(lane < head, *gathered).astype(BF16)
            gathered = []
    middle[...] = entering + dot_nn(context[...], mixing_out[...]) + across(mixing_bias)


def place_tall(pieces, grad, first_row, offset):
    for low in range(first_row, first_row + grad.shape[0], 16):
        piece, inside = low // HEIGHT, low % HEIGHT
        core, square, row = piece // (SQUARE * ROW), piece // ROW % SQUARE, piece % ROW
        for lane in range(ACROSS):
            at = offset + lane * HEIGHT + inside
            pieces[core, square, row, at : at + 16, :] = grad[
                low - first_row : low - first_row + 16, lane * LANES : (lane + 1) * LANES
            ]


def place_wide(pieces, grad, first_lane, offset, first_row=0):
    for block in range(grad.shape[0] // HEIGHT):
        for lane in range(grad.shape[1] // LANES):
            row, inside = (first_lane + lane) // ACROSS, (first_lane + lane) % ACROSS
            at = offset + inside * HEIGHT
            pieces[block // SQUARE, block % SQUARE, row - first_row, at : at + HEIGHT, :] = grad[
                block * HEIGHT : (block + 1) * HEIGHT, lane * LANES : (lane + 1) * LANES
            ]


def square_at(here, core, step):
    return here.square ^ jnp.where(core == 0, step, SWAPPED[step])


def row_at(here, step):
    return step % 2 * 2 + (here.row % 2 ^ step // 2)


def hand_out(pieces, keep, send):
    here = Here()
    for target, core in ((keep, here.core), (send, 1 - here.core)):
        for step in range(SQUARE):
            square = square_at(here, core, step)
            for along in range(ROW):
                target[step * ROW + along] = pieces[core, square, row_at(here, along)]


def mlp_kernel(
    inside, middle, sensitivity, gain, shift, enlarge, enlarge_bias, contract, contract_bias,
    output, grad_middle, keep, send, small, wide_small, blocks,
):
    rows, width = middle.shape
    images = rows // SLOTS
    hidden_width = enlarge.shape[1]
    valid = inside[...]
    center = middle[...]
    scaled, inverse = norm_parts(center)
    hidden = (scaled * across(gain) + across(shift)).astype(BF16)
    grad_out = own_share(sensitivity, rows).astype(F32) * valid
    out_low = grad_out.astype(BF16)
    total = jnp.zeros((rows, width), F32)
    grad_hidden = jnp.zeros((rows, width), F32)

    def products(start):
        part = slice(start, start + BLOCK)
        return dot_nn(hidden, enlarge[:, part]), dot_nt(out_low, contract[part, :])

    ahead = products(0)
    for start in range(0, hidden_width, BLOCK):
        part = slice(start, start + BLOCK)
        widened, grad_wide = ahead
        if start + BLOCK < hidden_width:
            ahead = products(start + BLOCK)
        widened = widened + enlarge_bias[part].reshape(1, -1)
        normal_cdf = 0.5 * (1.0 + lax.erf(widened * (1.0 / math.sqrt(2.0))))
        normal_pdf = jnp.exp(-0.5 * widened * widened) * (1.0 / math.sqrt(2.0 * math.pi))
        activated = (widened * normal_cdf).astype(BF16)
        grad_wide = grad_wide * (normal_cdf + widened * normal_pdf)
        wide_small[:, part] = total_rows(grad_wide)
        wide_low = grad_wide.astype(BF16)
        total = total + dot_nn(activated, contract[part, :])
        place_tall(blocks, dot_tn(activated, out_low).astype(BF16), start, 0)
        place_wide(blocks, dot_tn(hidden, wide_low).astype(BF16), start // LANES, PIECE)
        grad_hidden = grad_hidden + dot_nt(wide_low, enlarge[:, part])
    output[...] = ((center + total + across(contract_bias)) * valid).astype(BF16)
    gradient = grad_out + norm_reverse(grad_hidden, scaled, inverse, across(gain))
    grad_middle[...] = gradient
    small[0:1, :] = total_rows(grad_out)
    small[1:2, :] = total_rows(grad_hidden * scaled)
    small[2:3, :] = total_rows(grad_hidden)
    small[3:4, :] = total_rows(gradient)
    hand_out(blocks, keep, send)


def heads_back_kernel(
    grad_middle, qkv, weights, mixing_out, grad_qkv,
):
    rows, width = grad_middle.shape
    images = rows // SLOTS
    head = width // HEADS
    factor = 1.0 / math.sqrt(head)
    grad_context = dot_nt(grad_middle[...].astype(BF16), mixing_out[...]).astype(BF16)
    pair = 2 * head
    lane = head_lanes(pair)
    order = [(image, number) for image in range(images) for number in range(HEADS)]

    def where_of(image, number):
        at = number // 2 * pair
        return slice(image * SLOTS, (image + 1) * SLOTS), at

    def weights_of(image, number):
        place, at = where_of(image, number)
        low, high = number % 2 * head, (number % 2 + 1) * head
        values = qkv[place, 2 * width + at : 2 * width + at + pair]
        own = jnp.where((lane >= low) & (lane < high), values, jnp.zeros_like(values))
        return dot_nt(own, grad_context[place, at : at + pair])

    ahead = weights_of(*order[0])
    parts = []
    for turn, (image, number) in enumerate(order):
        grad_weights = ahead
        if turn + 1 < len(order):
            ahead = weights_of(*order[turn + 1])
        place, at = where_of(image, number)
        low = weights[image * HEADS + number]
        grad_values = dot_nn(low, grad_context[place, at : at + pair])
        soft = low.astype(F32)
        lifted = soft * grad_weights
        scores_low = (lifted - soft * jnp.sum(lifted, axis=0, keepdims=True)).astype(BF16)
        queries = qkv[place, at : at + pair]
        keys = qkv[place, width + at : width + at + pair]
        parts.append(
            (dot_tn(scores_low, keys) * factor, dot_nn(scores_low, queries) * factor, grad_values)
        )
        if number % 2:
            for which in range(3):
                merged = jnp.where(lane < head, parts[0][which], parts[1][which])
                grad_qkv[place, which * width + at : which * width + at + pair] = merged.astype(
                    BF16
                )
            parts = []


def sent_back_kernel(
    sent, grad_middle, grad_qkv, context, projected, active, gain, shift, mixing_in,
    conv_gain, grad_sent, proj_low, keep, send, small, blocks,
):
    rows, width = sent.shape
    gradient = grad_middle[...]
    entering = sent[...].astype(F32)
    scaled, inverse = norm_parts(entering)
    normed = (scaled * across(gain) + across(shift)).astype(BF16)
    lifted = jnp.zeros((rows, width), F32)
    for which in range(3):
        part = slice(which * width, (which + 1) * width)
        piece = grad_qkv[:, part]
        place_wide(blocks, dot_tn(normed, piece).astype(BF16), which * width // LANES, 0)
        lifted = lifted + dot_nt(piece, mixing_in[:, part])
    mixing = dot_tn(context[...], gradient.astype(BF16)).astype(BF16)
    place_wide(blocks, mixing, 3 * width // LANES, 0)
    grad_low = (gradient + norm_reverse(lifted, scaled, inverse, across(gain))).astype(BF16)
    grad_sent[...] = grad_low
    small[0:1, :] = total_rows(lifted * scaled)
    small[1:2, :] = total_rows(lifted)
    incoming = grad_low.astype(F32)
    scaled, inverse = norm_parts(projected[...])
    low = norm_reverse(incoming, scaled, inverse, across(conv_gain)).astype(BF16)
    proj_low[...] = low
    small[2:3, :] = total_rows(incoming * scaled)
    small[3:4, :] = total_rows(incoming)
    for start in range(0, active.shape[1], BLOCK):
        part = slice(start, start + BLOCK)
        place_tall(blocks, dot_tn(active[:, part], low).astype(BF16), start, PIECE)
    hand_out(blocks, keep, send)


def conv_part(
    inside, local_in, proj_low, expanded, slope, enlarge, taps, contract, wide_small, grad_cells,
    blocks, total, first, last, first_row=0,
):
    rows = local_in.shape[0]
    images = rows // SLOTS
    valid = inside[...]
    column = lax.broadcasted_iota(jnp.int32, (SIDE, LANES), 0)
    first_column, last_column = column == 0, column == SIDE - 1

    def cells_of(start):
        part = slice(start, start + BLOCK)
        grad_conv = dot_nt(proj_low, contract[part, :]) * slope[:, part].astype(F32)
        wide_small[9:10, part] = total_rows(grad_conv)
        grad_cells[start // BLOCK % 2] = grad_conv

    cells_of(first)
    for start in range(first, last, BLOCK):
        part = slice(start, start + BLOCK)
        number = start // BLOCK
        if start + BLOCK < last:
            cells_of(start + BLOCK)
        pieces = []
        for lanes in range(0, BLOCK, LANES):
            chans = slice(start + lanes, start + lanes + LANES)
            kernel = [taps[tap : tap + 1, chans] for tap in range(9)]
            sums = [jnp.zeros((SIDE, LANES), F32) for _ in range(9)]
            outcome = []
            for image in range(images):
                base = image * SLOTS
                shifted = {}
                for line in range(SIDE):
                    for ahead in (line, line + 1):
                        if ahead < SIDE and ahead not in shifted:
                            row = grad_cells[
                                number % 2,
                                base + ahead * SIDE : base + (ahead + 1) * SIDE,
                                lanes : lanes + LANES,
                            ]
                            before, after = column_shifts(row, first_column, last_column)
                            shifted[ahead] = (after, row, before)
                    place = slice(base + line * SIDE, base + (line + 1) * SIDE)
                    cells = expanded[place, chans].astype(F32)
                    grid = jnp.zeros((SIDE, LANES), F32)
                    for a in range(3):
                        if 0 <= line + 1 - a < SIDE:
                            for b in range(3):
                                moved = shifted[line + 1 - a][b]
                                sums[3 * a + b] = sums[3 * a + b] + cells * moved
                                grid = grid + moved * kernel[3 * a + b]
                    outcome.append(grid)
            for tap in range(9):
                wide_small[tap : tap + 1, chans] = total_rows(sums[tap])
            pieces.append(jnp.concatenate(outcome, axis=0) * valid)
        grad_expanded = jnp.concatenate(pieces, axis=1)
        wide_small[10:11, part] = total_rows(grad_expanded)
        expanded_low = grad_expanded.astype(BF16)
        place_wide(
            blocks, dot_tn(local_in, expanded_low).astype(BF16), start // LANES, 0, first_row
        )
        total = total + dot_nt(expanded_low, enlarge[:, part])
    return total


def conv_back_kernel(
    inside, tokens, grad_sent, proj_low, expanded, slope, enlarge, taps, contract,
    total, early, early_wide, grad_cells,
):
    rows, width = grad_sent.shape
    total[...] = conv_part(
        inside, own_share(tokens, rows), proj_low[...], expanded, slope, enlarge, taps,
        contract, early_wide, grad_cells, early, grad_sent[...].astype(F32), 0,
        enlarge.shape[1] // 2,
    )


def small_rows(small, wide):
    mlp, sent = small
    mlp_wide, conv_wide = wide
    found = []
    for source, rows in ((mlp, 4), (sent, 4), (mlp_wide, 1), (conv_wide, 11)):
        for row in range(rows):
            for at in range(0, source.shape[1], LANES):
                found.append((source, row, at))
    return found


def conv_end_kernel(
    inside, tokens, total, proj_low, expanded, slope, enlarge, taps, contract, early, early_wide,
    mlp_small, sent_small, mlp_wide, grad_in, keep, send, pieces, conv_wide, grad_cells, short,
):
    rows, width = total.shape
    channels = enlarge.shape[1]
    half = channels // 2
    conv_wide[:, 0:half] = early_wide[:, 0:half]
    pieces[:, :, 0 : ROW // 2, 0:PIECE, :] = early[...]
    grad_in[...] = conv_part(
        inside, own_share(tokens, rows), proj_low[...], expanded, slope, enlarge, taps,
        contract, conv_wide, grad_cells, pieces, total[...], half, channels,
    ).astype(BF16)
    short[...] = jnp.zeros_like(short)
    places = small_rows((mlp_small, sent_small), (mlp_wide, conv_wide))
    for number, (source, row, at) in enumerate(places):
        piece, inside = number // 8, number % 8
        short[piece, inside : inside + 1, :] = source[row : row + 1, at : at + LANES]
    for piece in range(2 * SQUARE * ROW):
        value = short[piece]
        high = value.astype(BF16).astype(F32)
        pair = jnp.concatenate([high, value - high], axis=0).astype(BF16)
        core, square, row = piece // (SQUARE * ROW), piece // ROW % SQUARE, piece % ROW
        pieces[core, square, row, PIECE : PIECE + 16, :] = pair
    hand_out(pieces, keep, send)


def summed(parts, short):
    total = parts[0].astype(F32)
    for part in parts[1:]:
        total = total + part.astype(F32)
    if not short:
        return total.astype(BF16)
    main = total.shape[0] - short
    value = total[main : main + 8] + total[main + 8 : main + 16]
    high = value.astype(BF16).astype(F32)
    return jnp.concatenate([total[:main], high, value - high], axis=0).astype(BF16)


def add_kernel(short, count, *refs):
    parts, outs = refs[:count], refs[count:]
    at = 0
    for out in outs:
        for step in range(out.shape[0]):
            out[step] = summed([part[at + step] for part in parts], short)
        at += out.shape[0]


def join_kernel(short, own, arrived, out):
    half = own.shape[0]
    out[0:half] = own[...]
    out[half:] = arrived[...]


def pieces_of(parts):
    half = len(parts) // 2
    here = Here()
    for side in range(2):
        core = here.core if side == 0 else 1 - here.core
        step = 0
        for part in parts[side * half : (side + 1) * half]:
            for inside in range(part.shape[0]):
                square = square_at(here, core, step // ROW)
                yield core * SQUARE + square, row_at(here, step % ROW), part, inside
                step += 1


class Leaving:
    def __init__(self, stage, semaphores):
        self.stage, self.semaphores, self.copies = stage, semaphores, []

    def put(self, part, step, offset):
        slot = len(self.copies)
        for lane in range(ACROSS):
            low = offset + lane * HEIGHT
            self.stage[slot, :, lane * LANES : (lane + 1) * LANES] = part[
                step, low : low + HEIGHT, :
            ].astype(F32)
        return self.stage.at[slot], self.semaphores.at[slot]

    def tall(self, target, block, row, part, step, offset):
        source, semaphore = self.put(part, step, offset)
        at = pl.multiple_of((block * ROW + row) * HEIGHT, 16)
        self.copies.append(
            pltpu.make_async_copy(source, target.at[pl.ds(at, HEIGHT)], semaphore)
        )
        self.copies[-1].start()

    def wide(self, targets, block, row, part, step, offset):
        source, semaphore = self.put(part, step, offset)
        at = pl.multiple_of(block * HEIGHT, 16)
        span = ACROSS * LANES
        if len(targets) == 1:
            lanes = pl.ds(pl.multiple_of(row * span, LANES), span)
            self.copies.append(
                pltpu.make_async_copy(source, targets[0].at[pl.ds(at, HEIGHT), lanes], semaphore)
            )
            self.copies[-1].start()
            return
        last = pltpu.make_async_copy(source, targets[1].at[pl.ds(at, HEIGHT)], semaphore)
        self.copies.append(last)
        lanes = pl.ds(pl.multiple_of(jnp.minimum(row, ROW - 2) * span, LANES), span)
        others = pltpu.make_async_copy(source, targets[0].at[pl.ds(at, HEIGHT), lanes], semaphore)
        pl.when(row == ROW - 1)(last.start)
        pl.when(row < ROW - 1)(others.start)

    def wait(self):
        for copy in self.copies:
            copy.wait()


def mlp_end_kernel(*refs):
    (narrower, widener, stage, semaphores), parts = refs[-4:], refs[:-4]
    leaving = Leaving(stage, semaphores)
    for block, row, part, step in pieces_of(parts):
        leaving.tall(narrower, block, row, part, step, 0)
        leaving.wide((widener,), block, row, part, step, PIECE)
    leaving.wait()


def sent_end_kernel(*refs):
    (attention, mixing, projector, stage, semaphores), parts = refs[-5:], refs[:-5]
    leaving = Leaving(stage, semaphores)
    for block, row, part, step in pieces_of(parts):
        leaving.wide((attention, mixing), block, row, part, step, 0)
        leaving.tall(projector, block, row, part, step, PIECE)
    leaving.wait()


def conv_all_kernel(*refs):
    (*shorts, short, stage, semaphores), (expander, *parts) = refs[-15:], refs[-16:-15] + refs[:-16]
    leaving = Leaving(stage, semaphores)
    for block, row, part, step in pieces_of(parts):
        leaving.wide((expander,), block, row, part, step, 0)
        pair = part[step, PIECE : PIECE + 16, :].astype(F32)
        short[pl.ds(pl.multiple_of((block * ROW + row) * 8, 8), 8), :] = pair[0:8] + pair[8:16]
    (upshift, depthwise, depthshift, postgain, postshift, pregain, preshift, mixshift, midgain,
     midshift, wideshift, narrowshift) = shorts
    lanes = narrowshift.shape[0] // LANES
    wide_lanes = upshift.shape[0] // LANES
    number = 0
    for target in (narrowshift, midgain, midshift, mixshift, pregain, preshift, postgain, postshift):
        for lane in range(lanes):
            target[lane * LANES : (lane + 1) * LANES] = short[number, :]
            number += 1
    for target in (wideshift,) + (depthwise,) * 9 + (depthshift, upshift):
        for lane in range(wide_lanes):
            value = short[number : number + 1, :]
            if target is depthwise:
                tap = number // wide_lanes - 3
                target[tap : tap + 1, lane * LANES : (lane + 1) * LANES] = value
            else:
                target[lane * LANES : (lane + 1) * LANES] = value.reshape(LANES)
            number += 1
    leaving.wait()


def give_kernel(output, grad_in, own, give):
    first = Here().section == 0
    own[...] = jnp.where(first, grad_in[...], output[...])
    give[...] = jnp.where(first, output[...], grad_in[...])


def ends_kernel(filled, own, arrived, ends, means, semaphores):
    share = ends.shape[0] // 2
    local, slots, width = ends.shape[1:]
    first = Here().section
    copies = []
    for source, section in ((own, first), (arrived, 1 - first)):
        for number in range(share * local):
            copies.append(
                pltpu.make_async_copy(
                    source.at[pl.ds(number * slots, slots)],
                    ends.at[section * share + number // local, number % local],
                    semaphores.at[len(copies)],
                )
            )
            copies[-1].start()
    for source, section in ((own, first), (arrived, 1 - first)):
        for number in range(share * local):
            value = source[number * slots : (number + 1) * slots, :].astype(F32)
            square = jnp.sum(value * value, axis=0, keepdims=True)
            image = (section * share + number // local) * local + number % local
            mean = jnp.sum(square, axis=1, keepdims=True) / filled[pl.ds(image, 1), 0:1]
            means[image, :, :] = jnp.broadcast_to(jnp.sqrt(mean), (1, LANES))
    for copy in copies:
        copy.wait()


WHOLE = pl.BlockSpec(memory_space=pltpu.VMEM)
ANYWHERE = pl.BlockSpec(memory_space=pl.ANY)
REMOTE = pl.BlockSpec(memory_space=pltpu.HBM)
SCALARS = pl.BlockSpec(memory_space=pltpu.SMEM)
COST = 30
COSTS = {'conv_first': 0, 'conv_second': 30, 'conv_far': 0, 'conv_join_square': 0, 'give': 0, 'mlp_cores': 30, 'conv_cores': 30, 'conv_all': 0, 'inner_cores': 30, 'conv_total': 0, 'inner_join_square': 30, 'mlp_end': 0, 'mlp_far': 0}
BOTH = ("section", "dp")


def shape(dims, kind):
    return jax.ShapeDtypeStruct(dims, kind)


class Calls:
    def __init__(self):
        self.last = None

    def __call__(self, kernel, name, ins, outs, scratch=(), mb=8, us=0, smem=(), hbm=(), hbm_outs=()):
        count = len(ins)
        after = () if self.last is None else (self.last,)


        def body(*refs):
            token = refs[count + len(after)]
            token[...] = jnp.zeros_like(token)
            kernel(*refs[:count], *refs[count + len(after) + 1 :])

        ins = [
            pltpu.with_memory_space_constraint(value, pltpu.HBM) if place in hbm else value
            for place, value in enumerate(ins)
        ]
        outs = [
            pltpu.HBM(out.shape, out.dtype) if place in hbm_outs else out
            for place, out in enumerate(outs)
        ]
        self.last, *result = pl.pallas_call(
            body,
            out_shape=[shape((8, LANES), F32)] + outs,
            in_specs=[
                SCALARS if place in smem else REMOTE if place in hbm else WHOLE
                for place in range(count)
            ]
            + [ANYWHERE] * len(after),
            out_specs=[WHOLE]
            + [REMOTE if place in hbm_outs else WHOLE for place in range(len(outs))],
            scratch_shapes=list(scratch),
            cost_estimate=pl.CostEstimate(
                flops=1 + int(COSTS.get(name, us) * 1e9), bytes_accessed=1, transcendentals=0
            ),
            compiler_params=pltpu.CompilerParams(vmem_limit_bytes=mb * 1024 * 1024),
            name=name,
        )(*ins, *after)
        return result


    def fence(self, value, name):
        def body(after, value, token, out):
            token[...] = jnp.zeros_like(token)

        self.last, value = pl.pallas_call(
            body,
            out_shape=[shape((8, LANES), F32), shape(value.shape, value.dtype)],
            in_specs=[ANYWHERE] * 2,
            out_specs=[WHOLE, ANYWHERE],
            input_output_aliases={1: 1},
            cost_estimate=pl.CostEstimate(
                flops=1 + int(COSTS.get(name, 0) * 1e9), bytes_accessed=1, transcendentals=0
            ),
            compiler_params=pltpu.CompilerParams(vmem_limit_bytes=1024 * 1024),
            name=name,
        )(self.last, value)
        return value


def swapped(value, digit, step=0):
    sections, members = (lax.axis_size(axis) for axis in BOTH)
    pairs = []
    for section in range(sections):
        for member in range(members):
            if digit == "first" or digit == "second":
                across = 2 if digit == "first" else 1
            else:
                across = step if digit == "square" else 0
            if member % 2:
                across = SWAPPED[across]
            along = {"near": 4}.get(digit, digit if isinstance(digit, int) else 0)
            other = (section ^ across // 2) * members + (member ^ (across % 2 * 2 + along))
            pairs.append((section * members + member, other))
    return lax.ppermute(value, BOTH, pairs)


class Group:
    def __init__(self, name, calls, keep, send, short=0, cost=COST):
        self.name, self.calls, self.short, self.cost = name, calls, short, cost
        self.rows = keep.shape[1]
        self.parts = [keep, swapped(send, 1)]

    def call(self, kernel, what, ins, outs):
        return self.calls(
            functools.partial(kernel, self.short), f"{self.name}_{what}", ins,
            [shape((count, self.rows, LANES), BF16) for count in outs], us=self.cost,
        )

    def add(self, what, outs=1):
        pieces = [self.parts[0].shape[0] // outs] * outs
        kernel = lambda short, *refs: add_kernel(short, len(self.parts), *refs)
        return self.call(kernel, what, self.parts, pieces)

    def halve(self, what):
        keep, send = self.add(what, 2)
        self.parts = [keep, swapped(send, what)]

    def first(self):
        self.halve("first")

    def second(self):
        self.halve("second")

    def square(self):
        keep, *send = self.add("square", SQUARE)
        self.parts = [keep] + [swapped(part, "square", 1 + at) for at, part in enumerate(send)]

    def near(self):
        self.halve("near")

    def far(self):
        stride, what = 4, "far"
        while stride < lax.axis_size("dp") // 2:
            stride *= 2
            (own,) = self.add(what)
            self.parts, what = [own, swapped(own, stride)], f"over_{stride}"

    def total(self):
        (own,) = self.add("total")
        self.parts = [own, swapped(own, "near")]

    def join(self, what):
        (own,) = self.call(join_kernel, what, self.parts, [2 * self.parts[0].shape[0]])
        return own

    def join_row(self):
        own = self.join("join_row")
        self.parts = [own, swapped(own, "second")]

    def join_square(self):
        own = self.join("join_square")
        self.parts = [own, swapped(own, "first")]
        self.near_half = swapped(own, 1)

    def join_cores(self):
        far_half = self.calls.fence(self.parts[1], f"{self.name}_cores")
        self.blocks = [self.parts[0], far_half, self.near_half, swapped(far_half, 1)]

    def join_all(self):
        own = self.join("join_row")
        self.parts = [own] + [swapped(own, "square", step) for step in range(1, SQUARE)]
        self.blocks = self.parts + [swapped(part, 1) for part in self.parts]


def shards(
    entering_tokens,
    output_sensitivity,
    picture_tile_extents,
    pointwise_enlarge,
    enlarge_bias,
    channelwise_kernel,
    channelwise_conv_bias,
    pointwise_contract,
    convblock_scale,
    convblock_offset,
    attend_scale,
    attend_offset,
    query_key_proj,
    heads_output_proj,
    heads_output_bias,
    feedforward_scale,
    feedforward_offset,
    feedforward_enlarge,
    feedforward_enlarge_bias,
    feedforward_contract,
    contract_bias,
):
    micro_count, local_images, slots, width = entering_tokens.shape
    channels = pointwise_enlarge.shape[1]
    share = micro_count // 2
    images = share * local_images
    rows = images * slots
    call = Calls()
    extents = jnp.transpose(picture_tile_extents, (1, 2, 0))
    sent, expanded, slope, active, projected, inside, filled = call(
        conv_ahead_kernel, "conv_ahead",
        (extents, entering_tokens, pointwise_enlarge, enlarge_bias, channelwise_kernel,
         channelwise_conv_bias, pointwise_contract, convblock_scale, convblock_offset),
        [shape((rows, width), BF16), shape((rows, channels), BF16), shape((rows, channels), BF16),
         shape((rows, channels), BF16), shape((rows, width), F32), shape((rows, 1), F32),
         shape((micro_count * local_images, LANES), F32)],
        [pltpu.VMEM((2, rows, BLOCK), F32), pltpu.VMEM((share, local_images, slots, width), BF16)]
        + [pltpu.VMEM(value.shape, value.dtype) for value in
           (pointwise_enlarge, enlarge_bias, channelwise_kernel, channelwise_conv_bias,
            pointwise_contract, convblock_scale, convblock_offset)]
        + [pltpu.SemaphoreType.DMA((6 + 2 * channels // BLOCK,))],
        mb=20, smem=(0,), hbm=range(1, 9),
    )
    qkv, weights, context, middle = call(
        attend_ahead_kernel, "attend_ahead",
        (inside, sent, attend_scale, attend_offset, query_key_proj, heads_output_proj,
         heads_output_bias),
        [shape((rows, 3 * width), BF16), shape((images * HEADS, slots, slots), BF16),
         shape((rows, width), BF16), shape((rows, width), F32)], mb=16,
    )
    halves = [shape((SQUARE * ROW, 2 * PIECE, LANES), BF16)] * 2
    whole = [pltpu.VMEM((2, SQUARE, ROW, 2 * PIECE, LANES), BF16)]
    output, grad_middle, keep, send, mlp_small, mlp_wide = call(
        mlp_kernel, "mlp",
        (inside, middle, output_sensitivity, feedforward_scale, feedforward_offset, feedforward_enlarge,
         feedforward_enlarge_bias, feedforward_contract, contract_bias),
        [shape((rows, width), BF16), shape((rows, width), F32)] + halves
        + [shape((8, width), F32), shape((1, channels), F32)],
        whole, mb=24,
    )
    mlp = Group("mlp", call, keep, send)
    (grad_qkv,) = call(
        heads_back_kernel, "heads_back", (grad_middle, qkv, weights, heads_output_proj),
        [shape((rows, 3 * width), BF16)], mb=16,
    )
    mlp.first()
    grad_sent, proj_low, keep, send, sent_small = call(
        sent_back_kernel, "sent_back",
        (sent, grad_middle, grad_qkv, context, projected, active, attend_scale, attend_offset,
         query_key_proj, convblock_scale),
        [shape((rows, width), BF16), shape((rows, width), BF16)] + halves
        + [shape((8, width), F32)],
        whole, mb=24,
    )
    inner = Group("inner", call, keep, send)
    early_pieces = shape((2, SQUARE, ROW // 2, PIECE, LANES), BF16)
    total, early, early_wide = call(
        conv_back_kernel, "conv_back",
        (inside, entering_tokens, grad_sent, proj_low, expanded, slope, pointwise_enlarge,
         channelwise_kernel, pointwise_contract),
        [shape((rows, width), F32), early_pieces, shape((16, channels), F32)],
        [pltpu.VMEM((2, rows, BLOCK), F32)], mb=20,
    )
    mlp.second()
    inner.first()
    halves = [shape((SQUARE * ROW, PIECE + 16, LANES), BF16)] * 2
    grad_in, keep, send = call(
        conv_end_kernel, "conv_end",
        (inside, entering_tokens, total, proj_low, expanded, slope, pointwise_enlarge, channelwise_kernel,
         pointwise_contract, early, early_wide, mlp_small, sent_small, mlp_wide),
        [shape((rows, width), BF16)] + halves,
        [pltpu.VMEM((2, SQUARE, ROW, PIECE + 16, LANES), BF16), pltpu.VMEM((16, channels), F32),
         pltpu.VMEM((2, rows, BLOCK), F32), pltpu.VMEM((2 * SQUARE * ROW, 8, LANES), F32)],
        mb=20,
    )
    conv = Group("conv", call, keep, send, 16)
    line, wide_line = shape((width,), F32), shape((channels,), F32)
    tall, wide = shape((channels, width), F32), shape((width, channels), F32)
    pieces = 2 * SQUARE * ROW

    def leaving(count):
        return [pltpu.VMEM((count, HEIGHT, ACROSS * LANES), F32), pltpu.SemaphoreType.DMA((count,))]

    mlp.near()
    conv.first()
    inner.second()
    mlp.far()
    conv.second()
    own, give = call(
        give_kernel, "give", (output, grad_in), [shape((rows, width), BF16)] * 2, us=COST
    )
    arrived = lax.ppermute(give, "section", [(0, 1), (1, 0)])
    inner.near()
    conv.near()
    mlp.total()
    inner.far()
    conv.far()
    mlp.join_row()
    ends, means = call(
        ends_kernel, "ends", (filled, own, arrived),
        [shape(entering_tokens.shape, BF16), shape((micro_count * local_images, 1, LANES), F32)],
        [pltpu.SemaphoreType.DMA((micro_count * local_images,))], hbm_outs=(0,), us=COST,
    )
    inner.total()
    mlp.join_square()
    conv.total()
    inner.join_row()
    conv.join_row()
    mlp.join_cores()
    conv.join_square()
    inner.join_square()
    narrower, widener = call(
        mlp_end_kernel, "mlp_end", mlp.blocks, [tall, wide], leaving(2 * pieces), mb=12,
        hbm_outs=(0, 1), us=COST,
    )
    inner.join_cores()
    conv.join_cores()
    attention, mixing, projector = call(
        sent_end_kernel, "sent_end", inner.blocks,
        [shape((width, 3 * width), F32), shape((width, width), F32), tall],
        leaving(2 * pieces), mb=12, hbm_outs=(0, 1, 2), us=COST,
    )
    (expander, upshift, depthwise, depthshift, postgain, postshift, pregain, preshift, mixshift,
     midgain, midshift, wideshift, narrowshift) = call(
        conv_all_kernel, "conv_all", conv.blocks,
        [wide, wide_line, shape((9, channels), F32), wide_line] + [line] * 7 + [wide_line, line],
        [pltpu.VMEM((pieces * 8, LANES), F32)] + leaving(pieces), hbm_outs=(0,), us=COST,
    )
    means = means[:, 0, 0].reshape(1, micro_count, local_images)
    return (
        ends[None], means, expander, upshift, depthwise, depthshift, projector, postgain,
        postshift, pregain, preshift, attention, mixing, mixshift, midgain, midshift, widener,
        wideshift, narrower, narrowshift,
    )


def solution(mesh):
    tokens = P(None, "dp", None, None)
    placed = (tokens, tokens, P(None, "dp", None)) + (P(),) * 18
    return jax.shard_map(
        shards,
        mesh=mesh,
        in_specs=placed,
        out_specs=(P("section", None, "dp", None, None), P("section", None, "dp")) + (P(),) * 18,
        check_vma=False,
    )
```

time: 128 us -> 110 us (0.86)
  Pallas kernels: 60 us -> 41.6 us
  local copies, waits for them, and re-layouts: 12.3 us -> 1.38 us
  starting transfers between devices: 35 us -> 41.9 us
  waiting for transfers between devices: 17.6 us -> 23.7 us
    pallas_call x32 -> x36, Pallas kernels: 60 us -> 41.6 us  [the longest x33 41.6 us: __call__(): pl.pallas_call(body, out_shape=[shape((8, LANES), F32)] + outs, in_specs=...]
    unnamed x57 -> x36, local copies, waits for them, and re-layouts: 12.3 us -> 0.75 us
    ppermute x30, starting transfers between devices: 33.8 us -> 41 us  [swapped(): return lax.ppermute(value, BOTH, pairs)]
    ppermute x30, waiting for transfers between devices: 17.6 us -> 23.7 us  [swapped(): return lax.ppermute(value, BOTH, pairs)]
  transfers between devices with their start and end apart: 31 -> 31, of which waited for: 9 -> 12; matrix products, arithmetic and copies ran while one was open for 0% -> 1% of each run, Pallas kernels for 31% -> 20%
where the time goes in v1:
time: 110 us
  starting transfers between devices  41.9 us (38%)
  Pallas kernels  41.6 us (38%)
  waiting for transfers between devices  23.7 us (22%)
  local copies, waits for them, and re-layouts  1.38 us (1%)
  between operations  1.27 us (1%)
    pallas_call x33, Pallas kernels, __call__(): pl.pallas_call(body, out_shape=[shape((8, LANES), F32)] + outs, in_specs=...  41.6 us
    ppermute x30, starting transfers between devices, swapped(): return lax.ppermute(value, BOTH, pairs)  41 us
    ppermute x30, waiting for transfers between devices, swapped(): return lax.ppermute(value, BOTH, pairs)  23.7 us
  transfers between devices with their start and end apart: 31, of which 12 were waited for; matrix products, arithmetic and copies ran while one was open for 1% of the time, Pallas kernels for 20%

profile of v1, /device:TPU:1, one launch (start us, length us, event | category | flops | bytes accessed | tf_op | source)
XLA Modules:
  0.0 109.9 jit_solution(14346343621677559115)
XLA Ops:
  1.4 7.8 %conv_ahead.1 = (f32[8,128]{1,0:T(8,128)S(1)}, bf16[512,384]{1,0:T(8,128)(2,1)S(1)}, bf16[512,1536]{1,0:T(8,128)(2,1)S(1)}, bf16[512,1536]{1,0:T(8,128)(2,1)S(1)...) custom-call(s32[1,2,4]{2,1,0:T(2,128)S(1)} %bitcast.5, ...), custom_call_target="tpu_custom_call" | custom-call | flops 1 | bytes 1 | tf_op jit(solution)/shard_map/conv_ahead/pallas_call | solution.py:759
  9.3 3.0 %attend_ahead.1 = (f32[8,128]{1,0:T(8,128)S(1)}, bf16[512,1152]{1,0:T(8,128)(2,1)S(1)}, bf16[12,256,256]{2,1,0:T(8,128)(2,1)S(1)}, bf16[512,384]{1,0:T(8,128)(2,1)S(1)}, f32[512,384]{1,0:T(8,128)S(1)}) custom-call(f32[512,1]{1,0:T(8,128)S(1)} %get-tuple-element.140.refs_0_, bf16[512,384]{1,0:T(8,128)(2,1)S(1)} %get-tuple-element.141.refs_1_.refs_0_, ...), custom_call_target="tpu_custom_call" | custom-call | flops 1 | bytes 1 | tf_op jit(solution)/shard_map/attend_ahead/pallas_call | solution.py:759
  12.3 6.4 %mlp.1 = (f32[8,128]{1,0:T(8,128)S(1)}, bf16[512,384]{1,0:T(8,128)(2,1)S(1)}, f32[512,384]{1,0:T(8,128)S(1)}, bf16[16,288,128]{2,1,0:T(8,128)(2,1)S(1)}, bf16[16...) custom-call(f32[512,1]{1,0:T(8,128)S(1)} %get-tuple-element.140.refs_0_, ...), custom_call_target="tpu_custom_call" | custom-call | flops 1 | bytes 1 | tf_op jit(solution)/shard_map/mlp/pallas_call | solution.py:759
  18.9 2.7 %heads_back.1 = (f32[8,128]{1,0:T(8,128)S(1)}, bf16[512,1152]{1,0:T(8,128)(2,1)S(1)}) custom-call(f32[512,384]{1,0:T(8,128)S(1)} %get-tuple-element.146.refs_0_.refs_1_, bf16[512,1152]{1,0:T(8,128)(2,1)S(1)} %get-tuple-element.147.refs_1_, bf16[12,256,256]{2,1,0:T(8,128)(2,1)S(1)} %get-tuple-element.148.refs_2_, bf16[384,384]{1,0:T(8,128)(2,1)S(1)} %copy-done.4, ...), custom_call_target="tpu_custom_call" | custom-call | flops 1 | bytes 1 | tf_op jit(solution)/shard_map/heads_back/pallas_call | solution.py:759
  22.0 2.7 %collective-permute-start.2 = (bf16[8,288,128]{2,1,0:T(8,128)(2,1)S(1)}, bf16[8,288,128]{2,1,0:T(8,128)(2,1)S(1)}, u32[]{:S(2)}, u32[]{:S(2)}) collective-permute-start(bf16[8,288,128]{2,1,0:T(8,128)(2,1)S(1)} %get-tuple-element.172), channel_id=1, source_target_pairs={{0,16},{1,3},{2,18},{3,1},{4,20},{5,7},{6,22},{7,5},{8,24},{9,11},... | collective-permute-start | bytes 1769480 | tf_op jit(solution)/shard_map/ppermute | solution.py:812
  24.7 3.7 %sent_back.1 = (f32[8,128]{1,0:T(8,128)S(1)}, bf16[512,384]{1,0:T(8,128)(2,1)S(1)}, bf16[512,384]{1,0:T(8,128)(2,1)S(1)}, bf16[16,288,128]{2,1,0:T(8,128)(2,1)S(...) custom-call(bf16[512,384]{1,0:T(8,128)(2,1)S(1)} %get-tuple-element.141.refs_1_.refs_0_, ...), custom_call_target="tpu_custom_call" | custom-call | flops 1 | bytes 1 | tf_op jit(solution)/shard_map/sent_back/pallas_call | solution.py:759
  28.8 3.5 %conv_back.1 = (f32[8,128]{1,0:T(8,128)S(1)}, f32[512,384]{1,0:T(8,128)S(1)}, bf16[2,4,2,144,128]{4,3,2,1,0:T(8,128)(2,1)S(1)}, f32[16,1536]{1,0:T(8,128)S(1)}) custom-call(f32[512,1]{1,0:T(8,128)S(1)} %get-tuple-element.140.refs_0_, bf16[4,1,256,384]{3,2,1,0:T(8,128)(2,1)S(1)} %copy-done.2, bf16[512,384]{1,0:T(8,128)(2,1)S(1)} %get-tuple-element.158.refs_2_, ...), custom_call_target="tpu_custom_call" | custom-call | flops 1 | bytes 1 | tf_op jit(solution)/shard_map/conv_back/pallas_call | solution.py:759
  32.4 1.4 %collective-permute-start.4 = (bf16[4,288,128]{2,1,0:T(8,128)(2,1)S(1)}, bf16[4,288,128]{2,1,0:T(8,128)(2,1)S(1)}, u32[]{:S(2)}, u32[]{:S(2)}) collective-permute-start(bf16[4,288,128]{2,1,0:T(8,128)(2,1)S(1)} %get-tuple-element.180), channel_id=1, source_target_pairs={{0,2},{1,17},{2,0},{3,19},{4,6},{5,21},{6,4},{7,23},{8,10},{9,25},... | collective-permute-start | bytes 884744 | tf_op jit(solution)/shard_map/ppermute | solution.py:812
  34.4 1.3 %collective-permute-start.7 = (bf16[8,288,128]{2,1,0:T(8,128)(2,1)S(1)}, bf16[8,288,128]{2,1,0:T(8,128)(2,1)S(1)}, u32[]{:S(2)}, u32[]{:S(2)}) collective-permute-start(bf16[8,288,128]{2,1,0:T(8,128)(2,1)S(1)} %get-tuple-element.188), channel_id=1, source_target_pairs={{0,16},{1,3},{2,18},{3,1},{4,20},{5,7},{6,22},{7,5},{8,24},{9,11},... | collective-permute-start | bytes 1769480 | tf_op jit(solution)/shard_map/ppermute | solution.py:812
  35.7 3.6 %conv_end.1 = (f32[8,128]{1,0:T(8,128)S(1)}, bf16[512,384]{1,0:T(8,128)(2,1)S(1)}, bf16[16,160,128]{2,1,0:T(8,128)(2,1)S(1)}, bf16[16,160,128]{2,1,0:T(8,128)(2,1)S(1)}) custom-call(f32[512,1]{1,0:T(8,128)S(1)} %get-tuple-element.140.refs_0_, bf16[4,1,256,384]{3,2,1,0:T(8,128)(2,1)S(1)} %copy-done.2, f32[512,384]{1,0:T(8,128)S(1)} %get-tuple-element.163.refs_2_, ...), custom_call_target="tpu_custom_call" | custom-call | flops 1 | bytes 1 | tf_op jit(solution)/shard_map/conv_end/pallas_call | solution.py:759
  39.3 1.6 %collective-permute-start.3 = (bf16[16,160,128]{2,1,0:T(8,128)(2,1)S(1)}, bf16[16,160,128]{2,1,0:T(8,128)(2,1)S(1)}, u32[]{:S(2)}, u32[]{:S(2)}) collective-permute-start(bf16[16,160,128]{2,1,0:T(8,128)(2,1)S(1)} %get-tuple-element.178), channel_id=1, source_target_pairs={{0,1},{1,0},{2,3},{3,2},{4,5},{5,4},{6,7},{7,6},{8,9},{9,8},{10,11... | collective-permute-start | bytes 1966088 | tf_op jit(solution)/shard_map/ppermute | solution.py:812
  41.0 1.4 %collective-permute-start.6 = (bf16[2,288,128]{2,1,0:T(8,128)(2,1)S(1)}, bf16[2,288,128]{2,1,0:T(8,128)(2,1)S(1)}, u32[]{:S(2)}, u32[]{:S(2)}) collective-permute-start(bf16[2,288,128]{2,1,0:T(8,128)(2,1)S(1)} %get-tuple-element.186), channel_id=1, source_target_pairs={{0,4},{1,5},{2,6},{3,7},{4,0},{5,1},{6,2},{7,3},{8,12},{9,13},{10,... | collective-permute-start | bytes 442376 | tf_op jit(solution)/shard_map/ppermute | solution.py:812
  43.1 2.3 %collective-permute-done.7.refs_1_ = bf16[8,288,128]{2,1,0:T(8,128)(2,1)S(1)} collective-permute-done((bf16[8,288,128]{2,1,0:T(8,128)(2,1)S(1)}, bf16[8,288,128]{2,1,0:T(8,128)(2,1)S(1)}, u32[]{:S(2)}, u32[]{:S(2)}) %collective-permute-start.7) | collective-permute-done | bytes 589856 | tf_op jit(solution)/shard_map/ppermute | solution.py:812
  45.7 2.9 %collective-permute-start.9 = (bf16[2,288,128]{2,1,0:T(8,128)(2,1)S(1)}, bf16[2,288,128]{2,1,0:T(8,128)(2,1)S(1)}, u32[]{:S(2)}, u32[]{:S(2)}) collective-permute-start(bf16[2,288,128]{2,1,0:T(8,128)(2,1)S(1)} %get-tuple-element.195.refs_0_), channel_id=1, source_target_pairs={{0,8},{1,9},{2,10},{3,11},{4,12},{5,13},{6,14},{7,15},{8,0},{9,1},... | collective-permute-start | bytes 442376 | tf_op jit(solution)/shard_map/ppermute | solution.py:812
  50.5 4.5 %collective-permute-done.11.refs_1_ = bf16[4,288,128]{2,1,0:T(8,128)(2,1)S(1)} collective-permute-done((bf16[4,288,128]{2,1,0:T(8,128)(2,1)S(1)}, bf16[4,288,128]{2,1,0:T(8,128)(2,1)S(1)}, u32[]{:S(2)}, u32[]{:S(2)}) %collective-permute-start.11) | collective-permute-done | bytes 294944 | tf_op jit(solution)/shard_map/ppermute | solution.py:812
  56.8 1.3 %collective-permute-start.13 = (bf16[2,160,128]{2,1,0:T(8,128)(2,1)S(1)}, bf16[2,160,128]{2,1,0:T(8,128)(2,1)S(1)}, u32[]{:S(2)}, u32[]{:S(2)}) collective-permute-start(bf16[2,160,128]{2,1,0:T(8,128)(2,1)S(1)} %get-tuple-element.205), channel_id=1, source_target_pairs={{0,4},{1,5},{2,6},{3,7},{4,0},{5,1},{6,2},{7,3},{8,12},{9,13},{10,... | collective-permute-start | bytes 245768 | tf_op jit(solution)/shard_map/ppermute | solution.py:812
  59.3 2.5 %collective-permute-start.17 = (bf16[2,288,128]{2,1,0:T(8,128)(2,1)S(1)}, bf16[2,288,128]{2,1,0:T(8,128)(2,1)S(1)}, u32[]{:S(2)}, u32[]{:S(2)}) collective-permute-start(bf16[2,288,128]{2,1,0:T(8,128)(2,1)S(1)} %get-tuple-element.216.refs_0_), channel_id=1, source_target_pairs={{0,8},{1,9},{2,10},{3,11},{4,12},{5,13},{6,14},{7,15},{8,0},{9,1},... | collective-permute-start | bytes 442376 | tf_op jit(solution)/shard_map/ppermute | solution.py:812
  61.9 1.3 %collective-permute-start.15 = (bf16[2,160,128]{2,1,0:T(8,128)(2,1)S(1)}, bf16[2,160,128]{2,1,0:T(8,128)(2,1)S(1)}, u32[]{:S(2)}, u32[]{:S(2)}) collective-permute-start(bf16[2,160,128]{2,1,0:T(8,128)(2,1)S(1)} %get-tuple-element.214.refs_0_), channel_id=1, source_target_pairs={{0,8},{1,9},{2,10},{3,11},{4,12},{5,13},{6,14},{7,15},{8,0},{9,1},... | collective-permute-start | bytes 245768 | tf_op jit(solution)/shard_map/ppermute | solution.py:812
  63.2 2.3 %collective-permute-done.12.refs_1_ = bf16[2,288,128]{2,1,0:T(8,128)(2,1)S(1)} collective-permute-done((bf16[2,288,128]{2,1,0:T(8,128)(2,1)S(1)}, bf16[2,288,128]{2,1,0:T(8,128)(2,1)S(1)}, u32[]{:S(2)}, u32[]{:S(2)}) %collective-permute-start.12) | collective-permute-done | bytes 147488 | tf_op jit(solution)/shard_map/ppermute | solution.py:812
  66.6 2.0 %collective-permute-start.19 = (bf16[2,288,128]{2,1,0:T(8,128)(2,1)S(1)}, bf16[2,288,128]{2,1,0:T(8,128)(2,1)S(1)}, u32[]{:S(2)}, u32[]{:S(2)}) collective-permute-start(bf16[2,288,128]{2,1,0:T(8,128)(2,1)S(1)} %get-tuple-element.221.refs_0_), channel_id=1, source_target_pairs={{0,4},{1,5},{2,6},{3,7},{4,0},{5,1},{6,2},{7,3},{8,12},{9,13},{10,... | collective-permute-start | bytes 442376 | tf_op jit(solution)/shard_map/ppermute | solution.py:812
  68.6 2.8 %collective-permute-done.16.refs_1_ = bf16[4,288,128]{2,1,0:T(8,128)(2,1)S(1)} collective-permute-done((bf16[4,288,128]{2,1,0:T(8,128)(2,1)S(1)}, bf16[4,288,128]{2,1,0:T(8,128)(2,1)S(1)}, u32[]{:S(2)}, u32[]{:S(2)}) %collective-permute-start.16) | collective-permute-done | bytes 294944 | tf_op jit(solution)/shard_map/ppermute | solution.py:812
  71.5 4.9 %collective-permute-start.22 = (bf16[8,288,128]{2,1,0:T(8,128)(2,1)S(1)}, bf16[8,288,128]{2,1,0:T(8,128)(2,1)S(1)}, u32[]{:S(2)}, u32[]{:S(2)}) collective-permute-start(bf16[8,288,128]{2,1,0:T(8,128)(2,1)S(1)} %get-tuple-element.226.refs_0_), channel_id=1, source_target_pairs={{0,1},{1,0},{2,3},{3,2},{4,5},{5,4},{6,7},{7,6},{8,9},{9,8},{10,11... | collective-permute-start | bytes 1769480 | tf_op jit(solution)/shard_map/ppermute | solution.py:812
  79.5 1.8 %collective-permute-done.18.refs_1_ = bf16[2,160,128]{2,1,0:T(8,128)(2,1)S(1)} collective-permute-done((bf16[2,160,128]{2,1,0:T(8,128)(2,1)S(1)}, bf16[2,160,128]{2,1,0:T(8,128)(2,1)S(1)}, u32[]{:S(2)}, u32[]{:S(2)}) %collective-permute-start.18) | collective-permute-done | bytes 81952 | tf_op jit(solution)/shard_map/ppermute | solution.py:812
  81.3 2.0 %collective-permute-start.20 = (bf16[4,160,128]{2,1,0:T(8,128)(2,1)S(1)}, bf16[4,160,128]{2,1,0:T(8,128)(2,1)S(1)}, u32[]{:S(2)}, u32[]{:S(2)}) collective-permute-start(bf16[4,160,128]{2,1,0:T(8,128)(2,1)S(1)} %get-tuple-element.224.refs_0_), channel_id=1, source_target_pairs={{0,2},{1,17},{2,0},{3,19},{4,6},{5,21},{6,4},{7,23},{8,10},{9,25},... | collective-permute-start | bytes 491528 | tf_op jit(solution)/shard_map/ppermute | solution.py:812
  83.3 4.0 %collective-permute-done.21.value = bf16[8,288,128]{2,1,0:T(8,128)(2,1)S(1)} collective-permute-done((bf16[8,288,128]{2,1,0:T(8,128)(2,1)S(1)}, bf16[8,288,128]{2,1,0:T(8,128)(2,1)S(1)}, u32[]{:S(2)}, u32[]{:S(2)}) %collective-permute-start.21) | collective-permute-done | bytes 589856 | tf_op jit(solution)/shard_map/ppermute | solution.py:812
  87.3 3.3 %collective-permute-start.23 = (bf16[8,288,128]{2,1,0:T(8,128)(2,1)S(1)}, bf16[8,288,128]{2,1,0:T(8,128)(2,1)S(1)}, u32[]{:S(2)}, u32[]{:S(2)}) collective-permute-start(bf16[8,288,128]{2,1,0:T(8,128)(2,1)S(1)} %get-tuple-element.229.refs_1_), channel_id=1, source_target_pairs={{0,1},{1,0},{2,3},{3,2},{4,5},{5,4},{6,7},{7,6},{8,9},{9,8},{10,11... | collective-permute-start | bytes 1769480 | tf_op jit(solution)/shard_map/ppermute | solution.py:812
  90.7 1.9 %collective-permute-start.25 = (bf16[8,288,128]{2,1,0:T(8,128)(2,1)S(1)}, bf16[8,288,128]{2,1,0:T(8,128)(2,1)S(1)}, u32[]{:S(2)}, u32[]{:S(2)}) collective-permute-start(bf16[8,288,128]{2,1,0:T(8,128)(2,1)S(1)} %get-tuple-element.234.refs_0_), channel_id=1, source_target_pairs={{0,16},{1,3},{2,18},{3,1},{4,20},{5,7},{6,22},{7,5},{8,24},{9,11},... | collective-permute-start | bytes 1769480 | tf_op jit(solution)/shard_map/ppermute | solution.py:812
  95.5 2.8 %mlp_end.1 = (f32[8,128]{1,0:T(8,128)S(1)}, f32[1536,384]{1,0:T(8,128)}, f32[384,1536]{1,0:T(8,128)}) custom-call(bf16[8,288,128]{2,1,0:T(8,128)(2,1)S(1)} %get-tuple-element.226.refs_0_, bf16[8,288,128]{2,1,0:T(8,128)(2,1)S(1)} %get-tuple-element.229.refs_1_, bf16[8,288,128]{2,1,0:T(8,128)(2,1)S(1)} %collective-permute-done.22.refs_2_, ...), custom_call_target="tpu_custom_call" | custom-call | flops 1 | bytes 1 | tf_op jit(solution)/shard_map/mlp_end/pallas_call | solution.py:759
  98.3 1.9 %collective-permute-done.25.value = bf16[8,288,128]{2,1,0:T(8,128)(2,1)S(1)} collective-permute-done((bf16[8,288,128]{2,1,0:T(8,128)(2,1)S(1)}, bf16[8,288,128]{2,1,0:T(8,128)(2,1)S(1)}, u32[]{:S(2)}, u32[]{:S(2)}) %collective-permute-start.25) | collective-permute-done | bytes 589856 | tf_op jit(solution)/shard_map/ppermute | solution.py:812
  100.9 2.8 %collective-permute-done.26.value = bf16[8,160,128]{2,1,0:T(8,128)(2,1)S(1)} collective-permute-done((bf16[8,160,128]{2,1,0:T(8,128)(2,1)S(1)}, bf16[8,160,128]{2,1,0:T(8,128)(2,1)S(1)}, u32[]{:S(2)}, u32[]{:S(2)}) %collective-permute-start.26) | collective-permute-done | bytes 327712 | tf_op jit(solution)/shard_map/ppermute | solution.py:812
  104.5 2.8 %sent_end.1 = (f32[8,128]{1,0:T(8,128)S(1)}, f32[384,1152]{1,0:T(8,128)}, f32[384,384]{1,0:T(8,128)}, f32[1536,384]{1,0:T(8,128)}) custom-call(bf16[8,288,128]{2,1,0:T(8,128)(2,1)S(1)} %get-tuple-element.234.refs_0_, bf16[8,288,128]{2,1,0:T(8,128)(2,1)S(1)} %get-tuple-element.237.refs_1_, bf16[8,288,128]{2,1,0:T(8,128)(2,1)S(1)} %collective-permute-done.29.refs_2_, ...), custom_call_target="tpu_custom_call" | custom-call | flops 30000001024 | bytes 1 | tf_op jit(solution)/shard_map/sent_end/pallas_call | solution.py:759
  107.3 2.4 %conv_all.1 = (f32[8,128]{1,0:T(8,128)}, f32[384,1536]{1,0:T(8,128)}, f32[1536]{0:T(1024)}, f32[9,1536]{1,0:T(8,128)}, f32[1536]{0:T(1024)}, /*index=5*/f32[384]...) custom-call(bf16[8,160,128]{2,1,0:T(8,128)(2,1)S(1)} %get-tuple-elem, ...), custom_call_target="tpu_custom_call" | custom-call | flops 1 | bytes 1 | tf_op jit(solution)/shard_map/conv_all/pallas_call | solution.py:759
  (103 shorter events, 16.8 us)
Async XLA Ops:
  1.4 10.9 %copy-start.6 = (bf16[1536,384]{1,0:T(8,128)(2,1)S(1)}, bf16[1536,384]{1,0:T(8,128)(2,1)}, u32[]{:S(2)}) copy-start(bf16[1536,384]{1,0:T(8,128)(2,1)} %refs_7_.6) | copy-start | bytes 3538948
  18.8 2.9 %collective-permute-start = (bf16[16,288,128]{2,1,0:T(8,128)(2,1)S(1)}, bf16[16,288,128]{2,1,0:T(8,128)(2,1)S(1)}, u32[]{:S(2)}, u32[]{:S(2)}) collective-permute-start(bf16[16,288,128]{2,1,0:T(8,128)(2,1)S(1)} %get-tuple-element.155), channel_id=1, source_target_pairs={{0,1},{1,0},{2,3},{3,2},{4,5},{5,4},{6,7},{7,6},{8,9},{9,8},{10,11... | collective-permute-start | bytes 3538952 | tf_op jit(solution)/shard_map/ppermute | solution.py:812
  22.0 10.3 %collective-permute-start.2 = (bf16[8,288,128]{2,1,0:T(8,128)(2,1)S(1)}, bf16[8,288,128]{2,1,0:T(8,128)(2,1)S(1)}, u32[]{:S(2)}, u32[]{:S(2)}) collective-permute-start(bf16[8,288,128]{2,1,0:T(8,128)(2,1)S(1)} %get-tuple-element.172), channel_id=1, source_target_pairs={{0,16},{1,3},{2,18},{3,1},{4,20},{5,7},{6,22},{7,5},{8,24},{9,11},... | collective-permute-start | bytes 1769480 | tf_op jit(solution)/shard_map/ppermute | solution.py:812
  28.4 5.5 %collective-permute-start.1 = (bf16[16,288,128]{2,1,0:T(8,128)(2,1)S(1)}, bf16[16,288,128]{2,1,0:T(8,128)(2,1)S(1)}, u32[]{:S(2)}, u32[]{:S(2)}) collective-permute-start(bf16[16,288,128]{2,1,0:T(8,128)(2,1)S(1)} %get-tuple-element.170), channel_id=1, source_target_pairs={{0,1},{1,0},{2,3},{3,2},{4,5},{5,4},{6,7},{7,6},{8,9},{9,8},{10,11... | collective-permute-start | bytes 3538952 | tf_op jit(solution)/shard_map/ppermute | solution.py:812
  32.4 8.5 %collective-permute-start.4 = (bf16[4,288,128]{2,1,0:T(8,128)(2,1)S(1)}, bf16[4,288,128]{2,1,0:T(8,128)(2,1)S(1)}, u32[]{:S(2)}, u32[]{:S(2)}) collective-permute-start(bf16[4,288,128]{2,1,0:T(8,128)(2,1)S(1)} %get-tuple-element.180), channel_id=1, source_target_pairs={{0,2},{1,17},{2,0},{3,19},{4,6},{5,21},{6,4},{7,23},{8,10},{9,25},... | collective-permute-start | bytes 884744 | tf_op jit(solution)/shard_map/ppermute | solution.py:812
  34.4 11.1 %collective-permute-start.7 = (bf16[8,288,128]{2,1,0:T(8,128)(2,1)S(1)}, bf16[8,288,128]{2,1,0:T(8,128)(2,1)S(1)}, u32[]{:S(2)}, u32[]{:S(2)}) collective-permute-start(bf16[8,288,128]{2,1,0:T(8,128)(2,1)S(1)} %get-tuple-element.188), channel_id=1, source_target_pairs={{0,16},{1,3},{2,18},{3,1},{4,20},{5,7},{6,22},{7,5},{8,24},{9,11},... | collective-permute-start | bytes 1769480 | tf_op jit(solution)/shard_map/ppermute | solution.py:812
  39.3 3.3 %collective-permute-start.3 = (bf16[16,160,128]{2,1,0:T(8,128)(2,1)S(1)}, bf16[16,160,128]{2,1,0:T(8,128)(2,1)S(1)}, u32[]{:S(2)}, u32[]{:S(2)}) collective-permute-start(bf16[16,160,128]{2,1,0:T(8,128)(2,1)S(1)} %get-tuple-element.178), channel_id=1, source_target_pairs={{0,1},{1,0},{2,3},{3,2},{4,5},{5,4},{6,7},{7,6},{8,9},{9,8},{10,11... | collective-permute-start | bytes 1966088 | tf_op jit(solution)/shard_map/ppermute | solution.py:812
  41.0 4.6 %collective-permute-start.6 = (bf16[2,288,128]{2,1,0:T(8,128)(2,1)S(1)}, bf16[2,288,128]{2,1,0:T(8,128)(2,1)S(1)}, u32[]{:S(2)}, u32[]{:S(2)}) collective-permute-start(bf16[2,288,128]{2,1,0:T(8,128)(2,1)S(1)} %get-tuple-element.186), channel_id=1, source_target_pairs={{0,4},{1,5},{2,6},{3,7},{4,0},{5,1},{6,2},{7,3},{8,12},{9,13},{10,... | collective-permute-start | bytes 442376 | tf_op jit(solution)/shard_map/ppermute | solution.py:812
  42.8 6.5 %collective-permute-start.5 = (bf16[8,160,128]{2,1,0:T(8,128)(2,1)S(1)}, bf16[8,160,128]{2,1,0:T(8,128)(2,1)S(1)}, u32[]{:S(2)}, u32[]{:S(2)}) collective-permute-start(bf16[8,160,128]{2,1,0:T(8,128)(2,1)S(1)} %get-tuple-element.184), channel_id=1, source_target_pairs={{0,16},{1,3},{2,18},{3,1},{4,20},{5,7},{6,22},{7,5},{8,24},{9,11},... | collective-permute-start | bytes 983048 | tf_op jit(solution)/shard_map/ppermute | solution.py:812
  45.7 12.5 %collective-permute-start.9 = (bf16[2,288,128]{2,1,0:T(8,128)(2,1)S(1)}, bf16[2,288,128]{2,1,0:T(8,128)(2,1)S(1)}, u32[]{:S(2)}, u32[]{:S(2)}) collective-permute-start(bf16[2,288,128]{2,1,0:T(8,128)(2,1)S(1)} %get-tuple-element.195.refs_0_), channel_id=1, source_target_pairs={{0,8},{1,9},{2,10},{3,11},{4,12},{5,13},{6,14},{7,15},{8,0},{9,1},... | collective-permute-start | bytes 442376 | tf_op jit(solution)/shard_map/ppermute | solution.py:812
  48.5 6.4 %collective-permute-start.11 = (bf16[4,288,128]{2,1,0:T(8,128)(2,1)S(1)}, bf16[4,288,128]{2,1,0:T(8,128)(2,1)S(1)}, u32[]{:S(2)}, u32[]{:S(2)}) collective-permute-start(bf16[4,288,128]{2,1,0:T(8,128)(2,1)S(1)} %get-tuple-element.199), channel_id=1, source_target_pairs={{0,2},{1,17},{2,0},{3,19},{4,6},{5,21},{6,4},{7,23},{8,10},{9,25},... | collective-permute-start | bytes 884744 | tf_op jit(solution)/shard_map/ppermute | solution.py:812
  49.4 7.4 %collective-permute-start.10 = (bf16[4,160,128]{2,1,0:T(8,128)(2,1)S(1)}, bf16[4,160,128]{2,1,0:T(8,128)(2,1)S(1)}, u32[]{:S(2)}, u32[]{:S(2)}) collective-permute-start(bf16[4,160,128]{2,1,0:T(8,128)(2,1)S(1)} %get-tuple-element.197), channel_id=1, source_target_pairs={{0,2},{1,17},{2,0},{3,19},{4,6},{5,21},{6,4},{7,23},{8,10},{9,25},... | collective-permute-start | bytes 491528 | tf_op jit(solution)/shard_map/ppermute | solution.py:812
  55.1 4.2 %collective-permute-start.14 = (bf16[2,288,128]{2,1,0:T(8,128)(2,1)S(1)}, bf16[2,288,128]{2,1,0:T(8,128)(2,1)S(1)}, u32[]{:S(2)}, u32[]{:S(2)}) collective-permute-start(bf16[2,288,128]{2,1,0:T(8,128)(2,1)S(1)} %get-tuple-element.207), channel_id=1, source_target_pairs={{0,4},{1,5},{2,6},{3,7},{4,0},{5,1},{6,2},{7,3},{8,12},{9,13},{10,... | collective-permute-start | bytes 442376 | tf_op jit(solution)/shard_map/ppermute | solution.py:812
  55.8 9.7 %collective-permute-start.8 = (bf16[512,384]{1,0:T(8,128)(2,1)S(1)}, bf16[512,384]{1,0:T(8,128)(2,1)S(1)}, u32[]{:S(2)}, u32[]{:S(2)}) collective-permute-start(bf16[512,384]{1,0:T(8,128)(2,1)S(1)} %get-tuple-element.194), channel_id=1, source_target_pairs={{0,16},{16,0},{1,17},{17,1},{2,18},{18,2},{3,19},{19,3},{4,20},{20... | collective-permute-start | bytes 1179656 | tf_op jit(solution)/shard_map/ppermute | solution.py:995
  56.8 5.0 %collective-permute-start.13 = (bf16[2,160,128]{2,1,0:T(8,128)(2,1)S(1)}, bf16[2,160,128]{2,1,0:T(8,128)(2,1)S(1)}, u32[]{:S(2)}, u32[]{:S(2)}) collective-permute-start(bf16[2,160,128]{2,1,0:T(8,128)(2,1)S(1)} %get-tuple-element.205), channel_id=1, source_target_pairs={{0,4},{1,5},{2,6},{3,7},{4,0},{5,1},{6,2},{7,3},{8,12},{9,13},{10,... | collective-permute-start | bytes 245768 | tf_op jit(solution)/shard_map/ppermute | solution.py:812
  58.2 7.3 %collective-permute-start.12 = (bf16[2,288,128]{2,1,0:T(8,128)(2,1)S(1)}, bf16[2,288,128]{2,1,0:T(8,128)(2,1)S(1)}, u32[]{:S(2)}, u32[]{:S(2)}) collective-permute-start(bf16[2,288,128]{2,1,0:T(8,128)(2,1)S(1)} %get-tuple-element.203.refs_0_), channel_id=1, source_target_pairs={{0,4},{1,5},{2,6},{3,7},{4,0},{5,1},{6,2},{7,3},{8,12},{9,13},{10,... | collective-permute-start | bytes 442376 | tf_op jit(solution)/shard_map/ppermute | solution.py:812
  59.3 7.2 %collective-permute-start.17 = (bf16[2,288,128]{2,1,0:T(8,128)(2,1)S(1)}, bf16[2,288,128]{2,1,0:T(8,128)(2,1)S(1)}, u32[]{:S(2)}, u32[]{:S(2)}) collective-permute-start(bf16[2,288,128]{2,1,0:T(8,128)(2,1)S(1)} %get-tuple-element.216.refs_0_), channel_id=1, source_target_pairs={{0,8},{1,9},{2,10},{3,11},{4,12},{5,13},{6,14},{7,15},{8,0},{9,1},... | collective-permute-start | bytes 442376 | tf_op jit(solution)/shard_map/ppermute | solution.py:812
  61.9 15.8 %collective-permute-start.15 = (bf16[2,160,128]{2,1,0:T(8,128)(2,1)S(1)}, bf16[2,160,128]{2,1,0:T(8,128)(2,1)S(1)}, u32[]{:S(2)}, u32[]{:S(2)}) collective-permute-start(bf16[2,160,128]{2,1,0:T(8,128)(2,1)S(1)} %get-tuple-element.214.refs_0_), channel_id=1, source_target_pairs={{0,8},{1,9},{2,10},{3,11},{4,12},{5,13},{6,14},{7,15},{8,0},{9,1},... | collective-permute-start | bytes 245768 | tf_op jit(solution)/shard_map/ppermute | solution.py:812
  65.5 5.9 %collective-permute-start.16 = (bf16[4,288,128]{2,1,0:T(8,128)(2,1)S(1)}, bf16[4,288,128]{2,1,0:T(8,128)(2,1)S(1)}, u32[]{:S(2)}, u32[]{:S(2)}) collective-permute-start(bf16[4,288,128]{2,1,0:T(8,128)(2,1)S(1)} %get-tuple-element.215.refs_0_), channel_id=1, source_target_pairs={{0,2},{1,17},{2,0},{3,19},{4,6},{5,21},{6,4},{7,23},{8,10},{9,25},... | collective-permute-start | bytes 884744 | tf_op jit(solution)/shard_map/ppermute | solution.py:812
  66.6 12.2 %collective-permute-start.19 = (bf16[2,288,128]{2,1,0:T(8,128)(2,1)S(1)}, bf16[2,288,128]{2,1,0:T(8,128)(2,1)S(1)}, u32[]{:S(2)}, u32[]{:S(2)}) collective-permute-start(bf16[2,288,128]{2,1,0:T(8,128)(2,1)S(1)} %get-tuple-element.221.refs_0_), channel_id=1, source_target_pairs={{0,4},{1,5},{2,6},{3,7},{4,0},{5,1},{6,2},{7,3},{8,12},{9,13},{10,... | collective-permute-start | bytes 442376 | tf_op jit(solution)/shard_map/ppermute | solution.py:812
  71.5 23.5 %collective-permute-start.22 = (bf16[8,288,128]{2,1,0:T(8,128)(2,1)S(1)}, bf16[8,288,128]{2,1,0:T(8,128)(2,1)S(1)}, u32[]{:S(2)}, u32[]{:S(2)}) collective-permute-start(bf16[8,288,128]{2,1,0:T(8,128)(2,1)S(1)} %get-tuple-element.226.refs_0_), channel_id=1, source_target_pairs={{0,1},{1,0},{2,3},{3,2},{4,5},{5,4},{6,7},{7,6},{8,9},{9,8},{10,11... | collective-permute-start | bytes 1769480 | tf_op jit(solution)/shard_map/ppermute | solution.py:812
  76.4 10.9 %collective-permute-start.21 = (bf16[8,288,128]{2,1,0:T(8,128)(2,1)S(1)}, bf16[8,288,128]{2,1,0:T(8,128)(2,1)S(1)}, u32[]{:S(2)}, u32[]{:S(2)}) collective-permute-start(bf16[8,288,128]{2,1,0:T(8,128)(2,1)S(1)} %get-tuple-element.226.refs_0_), channel_id=1, source_target_pairs={{0,16},{1,3},{2,18},{3,1},{4,20},{5,7},{6,22},{7,5},{8,24},{9,11},... | collective-permute-start | bytes 1769480 | tf_op jit(solution)/shard_map/ppermute | solution.py:812
  77.6 3.7 %collective-permute-start.18 = (bf16[2,160,128]{2,1,0:T(8,128)(2,1)S(1)}, bf16[2,160,128]{2,1,0:T(8,128)(2,1)S(1)}, u32[]{:S(2)}, u32[]{:S(2)}) collective-permute-start(bf16[2,160,128]{2,1,0:T(8,128)(2,1)S(1)} %get-tuple-element.220.refs_0_), channel_id=1, source_target_pairs={{0,4},{1,5},{2,6},{3,7},{4,0},{5,1},{6,2},{7,3},{8,12},{9,13},{10,... | collective-permute-start | bytes 245768 | tf_op jit(solution)/shard_map/ppermute | solution.py:812
  78.8 11.8 %collective-permute-start.24 = (bf16[4,288,128]{2,1,0:T(8,128)(2,1)S(1)}, bf16[4,288,128]{2,1,0:T(8,128)(2,1)S(1)}, u32[]{:S(2)}, u32[]{:S(2)}) collective-permute-start(bf16[4,288,128]{2,1,0:T(8,128)(2,1)S(1)} %get-tuple-element.230.refs_0_), channel_id=1, source_target_pairs={{0,2},{1,17},{2,0},{3,19},{4,6},{5,21},{6,4},{7,23},{8,10},{9,25},... | collective-permute-start | bytes 884744 | tf_op jit(solution)/shard_map/ppermute | solution.py:812
  81.3 9.3 %collective-permute-start.20 = (bf16[4,160,128]{2,1,0:T(8,128)(2,1)S(1)}, bf16[4,160,128]{2,1,0:T(8,128)(2,1)S(1)}, u32[]{:S(2)}, u32[]{:S(2)}) collective-permute-start(bf16[4,160,128]{2,1,0:T(8,128)(2,1)S(1)} %get-tuple-element.224.refs_0_), channel_id=1, source_target_pairs={{0,2},{1,17},{2,0},{3,19},{4,6},{5,21},{6,4},{7,23},{8,10},{9,25},... | collective-permute-start | bytes 491528 | tf_op jit(solution)/shard_map/ppermute | solution.py:812
  87.3 8.2 %collective-permute-start.23 = (bf16[8,288,128]{2,1,0:T(8,128)(2,1)S(1)}, bf16[8,288,128]{2,1,0:T(8,128)(2,1)S(1)}, u32[]{:S(2)}, u32[]{:S(2)}) collective-permute-start(bf16[8,288,128]{2,1,0:T(8,128)(2,1)S(1)} %get-tuple-element.229.refs_1_), channel_id=1, source_target_pairs={{0,1},{1,0},{2,3},{3,2},{4,5},{5,4},{6,7},{7,6},{8,9},{9,8},{10,11... | collective-permute-start | bytes 1769480 | tf_op jit(solution)/shard_map/ppermute | solution.py:812
  90.7 9.5 %collective-permute-start.25 = (bf16[8,288,128]{2,1,0:T(8,128)(2,1)S(1)}, bf16[8,288,128]{2,1,0:T(8,128)(2,1)S(1)}, u32[]{:S(2)}, u32[]{:S(2)}) collective-permute-start(bf16[8,288,128]{2,1,0:T(8,128)(2,1)S(1)} %get-tuple-element.234.refs_0_), channel_id=1, source_target_pairs={{0,16},{1,3},{2,18},{3,1},{4,20},{5,7},{6,22},{7,5},{8,24},{9,11},... | collective-permute-start | bytes 1769480 | tf_op jit(solution)/shard_map/ppermute | solution.py:812
  93.3 14.0 %collective-permute-start.27 = (bf16[8,160,128]{2,1,0:T(8,128)(2,1)S(1)}, bf16[8,160,128]{2,1,0:T(8,128)(2,1)S(1)}, u32[]{:S(2)}, u32[]{:S(2)}) collective-permute-start(bf16[8,160,128]{2,1,0:T(8,128)(2,1)S(1)} %get-tuple-element.228.refs_0_), channel_id=1, source_target_pairs={{0,1},{1,0},{2,3},{3,2},{4,5},{5,4},{6,7},{7,6},{8,9},{9,8},{10,11... | collective-permute-start | bytes 983048 | tf_op jit(solution)/shard_map/ppermute | solution.py:812
  93.7 10.0 %collective-permute-start.26 = (bf16[8,160,128]{2,1,0:T(8,128)(2,1)S(1)}, bf16[8,160,128]{2,1,0:T(8,128)(2,1)S(1)}, u32[]{:S(2)}, u32[]{:S(2)}) collective-permute-start(bf16[8,160,128]{2,1,0:T(8,128)(2,1)S(1)} %get-tuple-element.228.refs_0_), channel_id=1, source_target_pairs={{0,16},{1,3},{2,18},{3,1},{4,20},{5,7},{6,22},{7,5},{8,24},{9,11},... | collective-permute-start | bytes 983048 | tf_op jit(solution)/shard_map/ppermute | solution.py:812
  94.9 9.5 %collective-permute-start.29 = (bf16[8,288,128]{2,1,0:T(8,128)(2,1)S(1)}, bf16[8,288,128]{2,1,0:T(8,128)(2,1)S(1)}, u32[]{:S(2)}, u32[]{:S(2)}) collective-permute-start(bf16[8,288,128]{2,1,0:T(8,128)(2,1)S(1)} %get-tuple-element.234.refs_0_), channel_id=1, source_target_pairs={{0,1},{1,0},{2,3},{3,2},{4,5},{5,4},{6,7},{7,6},{8,9},{9,8},{10,11... | collective-permute-start | bytes 1769480 | tf_op jit(solution)/shard_map/ppermute | solution.py:812
  100.2 4.2 %collective-permute-start.30 = (bf16[8,288,128]{2,1,0:T(8,128)(2,1)S(1)}, bf16[8,288,128]{2,1,0:T(8,128)(2,1)S(1)}, u32[]{:S(2)}, u32[]{:S(2)}) collective-permute-start(bf16[8,288,128]{2,1,0:T(8,128)(2,1)S(1)} %get-tuple-element.237.refs_1_), channel_id=1, source_target_pairs={{0,1},{1,0},{2,3},{3,2},{4,5},{5,4},{6,7},{7,6},{8,9},{9,8},{10,11... | collective-permute-start | bytes 1769480 | tf_op jit(solution)/shard_map/ppermute | solution.py:812
  103.7 3.6 %collective-permute-start.28 = (bf16[8,160,128]{2,1,0:T(8,128)(2,1)S(1)}, bf16[8,160,128]{2,1,0:T(8,128)(2,1)S(1)}, u32[]{:S(2)}, u32[]{:S(2)}) collective-permute-start(bf16[8,160,128]{2,1,0:T(8,128)(2,1)S(1)} %get-tuple-element.236.refs_1_), channel_id=1, source_target_pairs={{0,1},{1,0},{2,3},{3,2},{4,5},{5,4},{6,7},{7,6},{8,9},{9,8},{10,11... | collective-permute-start | bytes 983048 | tf_op jit(solution)/shard_map/ppermute | solution.py:812
  (17 other events, 86.3 us)

commit v2 on v1

--- a/solution.py
+++ b/solution.py
@@ -14,7 +14,8 @@
 EPSILON = 1e-05
 BLOCKED = -1000000000.0
 LANES = 128
-BLOCK = 256
+BLOCK = 512
+WIDE = 768
 SQUARE = 4
 ROW = 4
 PIECE = 144
@@ -110,23 +111,6 @@
     return jnp.sum(values, axis=0, keepdims=True)
 
 
-def extent(numbers, image, local, side):
-    micros, images = numbers.shape[1] - FIXED, numbers.shape[0] // 2
-    first = numbers[0, 0] * (micros // 2) if local else 0
-    return numbers[image % images * 2 + side, FIXED + first + image // images]
-
-
-def valid_column(numbers, image):
-    slot = lax.broadcasted_iota(jnp.int32, (SLOTS, 1), 0)
-    height, width = (extent(numbers, image, True, side) for side in range(2))
-    inside = (slot // SIDE < height) & (slot % SIDE < width)
-    return inside.astype(F32)
-
-
-def valid_rows(numbers, images):
-    return jnp.concatenate([valid_column(numbers, image) for image in range(images)], axis=0)
-
-
 def column_shifts(row, first_column, last_column):
     before = jnp.where(first_column, 0.0, pltpu.roll(row, 1, 0))
     after = jnp.where(last_column, 0.0, pltpu.roll(row, SIDE - 1, 0))
@@ -134,9 +118,9 @@
 
 
 def conv_ahead_kernel(
-    extents, tokens, enlarge_from, enlarge_bias_from, taps_from, taps_bias_from, contract_from,
+    extents_from, tokens, enlarge_from, enlarge_bias_from, taps_from, taps_bias_from, contract_from,
     gain_from, shift_from, sent, expanded, slope, active, projected, inside, filled,
-    grid_cells, entering, enlarge, enlarge_bias, taps, taps_bias, contract, gain, shift, arrivals,
+    grid_cells, entering, enlarge, enlarge_bias, taps, taps_bias, contract, gain, shift, extents, arrivals,
 ):
     rows, width = sent.shape
     images = rows // SLOTS
@@ -144,7 +128,12 @@
     share = entering.shape[0]
     starts = range(0, channels, BLOCK)
     section = Here().section
-    copies = [(tokens.at[pl.ds(section * share, share)], entering)]
+    copies = [(extents_from, extents)]
+    copies += [
+        (tokens.at[section * share + number // 2, :, half], entering.at[number // 2, :, half])
+        for number in range(2 * share)
+        for half in (pl.ds(number % 2 * (SLOTS // 2), SLOTS // 2),)
+    ]
     copies += [(enlarge_from.at[:, pl.ds(0, BLOCK)], enlarge.at[:, pl.ds(0, BLOCK)])]
     copies += [
         (enlarge_bias_from, enlarge_bias), (taps_from, taps), (taps_bias_from, taps_bias),
@@ -162,6 +151,7 @@
     ]
     for copy in copies:
         copy.start()
+    copies[0].wait()
     micros, local = extents.shape[2], extents.shape[0]
     for image in range(micros * local):
         count = extents[image % local, 0, image // local] * extents[image % local, 1, image // local]
@@ -173,12 +163,12 @@
         )
         held = (slot // SIDE < height) & (slot % SIDE < across_it)
         inside[image * SLOTS : (image + 1) * SLOTS, :] = held.astype(F32)
-    for copy in copies[:early]:
+    for copy in copies[1:early]:
         copy.wait()
     later = copies[early:]
     local_in = entering[...].reshape(rows, width)
     valid = inside[...]
-    column = lax.broadcasted_iota(jnp.int32, (SIDE, BLOCK), 0)
+    column = lax.broadcasted_iota(jnp.int32, (SIDE, LANES), 0)
     first_column, last_column = column == 0, column == SIDE - 1
     total = jnp.zeros((rows, width), F32)
 
@@ -196,29 +186,37 @@
         number = start // BLOCK
         if start + BLOCK < channels:
             cells_of(start + BLOCK)
-        kernel = [taps[tap : tap + 1, part] for tap in range(9)]
-        bias = taps_bias[part].reshape(1, -1)
-        for image in range(images):
-            base = image * SLOTS
-            above = here = None
-            for line in range(SIDE + 1):
-                if line < SIDE:
-                    row = grid_cells[number % 2, base + line * SIDE : base + (line + 1) * SIDE, :]
-                    before, after = column_shifts(row, first_column, last_column)
-                    sums = [
-                        before * kernel[3 * a] + row * kernel[3 * a + 1] + after * kernel[3 * a + 2]
-                        for a in range(3)
-                    ]
-                if line > 0:
-                    convolved = above + sums[2] if line < SIDE else above
-                    gate = jax.nn.sigmoid(convolved)
-                    lit = convolved * gate
-                    place = slice(base + (line - 1) * SIDE, base + line * SIDE)
-                    active[place, part] = lit.astype(BF16)
-                    slope[place, part] = (gate + lit * (1.0 - gate)).astype(BF16)
-                if line < SIDE:
-                    above = (here if line > 0 else bias) + sums[1]
-                    here = bias + sums[0]
+        for left in range(0, BLOCK, LANES):
+            inner = slice(start + left, start + left + LANES)
+            kernel = [taps[tap : tap + 1, inner] for tap in range(9)]
+            bias = taps_bias[inner].reshape(1, -1)
+            for image in range(images):
+                base = image * SLOTS
+                above = here = None
+                for line in range(SIDE + 1):
+                    if line < SIDE:
+                        row = grid_cells[
+                            number % 2,
+                            base + line * SIDE : base + (line + 1) * SIDE,
+                            left : left + LANES,
+                        ]
+                        before, after = column_shifts(row, first_column, last_column)
+                        sums = [
+                            before * kernel[3 * a]
+                            + row * kernel[3 * a + 1]
+                            + after * kernel[3 * a + 2]
+                            for a in range(3)
+                        ]
+                    if line > 0:
+                        convolved = above + sums[2] if line < SIDE else above
+                        gate = jax.nn.sigmoid(convolved)
+                        lit = convolved * gate
+                        place = slice(base + (line - 1) * SIDE, base + line * SIDE)
+                        active[place, inner] = lit.astype(BF16)
+                        slope[place, inner] = (gate + lit * (1.0 - gate)).astype(BF16)
+                    if line < SIDE:
+                        above = (here if line > 0 else bias) + sums[1]
+                        here = bias + sums[0]
         later[2 * number].wait()
         total = total + dot_nn(active[:, part], contract[part, :])
     projected[...] = total
@@ -307,18 +305,9 @@
     return step % 2 * 2 + (here.row % 2 ^ step // 2)
 
 
-def hand_out(pieces, keep, send):
-    here = Here()
-    for target, core in ((keep, here.core), (send, 1 - here.core)):
-        for step in range(SQUARE):
-            square = square_at(here, core, step)
-            for along in range(ROW):
-                target[step * ROW + along] = pieces[core, square, row_at(here, along)]
-
-
 def mlp_kernel(
-    inside, middle, sensitivity, gain, shift, enlarge, enlarge_bias, contract, contract_bias,
-    output, grad_middle, keep, send, small, wide_small, blocks,
+    inside, middle, sensitivity, gain, shift, enlarge, enlarge_bias, contract,
+    lit, grad_middle, blocks, send, small, wide_small,
 ):
     rows, width = middle.shape
     images = rows // SLOTS
@@ -329,38 +318,37 @@
     hidden = (scaled * across(gain) + across(shift)).astype(BF16)
     grad_out = own_share(sensitivity, rows).astype(F32) * valid
     out_low = grad_out.astype(BF16)
-    total = jnp.zeros((rows, width), F32)
     grad_hidden = jnp.zeros((rows, width), F32)
+    out_turned, hidden_turned = out_low.T, hidden.T
 
     def products(start):
-        part = slice(start, start + BLOCK)
+        part = slice(start, start + WIDE)
         return dot_nn(hidden, enlarge[:, part]), dot_nt(out_low, contract[part, :])
 
     ahead = products(0)
-    for start in range(0, hidden_width, BLOCK):
-        part = slice(start, start + BLOCK)
+    for start in range(0, hidden_width, WIDE):
+        part = slice(start, start + WIDE)
         widened, grad_wide = ahead
-        if start + BLOCK < hidden_width:
-            ahead = products(start + BLOCK)
+        if start + WIDE < hidden_width:
+            ahead = products(start + WIDE)
         widened = widened + enlarge_bias[part].reshape(1, -1)
         normal_cdf = 0.5 * (1.0 + lax.erf(widened * (1.0 / math.sqrt(2.0))))
         normal_pdf = jnp.exp(-0.5 * widened * widened) * (1.0 / math.sqrt(2.0 * math.pi))
         activated = (widened * normal_cdf).astype(BF16)
+        lit[:, part] = activated
         grad_wide = grad_wide * (normal_cdf + widened * normal_pdf)
         wide_small[:, part] = total_rows(grad_wide)
         wide_low = grad_wide.astype(BF16)
-        total = total + dot_nn(activated, contract[part, :])
-        place_tall(blocks, dot_tn(activated, out_low).astype(BF16), start, 0)
-        place_wide(blocks, dot_tn(hidden, wide_low).astype(BF16), start // LANES, PIECE)
+        place_tall(blocks, dot_nn(out_turned, activated).astype(BF16).T, start, 0)
+        place_wide(blocks, dot_nn(hidden_turned, wide_low).astype(BF16), start // LANES, PIECE)
         grad_hidden = grad_hidden + dot_nt(wide_low, enlarge[:, part])
-    output[...] = ((center + total + across(contract_bias)) * valid).astype(BF16)
     gradient = grad_out + norm_reverse(grad_hidden, scaled, inverse, across(gain))
     grad_middle[...] = gradient
     small[0:1, :] = total_rows(grad_out)
     small[1:2, :] = total_rows(grad_hidden * scaled)
     small[2:3, :] = total_rows(grad_hidden)
     small[3:4, :] = total_rows(gradient)
-    hand_out(blocks, keep, send)
+    send[...] = blocks[1 - Here().core]
 
 
 def heads_back_kernel(
@@ -400,12 +388,22 @@
         scores_low = (lifted - soft * jnp.sum(lifted, axis=0, keepdims=True)).astype(BF16)
         queries = qkv[place, at : at + pair]
         keys = qkv[place, width + at : width + at + pair]
+        if number % 2 == 0:
+            keys_turned = keys.T
+        mine = slice(number % 2 * head, (number % 2 + 1) * head)
         parts.append(
-            (dot_tn(scores_low, keys) * factor, dot_nn(scores_low, queries) * factor, grad_values)
+            (
+                dot_nn(keys_turned[mine], scores_low) * factor,
+                dot_nn(scores_low, queries) * factor,
+                grad_values,
+            )
         )
         if number % 2:
             for which in range(3):
-                merged = jnp.where(lane < head, parts[0][which], parts[1][which])
+                if which:
+                    merged = jnp.where(lane < head, parts[0][which], parts[1][which])
+                else:
+                    merged = jnp.concatenate([parts[0][0], parts[1][0]], axis=0).T
                 grad_qkv[place, which * width + at : which * width + at + pair] = merged.astype(
                     BF16
                 )
@@ -414,19 +412,15 @@
 
 def sent_back_kernel(
     sent, grad_middle, grad_qkv, context, projected, active, gain, shift, mixing_in,
-    conv_gain, grad_sent, proj_low, keep, send, small, blocks,
+    conv_gain, grad_sent, proj_low, blocks, send, small,
 ):
     rows, width = sent.shape
     gradient = grad_middle[...]
     entering = sent[...].astype(F32)
     scaled, inverse = norm_parts(entering)
     normed = (scaled * across(gain) + across(shift)).astype(BF16)
-    lifted = jnp.zeros((rows, width), F32)
-    for which in range(3):
-        part = slice(which * width, (which + 1) * width)
-        piece = grad_qkv[:, part]
-        place_wide(blocks, dot_tn(normed, piece).astype(BF16), which * width // LANES, 0)
-        lifted = lifted + dot_nt(piece, mixing_in[:, part])
+    place_wide(blocks, dot_tn(normed, grad_qkv[...]).astype(BF16), 0, 0)
+    lifted = dot_nt(grad_qkv[...], mixing_in[...])
     mixing = dot_tn(context[...], gradient.astype(BF16)).astype(BF16)
     place_wide(blocks, mixing, 3 * width // LANES, 0)
     grad_low = (gradient + norm_reverse(lifted, scaled, inverse, across(gain))).astype(BF16)
@@ -439,36 +433,29 @@
     proj_low[...] = low
     small[2:3, :] = total_rows(incoming * scaled)
     small[3:4, :] = total_rows(incoming)
-    for start in range(0, active.shape[1], BLOCK):
-        part = slice(start, start + BLOCK)
-        place_tall(blocks, dot_tn(active[:, part], low).astype(BF16), start, PIECE)
-    hand_out(blocks, keep, send)
+    turned = low.T
+    for start in range(0, active.shape[1], WIDE):
+        grad = dot_nn(turned, active[:, start : start + WIDE]).astype(BF16).T
+        place_tall(blocks, grad, start, PIECE)
+    send[...] = blocks[1 - Here().core]
 
 
 def conv_part(
-    inside, local_in, proj_low, expanded, slope, enlarge, taps, contract, wide_small, grad_cells,
-    blocks, total, first, last, first_row=0,
+    inside, local_in, proj_low, expanded, slope, taps, contract, wide_small, grad_cells, blocks,
+    grad_low, first, last, first_row=0,
 ):
     rows = local_in.shape[0]
     images = rows // SLOTS
     valid = inside[...]
     column = lax.broadcasted_iota(jnp.int32, (SIDE, LANES), 0)
     first_column, last_column = column == 0, column == SIDE - 1
-
-    def cells_of(start):
-        part = slice(start, start + BLOCK)
+    for start in range(first, last, WIDE):
+        part = slice(start, start + WIDE)
         grad_conv = dot_nt(proj_low, contract[part, :]) * slope[:, part].astype(F32)
         wide_small[9:10, part] = total_rows(grad_conv)
-        grad_cells[start // BLOCK % 2] = grad_conv
-
-    cells_of(first)
-    for start in range(first, last, BLOCK):
-        part = slice(start, start + BLOCK)
-        number = start // BLOCK
-        if start + BLOCK < last:
-            cells_of(start + BLOCK)
+        grad_cells[0] = grad_conv
         pieces = []
-        for lanes in range(0, BLOCK, LANES):
+        for lanes in range(0, WIDE, LANES):
             chans = slice(start + lanes, start + lanes + LANES)
             kernel = [taps[tap : tap + 1, chans] for tap in range(9)]
             sums = [jnp.zeros((SIDE, LANES), F32) for _ in range(9)]
@@ -480,7 +467,7 @@
                     for ahead in (line, line + 1):
                         if ahead < SIDE and ahead not in shifted:
                             row = grad_cells[
-                                number % 2,
+                                0,
                                 base + ahead * SIDE : base + (ahead + 1) * SIDE,
                                 lanes : lanes + LANES,
                             ]
@@ -505,19 +492,16 @@
         place_wide(
             blocks, dot_tn(local_in, expanded_low).astype(BF16), start // LANES, 0, first_row
         )
-        total = total + dot_nt(expanded_low, enlarge[:, part])
-    return total
+        grad_low[:, start - first : start - first + WIDE] = expanded_low
 
 
 def conv_back_kernel(
-    inside, tokens, grad_sent, proj_low, expanded, slope, enlarge, taps, contract,
-    total, early, early_wide, grad_cells,
+    inside, tokens, proj_low, expanded, slope, taps, contract,
+    grad_low, early, early_wide, grad_cells,
 ):
-    rows, width = grad_sent.shape
-    total[...] = conv_part(
-        inside, own_share(tokens, rows), proj_low[...], expanded, slope, enlarge, taps,
-        contract, early_wide, grad_cells, early, grad_sent[...].astype(F32), 0,
-        enlarge.shape[1] // 2,
+    conv_part(
+        inside, own_share(tokens, proj_low.shape[0]), proj_low[...], expanded, slope, taps,
+        contract, early_wide, grad_cells, early, grad_low, 0, expanded.shape[1] // 2,
     )
 
 
@@ -533,18 +517,17 @@
 
 
 def conv_end_kernel(
-    inside, tokens, total, proj_low, expanded, slope, enlarge, taps, contract, early, early_wide,
-    mlp_small, sent_small, mlp_wide, grad_in, keep, send, pieces, conv_wide, grad_cells, short,
+    inside, tokens, proj_low, expanded, slope, taps, contract, early, early_wide,
+    mlp_small, sent_small, mlp_wide, grad_low, pieces, send, conv_wide, grad_cells, short,
 ):
-    rows, width = total.shape
-    channels = enlarge.shape[1]
+    channels = expanded.shape[1]
     half = channels // 2
     conv_wide[:, 0:half] = early_wide[:, 0:half]
     pieces[:, :, 0 : ROW // 2, 0:PIECE, :] = early[...]
-    grad_in[...] = conv_part(
-        inside, own_share(tokens, rows), proj_low[...], expanded, slope, enlarge, taps,
-        contract, conv_wide, grad_cells, pieces, total[...], half, channels,
-    ).astype(BF16)
+    conv_part(
+        inside, own_share(tokens, proj_low.shape[0]), proj_low[...], expanded, slope, taps,
+        contract, conv_wide, grad_cells, pieces, grad_low, half, channels,
+    )
     short[...] = jnp.zeros_like(short)
     places = small_rows((mlp_small, sent_small), (mlp_wide, conv_wide))
     for number, (source, row, at) in enumerate(places):
@@ -556,7 +539,7 @@
         pair = jnp.concatenate([high, value - high], axis=0).astype(BF16)
         core, square, row = piece // (SQUARE * ROW), piece // ROW % SQUARE, piece % ROW
         pieces[core, square, row, PIECE : PIECE + 16, :] = pair
-    hand_out(pieces, keep, send)
+    send[...] = pieces[1 - Here().core]
 
 
 def summed(parts, short):
@@ -580,18 +563,27 @@
         at += out.shape[0]
 
 
+def first_kernel(short, pieces, arrived, kept, send):
+    here = Here()
+    half = kept.shape[0]
+    for step in range(2 * half):
+        square, row = square_at(here, here.core, step // ROW), row_at(here, step % ROW)
+        parts = (pieces[here.core, square, row], arrived[square, row])
+        (kept, send)[step // half][step % half] = summed(parts, short)
+
+
 def join_kernel(short, own, arrived, out):
     half = own.shape[0]
     out[0:half] = own[...]
     out[half:] = arrived[...]
 
 
-def pieces_of(parts):
+def pieces_of(parts, begin=0):
     half = len(parts) // 2
     here = Here()
     for side in range(2):
         core = here.core if side == 0 else 1 - here.core
-        step = 0
+        step = begin
         for part in parts[side * half : (side + 1) * half]:
             for inside in range(part.shape[0]):
                 square = square_at(here, core, step // ROW)
@@ -689,10 +681,18 @@
     leaving.wait()
 
 
-def give_kernel(output, grad_in, own, give):
+def give_kernel(
+    inside, middle, lit, contract, contract_bias, grad_sent, early_low, late_low, enlarge,
+    own, give,
+):
+    half = early_low.shape[1]
+    total = middle[...] + dot_nn(lit[...], contract[...]) + across(contract_bias)
+    output = (total * inside[...]).astype(BF16)
+    gradient = grad_sent[...].astype(F32) + dot_nt(early_low[...], enlarge[:, 0:half])
+    gradient = (gradient + dot_nt(late_low[...], enlarge[:, half:])).astype(BF16)
     first = Here().section == 0
-    own[...] = jnp.where(first, grad_in[...], output[...])
-    give[...] = jnp.where(first, output[...], grad_in[...])
+    own[...] = jnp.where(first, gradient, output)
+    give[...] = jnp.where(first, output, gradient)
 
 
 def ends_kernel(filled, own, arrived, ends, means, semaphores):
@@ -710,13 +710,18 @@
                 )
             )
             copies[-1].start()
+    micro = lax.broadcasted_iota(jnp.int32, (1, ends.shape[0]), 1)
+    rows = [jnp.zeros((1, ends.shape[0]), F32) for _ in range(local)]
     for source, section in ((own, first), (arrived, 1 - first)):
         for number in range(share * local):
             value = source[number * slots : (number + 1) * slots, :].astype(F32)
             square = jnp.sum(value * value, axis=0, keepdims=True)
             image = (section * share + number // local) * local + number % local
             mean = jnp.sum(square, axis=1, keepdims=True) / filled[pl.ds(image, 1), 0:1]
-            means[image, :, :] = jnp.broadcast_to(jnp.sqrt(mean), (1, LANES))
+            held = micro == section * share + number // local
+            rows[number % local] = jnp.where(held, jnp.sqrt(mean), rows[number % local])
+    for image in range(local):
+        means[0, image : image + 1, :] = rows[image]
     for copy in copies:
         copy.wait()
 
@@ -726,7 +731,18 @@
 REMOTE = pl.BlockSpec(memory_space=pltpu.HBM)
 SCALARS = pl.BlockSpec(memory_space=pltpu.SMEM)
 COST = 30
-COSTS = {'conv_first': 0, 'conv_second': 30, 'conv_far': 0, 'conv_join_square': 0, 'give': 0, 'mlp_cores': 30, 'conv_cores': 30, 'conv_all': 0, 'inner_cores': 30, 'conv_total': 0, 'inner_join_square': 30, 'mlp_end': 0, 'mlp_far': 0}
+ORDER = (
+    "mlp.near", "conv.first", "inner.second", "mlp.far", "conv.second", "swap_ends", "inner.near",
+    "conv.near", "mlp.total", "inner.far", "conv.far", "mlp.join_row", "put_ends", "inner.total",
+    "conv.total", "inner.join_row", "mlp.join_square", "conv.join_row", "inner.join_square",
+    "mlp.join_cores", "conv.join_square", "put_mlp", "inner.join_cores", "conv.join_cores",
+    "put_inner", "put_conv",
+)
+COSTS = {
+    "conv_first": 0, "conv_second": 30, "conv_far": 0, "conv_join_square": 30, "give": 30,
+    "mlp_cores": 0, "conv_cores": 30, "conv_all": 0, "inner_cores": 30, "conv_total": 30,
+    "inner_join_square": 0, "mlp_end": 0, "mlp_far": 0, "conv_near": 0,
+}
 BOTH = ("section", "dp")
 
 
@@ -738,7 +754,7 @@
     def __init__(self):
         self.last = None
 
-    def __call__(self, kernel, name, ins, outs, scratch=(), mb=8, us=0, smem=(), hbm=(), hbm_outs=()):
+    def __call__(self, kernel, name, ins, outs, scratch=(), mb=8, us=0, smem=(), hbm=(), hbm_outs=(), aliases={}):
         count = len(ins)
         after = () if self.last is None else (self.last,)
 
@@ -767,6 +783,7 @@
             out_specs=[WHOLE]
             + [REMOTE if place in hbm_outs else WHOLE for place in range(len(outs))],
             scratch_shapes=list(scratch),
+            input_output_aliases={place: out + 1 for place, out in aliases.items()},
             cost_estimate=pl.CostEstimate(
                 flops=1 + int(COSTS.get(name, us) * 1e9), bytes_accessed=1, transcendentals=0
             ),
@@ -815,7 +832,7 @@
 class Group:
     def __init__(self, name, calls, keep, send, short=0, cost=COST):
         self.name, self.calls, self.short, self.cost = name, calls, short, cost
-        self.rows = keep.shape[1]
+        self.rows = keep.shape[3]
         self.parts = [keep, swapped(send, 1)]
 
     def call(self, kernel, what, ins, outs):
@@ -834,7 +851,9 @@
         self.parts = [keep, swapped(send, what)]
 
     def first(self):
-        self.halve("first")
+        half = SQUARE * ROW // 2
+        keep, send = self.call(first_kernel, "first", self.parts, [half] * 2)
+        self.parts = [keep, swapped(send, "first")]
 
     def second(self):
         self.halve("second")
@@ -873,6 +892,12 @@
     def join_cores(self):
         far_half = self.calls.fence(self.parts[1], f"{self.name}_cores")
         self.blocks = [self.parts[0], far_half, self.near_half, swapped(far_half, 1)]
+
+    def early(self):
+        return [self.parts[0], self.near_half]
+
+    def late(self):
+        return self.blocks[1::2]
 
     def join_all(self):
         own = self.join("join_row")
@@ -921,30 +946,30 @@
         + [pltpu.VMEM(value.shape, value.dtype) for value in
            (pointwise_enlarge, enlarge_bias, channelwise_kernel, channelwise_conv_bias,
             pointwise_contract, convblock_scale, convblock_offset)]
-        + [pltpu.SemaphoreType.DMA((6 + 2 * channels // BLOCK,))],
-        mb=20, smem=(0,), hbm=range(1, 9),
+        + [pltpu.SMEM(extents.shape, jnp.int32), pltpu.SemaphoreType.DMA((6 + 2 * share + 2 * channels // BLOCK,))],
+        mb=14, hbm=range(9),
     )
     qkv, weights, context, middle = call(
         attend_ahead_kernel, "attend_ahead",
         (inside, sent, attend_scale, attend_offset, query_key_proj, heads_output_proj,
          heads_output_bias),
         [shape((rows, 3 * width), BF16), shape((images * HEADS, slots, slots), BF16),
-         shape((rows, width), BF16), shape((rows, width), F32)], mb=16,
-    )
-    halves = [shape((SQUARE * ROW, 2 * PIECE, LANES), BF16)] * 2
-    whole = [pltpu.VMEM((2, SQUARE, ROW, 2 * PIECE, LANES), BF16)]
-    output, grad_middle, keep, send, mlp_small, mlp_wide = call(
+         shape((rows, width), BF16), shape((rows, width), F32)], mb=10,
+    )
+    halves = [shape((cores, SQUARE, ROW, 2 * PIECE, LANES), BF16) for cores in (2, 1)]
+    halves[1] = shape(halves[1].shape[1:], BF16)
+    lit, grad_middle, keep, send, mlp_small, mlp_wide = call(
         mlp_kernel, "mlp",
         (inside, middle, output_sensitivity, feedforward_scale, feedforward_offset, feedforward_enlarge,
-         feedforward_enlarge_bias, feedforward_contract, contract_bias),
-        [shape((rows, width), BF16), shape((rows, width), F32)] + halves
+         feedforward_enlarge_bias, feedforward_contract),
+        [shape((rows, channels), BF16), shape((rows, width), F32)] + halves
         + [shape((8, width), F32), shape((1, channels), F32)],
-        whole, mb=24,
+        mb=18,
     )
     mlp = Group("mlp", call, keep, send)
     (grad_qkv,) = call(
         heads_back_kernel, "heads_back", (grad_middle, qkv, weights, heads_output_proj),
-        [shape((rows, 3 * width), BF16)], mb=16,
+        [shape((rows, 3 * width), BF16)], mb=10,
     )
     mlp.first()
     grad_sent, proj_low, keep, send, sent_small = call(
@@ -953,28 +978,29 @@
          query_key_proj, convblock_scale),
         [shape((rows, width), BF16), shape((rows, width), BF16)] + halves
         + [shape((8, width), F32)],
-        whole, mb=24,
+        mb=14,
     )
     inner = Group("inner", call, keep, send)
     early_pieces = shape((2, SQUARE, ROW // 2, PIECE, LANES), BF16)
-    total, early, early_wide = call(
+    early_low, early, early_wide = call(
         conv_back_kernel, "conv_back",
-        (inside, entering_tokens, grad_sent, proj_low, expanded, slope, pointwise_enlarge,
-         channelwise_kernel, pointwise_contract),
-        [shape((rows, width), F32), early_pieces, shape((16, channels), F32)],
-        [pltpu.VMEM((2, rows, BLOCK), F32)], mb=20,
+        (inside, entering_tokens, proj_low, expanded, slope, channelwise_kernel,
+         pointwise_contract),
+        [shape((rows, channels // 2), BF16), early_pieces, shape((16, channels), F32)],
+        [pltpu.VMEM((1, rows, WIDE), F32)], mb=12,
     )
     mlp.second()
     inner.first()
-    halves = [shape((SQUARE * ROW, PIECE + 16, LANES), BF16)] * 2
-    grad_in, keep, send = call(
+    halves = [shape((cores, SQUARE, ROW, PIECE + 16, LANES), BF16) for cores in (2, 1)]
+    halves[1] = shape(halves[1].shape[1:], BF16)
+    late_low, keep, send = call(
         conv_end_kernel, "conv_end",
-        (inside, entering_tokens, total, proj_low, expanded, slope, pointwise_enlarge, channelwise_kernel,
+        (inside, entering_tokens, proj_low, expanded, slope, channelwise_kernel,
          pointwise_contract, early, early_wide, mlp_small, sent_small, mlp_wide),
-        [shape((rows, width), BF16)] + halves,
-        [pltpu.VMEM((2, SQUARE, ROW, PIECE + 16, LANES), BF16), pltpu.VMEM((16, channels), F32),
-         pltpu.VMEM((2, rows, BLOCK), F32), pltpu.VMEM((2 * SQUARE * ROW, 8, LANES), F32)],
-        mb=20,
+        [shape((rows, channels // 2), BF16)] + halves,
+        [pltpu.VMEM((16, channels), F32), pltpu.VMEM((1, rows, WIDE), F32),
+         pltpu.VMEM((2 * SQUARE * ROW, 8, LANES), F32)],
+        mb=14,
     )
     conv = Group("conv", call, keep, send, 16)
     line, wide_line = shape((width,), F32), shape((channels,), F32)
@@ -984,52 +1010,60 @@
     def leaving(count):
         return [pltpu.VMEM((count, HEIGHT, ACROSS * LANES), F32), pltpu.SemaphoreType.DMA((count,))]
 
-    mlp.near()
-    conv.first()
-    inner.second()
-    mlp.far()
-    conv.second()
-    own, give = call(
-        give_kernel, "give", (output, grad_in), [shape((rows, width), BF16)] * 2, us=COST
-    )
-    arrived = lax.ppermute(give, "section", [(0, 1), (1, 0)])
-    inner.near()
-    conv.near()
-    mlp.total()
-    inner.far()
-    conv.far()
-    mlp.join_row()
-    ends, means = call(
-        ends_kernel, "ends", (filled, own, arrived),
-        [shape(entering_tokens.shape, BF16), shape((micro_count * local_images, 1, LANES), F32)],
-        [pltpu.SemaphoreType.DMA((micro_count * local_images,))], hbm_outs=(0,), us=COST,
-    )
-    inner.total()
-    mlp.join_square()
-    conv.total()
-    inner.join_row()
-    conv.join_row()
-    mlp.join_cores()
-    conv.join_square()
-    inner.join_square()
-    narrower, widener = call(
-        mlp_end_kernel, "mlp_end", mlp.blocks, [tall, wide], leaving(2 * pieces), mb=12,
-        hbm_outs=(0, 1), us=COST,
-    )
-    inner.join_cores()
-    conv.join_cores()
-    attention, mixing, projector = call(
-        sent_end_kernel, "sent_end", inner.blocks,
-        [shape((width, 3 * width), F32), shape((width, width), F32), tall],
-        leaving(2 * pieces), mb=12, hbm_outs=(0, 1, 2), us=COST,
-    )
+    def swap_ends():
+        own, give = call(
+            give_kernel, "give",
+            (inside, middle, lit, feedforward_contract, contract_bias, grad_sent, early_low,
+             late_low, pointwise_enlarge),
+            [shape((rows, width), BF16)] * 2, mb=10, us=COST,
+        )
+        return own, lax.ppermute(give, "section", [(0, 1), (1, 0)])
+
+    def put_ends(own, arrived):
+        return call(
+            ends_kernel, "ends", (filled, own, arrived),
+            [shape(entering_tokens.shape, BF16), shape((1, local_images, micro_count), F32)],
+            [pltpu.SemaphoreType.DMA((micro_count * local_images,))], hbm_outs=(0,), us=COST,
+        )
+
+    def put_mlp():
+        return call(
+            mlp_end_kernel, "mlp_end", mlp.blocks, [tall, wide], leaving(2 * pieces), mb=12,
+            hbm_outs=(0, 1), us=COST,
+        )
+
+    def put_inner():
+        return call(
+            sent_end_kernel, "sent_end", inner.blocks,
+            [shape((width, 3 * width), F32), shape((width, width), F32), tall],
+            leaving(2 * pieces), mb=12, hbm_outs=(0, 1, 2), us=COST,
+        )
+
+    def put_conv():
+        return call(
+            conv_all_kernel, "conv_all", conv.blocks,
+            [wide, wide_line, shape((9, channels), F32), wide_line] + [line] * 7
+            + [wide_line, line],
+            [pltpu.VMEM((pieces * 8, LANES), F32)] + leaving(pieces), hbm_outs=(0,), us=COST,
+        )
+
+    done = {}
+    for step in ORDER:
+        name, _, what = step.partition(".")
+        if what:
+            getattr({"mlp": mlp, "inner": inner, "conv": conv}[name], what)()
+        elif name == "swap_ends":
+            done[name] = swap_ends()
+        elif name == "put_ends":
+            done[name] = put_ends(*done["swap_ends"])
+        else:
+            done[name] = {"put_mlp": put_mlp, "put_inner": put_inner, "put_conv": put_conv}[name]()
+    narrower, widener = done["put_mlp"]
+    attention, mixing, projector = done["put_inner"]
     (expander, upshift, depthwise, depthshift, postgain, postshift, pregain, preshift, mixshift,
-     midgain, midshift, wideshift, narrowshift) = call(
-        conv_all_kernel, "conv_all", conv.blocks,
-        [wide, wide_line, shape((9, channels), F32), wide_line] + [line] * 7 + [wide_line, line],
-        [pltpu.VMEM((pieces * 8, LANES), F32)] + leaving(pieces), hbm_outs=(0,), us=COST,
-    )
-    means = means[:, 0, 0].reshape(1, micro_count, local_images)
+     midgain, midshift, wideshift, narrowshift) = done["put_conv"]
+    ends, means = done["put_ends"]
+    means = jnp.transpose(means, (0, 2, 1))
     return (
         ends[None], means, expander, upshift, depthwise, depthshift, projector, postgain,
         postshift, pregain, preshift, attention, mixing, mixshift, midgain, midshift, widener,

time: 110 us -> 103 us (0.936)
  waiting for transfers between devices: 23.7 us -> 18.4 us
  Pallas kernels: 41.6 us -> 40.1 us
    ppermute x30, waiting for transfers between devices: 23.7 us -> 18.4 us  [swapped(): return lax.ppermute(value, BOTH, pairs)]
    pallas_call x33, Pallas kernels: 41.6 us -> 40.1 us  [__call__(): pl.pallas_call(body, out_shape=[shape((8, LANES), F32)] + outs, in_specs=...]
  transfers between devices with their start and end apart: 31 -> 31, of which waited for: 12 -> 14; matrix products, arithmetic and copies ran while one was open for 1% -> 0% of each run, Pallas kernels for 20% -> 22%
where the time goes in v2:
time: 103 us
  starting transfers between devices  42.3 us (41%)
  Pallas kernels  40.1 us (39%)
  waiting for transfers between devices  18.4 us (18%)
  between operations  1.28 us (1%)
  local copies, waits for them, and re-layouts  1.05 us (1%)
    ppermute x30, starting transfers between devices, swapped(): return lax.ppermute(value, BOTH, pairs)  41.2 us
    pallas_call x33, Pallas kernels, __call__(): pl.pallas_call(body, out_shape=[shape((8, LANES), F32)] + outs, in_specs=...  40.1 us
    ppermute x30, waiting for transfers between devices, swapped(): return lax.ppermute(value, BOTH, pairs)  18.4 us
  transfers between devices with their start and end apart: 31, of which 14 were waited for; matrix products, arithmetic and copies ran while one was open for 0% of the time, Pallas kernels for 22%

profile of v2, /device:TPU:1, one launch (start us, length us, event | category | flops | bytes accessed | tf_op | source)
XLA Modules:
  0.0 103.1 jit_solution(6261714174139190557)
XLA Ops:
  0.7 6.5 %conv_ahead.1 = (f32[8,128]{1,0:T(8,128)S(1)}, bf16[512,384]{1,0:T(8,128)(2,1)S(1)}, bf16[512,1536]{1,0:T(8,128)(2,1)S(1)}, bf16[512,1536]{1,0:T(8,128)(2,1)S(1)...) custom-call(s32[1,2,4]{2,1,0:T(2,128)} %bitcast.5, ...), custom_call_target="tpu_custom_call" | custom-call | flops 1 | bytes 1 | tf_op jit(solution)/shard_map/conv_ahead/pallas_call | solution.py:775
  7.3 3.0 %attend_ahead.1 = (f32[8,128]{1,0:T(8,128)S(1)}, bf16[512,1152]{1,0:T(8,128)(2,1)S(1)}, bf16[12,256,256]{2,1,0:T(8,128)(2,1)S(1)}, bf16[512,384]{1,0:T(8,128)(2,1)S(1)}, f32[512,384]{1,0:T(8,128)S(1)}) custom-call(f32[512,1]{1,0:T(8,128)S(1)} %get-tuple-element.140.refs_0_, bf16[512,384]{1,0:T(8,128)(2,1)S(1)} %get-tuple-element.141.refs_1_.refs_0_, ...), custom_call_target="tpu_custom_call" | custom-call | flops 1 | bytes 1 | tf_op jit(solution)/shard_map/attend_ahead/pallas_call | solution.py:775
  10.5 5.0 %mlp.1 = (f32[8,128]{1,0:T(8,128)S(1)}, bf16[512,1536]{1,0:T(8,128)(2,1)S(1)}, f32[512,384]{1,0:T(8,128)S(1)}, bf16[2,4,4,288,128]{4,3,2,1,0:T(8,128)(2,1)S(1)},...) custom-call(f32[512,1]{1,0:T(8,128)S(1)} %get-tuple-element.140.refs_0_, ...), custom_call_target="tpu_custom_call" | custom-call | flops 1 | bytes 1 | tf_op jit(solution)/shard_map/mlp/pallas_call | solution.py:775
  15.7 2.5 %heads_back.1 = (f32[8,128]{1,0:T(8,128)S(1)}, bf16[512,1152]{1,0:T(8,128)(2,1)S(1)}) custom-call(f32[512,384]{1,0:T(8,128)S(1)} %get-tuple-element.146.refs_0_.refs_1_, bf16[512,1152]{1,0:T(8,128)(2,1)S(1)} %get-tuple-element.147.refs_1_, bf16[12,256,256]{2,1,0:T(8,128)(2,1)S(1)} %get-tuple-element.148.refs_2_, bf16[384,384]{1,0:T(8,128)(2,1)S(1)} %copy-done.4, ...), custom_call_target="tpu_custom_call" | custom-call | flops 1 | bytes 1 | tf_op jit(solution)/shard_map/heads_back/pallas_call | solution.py:775
  18.7 2.6 %collective-permute-start.2 = (bf16[8,288,128]{2,1,0:T(8,128)(2,1)S(1)}, bf16[8,288,128]{2,1,0:T(8,128)(2,1)S(1)}, u32[]{:S(2)}, u32[]{:S(2)}) collective-permute-start(bf16[8,288,128]{2,1,0:T(8,128)(2,1)S(1)} %get-tuple-element.172), channel_id=1, source_target_pairs={{0,16},{1,3},{2,18},{3,1},{4,20},{5,7},{6,22},{7,5},{8,24},{9,11},... | collective-permute-start | bytes 1769480 | tf_op jit(solution)/shard_map/ppermute | solution.py:829
  21.3 3.4 %sent_back.1 = (f32[8,128]{1,0:T(8,128)S(1)}, bf16[512,384]{1,0:T(8,128)(2,1)S(1)}, bf16[512,384]{1,0:T(8,128)(2,1)S(1)}, bf16[2,4,4,288,128]{4,3,2,1,0:T(8,128)...) custom-call(bf16[512,384]{1,0:T(8,128)(2,1)S(1)} %get-tuple-element.141.refs_1_.refs_0_, ...), custom_call_target="tpu_custom_call" | custom-call | flops 1 | bytes 1 | tf_op jit(solution)/shard_map/sent_back/pallas_call | solution.py:775
  25.4 3.1 %conv_back.1 = (f32[8,128]{1,0:T(8,128)S(1)}, bf16[512,768]{1,0:T(8,128)(2,1)S(1)}, bf16[2,4,2,144,128]{4,3,2,1,0:T(8,128)(2,1)S(1)}, f32[16,1536]{1,0:T(8,128)S(1)}) custom-call(f32[512,1]{1,0:T(8,128)S(1)} %get-tuple-element.140.refs_0_, bf16[4,1,256,384]{3,2,1,0:T(8,128)(2,1)S(1)} %copy-done.1, bf16[512,384]{1,0:T(8,128)(2,1)S(1)} %get-tuple-element.159.refs_2_, ...), custom_call_target="tpu_custom_call" | custom-call | flops 1 | bytes 1 | tf_op jit(solution)/shard_map/conv_back/pallas_call | solution.py:775
  29.0 1.5 %collective-permute-start.4 = (bf16[4,288,128]{2,1,0:T(8,128)(2,1)S(1)}, bf16[4,288,128]{2,1,0:T(8,128)(2,1)S(1)}, u32[]{:S(2)}, u32[]{:S(2)}) collective-permute-start(bf16[4,288,128]{2,1,0:T(8,128)(2,1)S(1)} %get-tuple-element.180), channel_id=1, source_target_pairs={{0,2},{1,17},{2,0},{3,19},{4,6},{5,21},{6,4},{7,23},{8,10},{9,25},... | collective-permute-start | bytes 884744 | tf_op jit(solution)/shard_map/ppermute | solution.py:829
  30.8 1.3 %collective-permute-start.7 = (bf16[8,288,128]{2,1,0:T(8,128)(2,1)S(1)}, bf16[8,288,128]{2,1,0:T(8,128)(2,1)S(1)}, u32[]{:S(2)}, u32[]{:S(2)}) collective-permute-start(bf16[8,288,128]{2,1,0:T(8,128)(2,1)S(1)} %get-tuple-element.188), channel_id=1, source_target_pairs={{0,16},{1,3},{2,18},{3,1},{4,20},{5,7},{6,22},{7,5},{8,24},{9,11},... | collective-permute-start | bytes 1769480 | tf_op jit(solution)/shard_map/ppermute | solution.py:829
  32.1 3.5 %conv_end.1 = (f32[8,128]{1,0:T(8,128)S(1)}, bf16[512,768]{1,0:T(8,128)(2,1)S(1)}, bf16[2,4,4,160,128]{4,3,2,1,0:T(8,128)(2,1)S(1)}, bf16[4,4,160,128]{3,2,1,0:T(8,128)(2,1)S(1)}) custom-call(f32[512,1]{1,0:T(8,128)S(1)} %get-tuple-element.140.refs_0_, bf16[4,1,256,384]{3,2,1,0:T(8,128)(2,1)S(1)} %copy-done.1, ...), custom_call_target="tpu_custom_call" | custom-call | flops 1 | bytes 1 | tf_op jit(solution)/shard_map/conv_end/pallas_call | solution.py:775
  35.6 1.8 %collective-permute-start.3 = (bf16[4,4,160,128]{3,2,1,0:T(8,128)(2,1)S(1)}, bf16[4,4,160,128]{3,2,1,0:T(8,128)(2,1)S(1)}, u32[]{:S(2)}, u32[]{:S(2)}) collective-permute-start(bf16[4,4,160,128]{3,2,1,0:T(8,128)(2,1)S(1)} %get-tuple-element.178), channel_id=1, source_target_pairs={{0,1},{1,0},{2,3},{3,2},{4,5},{5,4},{6,7},{7,6},{8,9},{9,8},{10,11... | collective-permute-start | bytes 1966088 | tf_op jit(solution)/shard_map/ppermute | solution.py:829
  37.5 1.4 %collective-permute-start.6 = (bf16[2,288,128]{2,1,0:T(8,128)(2,1)S(1)}, bf16[2,288,128]{2,1,0:T(8,128)(2,1)S(1)}, u32[]{:S(2)}, u32[]{:S(2)}) collective-permute-start(bf16[2,288,128]{2,1,0:T(8,128)(2,1)S(1)} %get-tuple-element.186), channel_id=1, source_target_pairs={{0,4},{1,5},{2,6},{3,7},{4,0},{5,1},{6,2},{7,3},{8,12},{9,13},{10,... | collective-permute-start | bytes 442376 | tf_op jit(solution)/shard_map/ppermute | solution.py:829
  39.6 2.7 %collective-permute-done.7.refs_1_ = bf16[8,288,128]{2,1,0:T(8,128)(2,1)S(1)} collective-permute-done((bf16[8,288,128]{2,1,0:T(8,128)(2,1)S(1)}, bf16[8,288,128]{2,1,0:T(8,128)(2,1)S(1)}, u32[]{:S(2)}, u32[]{:S(2)}) %collective-permute-start.7) | collective-permute-done | bytes 589856 | tf_op jit(solution)/shard_map/ppermute | solution.py:829
  42.5 2.8 %collective-permute-start.9 = (bf16[2,288,128]{2,1,0:T(8,128)(2,1)S(1)}, bf16[2,288,128]{2,1,0:T(8,128)(2,1)S(1)}, u32[]{:S(2)}, u32[]{:S(2)}) collective-permute-start(bf16[2,288,128]{2,1,0:T(8,128)(2,1)S(1)} %get-tuple-element.195.refs_0_), channel_id=1, source_target_pairs={{0,8},{1,9},{2,10},{3,11},{4,12},{5,13},{6,14},{7,15},{8,0},{9,1},... | collective-permute-start | bytes 442376 | tf_op jit(solution)/shard_map/ppermute | solution.py:829
  47.9 1.8 %give.1 = (f32[8,128]{1,0:T(8,128)S(1)}, bf16[512,384]{1,0:T(8,128)(2,1)S(1)}, bf16[512,384]{1,0:T(8,128)(2,1)S(1)}) custom-call(f32[512,1]{1,0:T(8,128)S(1)} %get-tuple-element.140.refs_0_, f32[512,384]{1,0:T(8,128)S(1)} %copy-done.11, bf16[512,1536]{1,0:T(8,128)(2,1)S(1)} %get-tuple-element.145.refs_2_, bf16[1536,384]{1,0:T(8,128)(2,1)S(1)} %copy-done.7, ...), custom_call_target="tpu_custom_call" | custom-call | flops 30000001024 | bytes 1 | tf_op jit(solution)/shard_map/give/pallas_call | solution.py:775
  49.8 2.3 %collective-permute-done.11.refs_1_ = bf16[4,288,128]{2,1,0:T(8,128)(2,1)S(1)} collective-permute-done((bf16[4,288,128]{2,1,0:T(8,128)(2,1)S(1)}, bf16[4,288,128]{2,1,0:T(8,128)(2,1)S(1)}, u32[]{:S(2)}, u32[]{:S(2)}) %collective-permute-start.11) | collective-permute-done | bytes 294944 | tf_op jit(solution)/shard_map/ppermute | solution.py:829
  53.9 1.1 %collective-permute-start.13 = (bf16[2,160,128]{2,1,0:T(8,128)(2,1)S(1)}, bf16[2,160,128]{2,1,0:T(8,128)(2,1)S(1)}, u32[]{:S(2)}, u32[]{:S(2)}) collective-permute-start(bf16[2,160,128]{2,1,0:T(8,128)(2,1)S(1)} %get-tuple-element.205), channel_id=1, source_target_pairs={{0,4},{1,5},{2,6},{3,7},{4,0},{5,1},{6,2},{7,3},{8,12},{9,13},{10,... | collective-permute-start | bytes 245768 | tf_op jit(solution)/shard_map/ppermute | solution.py:829
  56.4 2.5 %collective-permute-start.16 = (bf16[2,288,128]{2,1,0:T(8,128)(2,1)S(1)}, bf16[2,288,128]{2,1,0:T(8,128)(2,1)S(1)}, u32[]{:S(2)}, u32[]{:S(2)}) collective-permute-start(bf16[2,288,128]{2,1,0:T(8,128)(2,1)S(1)} %get-tuple-element.215.refs_0_), channel_id=1, source_target_pairs={{0,8},{1,9},{2,10},{3,11},{4,12},{5,13},{6,14},{7,15},{8,0},{9,1},... | collective-permute-start | bytes 442376 | tf_op jit(solution)/shard_map/ppermute | solution.py:829
  59.7 1.8 %collective-permute-done.12.refs_1_ = bf16[2,288,128]{2,1,0:T(8,128)(2,1)S(1)} collective-permute-done((bf16[2,288,128]{2,1,0:T(8,128)(2,1)S(1)}, bf16[2,288,128]{2,1,0:T(8,128)(2,1)S(1)}, u32[]{:S(2)}, u32[]{:S(2)}) %collective-permute-start.12) | collective-permute-done | bytes 147488 | tf_op jit(solution)/shard_map/ppermute | solution.py:829
  61.7 1.5 %ends.1 = (f32[8,128]{1,0:T(8,128)S(1)}, bf16[4,1,256,384]{3,2,1,0:T(8,128)(2,1)}, f32[1,1,4]{2,1,0:T(1,128)}) custom-call(f32[4,128]{1,0:T(4,128)S(1)} %get-tuple-element.139.refs_0_, bf16[512,384]{1,0:T(8,128)(2,1)S(1)} %get-tuple-element.193.refs_1_, bf16[512,384]{1,0:T(8,128)(2,1)S(1)} %collective-permute-done.8.refs_2_, ...), custom_call_target="tpu_custom_call" | custom-call | flops 30000001024 | bytes 1 | tf_op jit(solution)/shard_map/ends/pallas_call | solution.py:775
  65.2 2.9 %collective-permute-done.19.refs_1_ = bf16[2,288,128]{2,1,0:T(8,128)(2,1)S(1)} collective-permute-done((bf16[2,288,128]{2,1,0:T(8,128)(2,1)S(1)}, bf16[2,288,128]{2,1,0:T(8,128)(2,1)S(1)}, u32[]{:S(2)}, u32[]{:S(2)}) %collective-permute-start.19) | collective-permute-done | bytes 147488 | tf_op jit(solution)/shard_map/ppermute | solution.py:829
  68.2 3.2 %collective-permute-start.21 = (bf16[4,288,128]{2,1,0:T(8,128)(2,1)S(1)}, bf16[4,288,128]{2,1,0:T(8,128)(2,1)S(1)}, u32[]{:S(2)}, u32[]{:S(2)}) collective-permute-start(bf16[4,288,128]{2,1,0:T(8,128)(2,1)S(1)} %get-tuple-element.225.refs_0_), channel_id=1, source_target_pairs={{0,2},{1,17},{2,0},{3,19},{4,6},{5,21},{6,4},{7,23},{8,10},{9,25},... | collective-permute-start | bytes 884744 | tf_op jit(solution)/shard_map/ppermute | solution.py:829
  71.4 1.4 %collective-permute-start.22 = (bf16[8,288,128]{2,1,0:T(8,128)(2,1)S(1)}, bf16[8,288,128]{2,1,0:T(8,128)(2,1)S(1)}, u32[]{:S(2)}, u32[]{:S(2)}) collective-permute-start(bf16[8,288,128]{2,1,0:T(8,128)(2,1)S(1)} %get-tuple-element.228.refs_0_), channel_id=1, source_target_pairs={{0,16},{1,3},{2,18},{3,1},{4,20},{5,7},{6,22},{7,5},{8,24},{9,11},... | collective-permute-start | bytes 1769480 | tf_op jit(solution)/shard_map/ppermute | solution.py:829
  73.0 5.8 %collective-permute-start.23 = (bf16[8,288,128]{2,1,0:T(8,128)(2,1)S(1)}, bf16[8,288,128]{2,1,0:T(8,128)(2,1)S(1)}, u32[]{:S(2)}, u32[]{:S(2)}) collective-permute-start(bf16[8,288,128]{2,1,0:T(8,128)(2,1)S(1)} %get-tuple-element.228.refs_0_), channel_id=1, source_target_pairs={{0,1},{1,0},{2,3},{3,2},{4,5},{5,4},{6,7},{7,6},{8,9},{9,8},{10,11... | collective-permute-start | bytes 1769480 | tf_op jit(solution)/shard_map/ppermute | solution.py:829
  78.9 5.3 %collective-permute-start.29 = (bf16[8,288,128]{2,1,0:T(8,128)(2,1)S(1)}, bf16[8,288,128]{2,1,0:T(8,128)(2,1)S(1)}, u32[]{:S(2)}, u32[]{:S(2)}) collective-permute-start(bf16[8,288,128]{2,1,0:T(8,128)(2,1)S(1)} %get-tuple-element.234.refs_0_), channel_id=1, source_target_pairs={{0,1},{1,0},{2,3},{3,2},{4,5},{5,4},{6,7},{7,6},{8,9},{9,8},{10,11... | collective-permute-start | bytes 1769480 | tf_op jit(solution)/shard_map/ppermute | solution.py:829
  84.2 1.3 %collective-permute-start.25 = (bf16[8,288,128]{2,1,0:T(8,128)(2,1)S(1)}, bf16[8,288,128]{2,1,0:T(8,128)(2,1)S(1)}, u32[]{:S(2)}, u32[]{:S(2)}) collective-permute-start(bf16[8,288,128]{2,1,0:T(8,128)(2,1)S(1)} %get-tuple-element.234.refs_0_), channel_id=1, source_target_pairs={{0,16},{1,3},{2,18},{3,1},{4,20},{5,7},{6,22},{7,5},{8,24},{9,11},... | collective-permute-start | bytes 1769480 | tf_op jit(solution)/shard_map/ppermute | solution.py:829
  85.5 1.7 %collective-permute-start.24 = (bf16[8,288,128]{2,1,0:T(8,128)(2,1)S(1)}, bf16[8,288,128]{2,1,0:T(8,128)(2,1)S(1)}, u32[]{:S(2)}, u32[]{:S(2)}) collective-permute-start(bf16[8,288,128]{2,1,0:T(8,128)(2,1)S(1)} %get-tuple-element.231.refs_1_), channel_id=1, source_target_pairs={{0,1},{1,0},{2,3},{3,2},{4,5},{5,4},{6,7},{7,6},{8,9},{9,8},{10,11... | collective-permute-start | bytes 1769480 | tf_op jit(solution)/shard_map/ppermute | solution.py:829
  88.8 2.8 %mlp_end.1 = (f32[8,128]{1,0:T(8,128)S(1)}, f32[1536,384]{1,0:T(8,128)}, f32[384,1536]{1,0:T(8,128)}) custom-call(bf16[8,288,128]{2,1,0:T(8,128)(2,1)S(1)} %get-tuple-element.228.refs_0_, bf16[8,288,128]{2,1,0:T(8,128)(2,1)S(1)} %get-tuple-element.231.refs_1_, bf16[8,288,128]{2,1,0:T(8,128)(2,1)S(1)} %collective-permute-done.23.refs_2_, ...), custom_call_target="tpu_custom_call" | custom-call | flops 1 | bytes 1 | tf_op jit(solution)/shard_map/mlp_end/pallas_call | solution.py:775
  91.6 1.5 %collective-permute-done.25.value = bf16[8,288,128]{2,1,0:T(8,128)(2,1)S(1)} collective-permute-done((bf16[8,288,128]{2,1,0:T(8,128)(2,1)S(1)}, bf16[8,288,128]{2,1,0:T(8,128)(2,1)S(1)}, u32[]{:S(2)}, u32[]{:S(2)}) %collective-permute-start.25) | collective-permute-done | bytes 589856 | tf_op jit(solution)/shard_map/ppermute | solution.py:829
  94.1 2.6 %collective-permute-done.26.value = bf16[8,160,128]{2,1,0:T(8,128)(2,1)S(1)} collective-permute-done((bf16[8,160,128]{2,1,0:T(8,128)(2,1)S(1)}, bf16[8,160,128]{2,1,0:T(8,128)(2,1)S(1)}, u32[]{:S(2)}, u32[]{:S(2)}) %collective-permute-start.26) | collective-permute-done | bytes 327712 | tf_op jit(solution)/shard_map/ppermute | solution.py:829
  97.6 2.8 %sent_end.1 = (f32[8,128]{1,0:T(8,128)S(1)}, f32[384,1152]{1,0:T(8,128)}, f32[384,384]{1,0:T(8,128)}, f32[1536,384]{1,0:T(8,128)}) custom-call(bf16[8,288,128]{2,1,0:T(8,128)(2,1)S(1)} %get-tuple-element.234.refs_0_, bf16[8,288,128]{2,1,0:T(8,128)(2,1)S(1)} %get-tuple-element.237.refs_1_, bf16[8,288,128]{2,1,0:T(8,128)(2,1)S(1)} %collective-permute-done.29.refs_2_, ...), custom_call_target="tpu_custom_call" | custom-call | flops 30000001024 | bytes 1 | tf_op jit(solution)/shard_map/sent_end/pallas_call | solution.py:775
  100.5 2.4 %conv_all.1 = (f32[8,128]{1,0:T(8,128)}, f32[384,1536]{1,0:T(8,128)}, f32[1536]{0:T(1024)}, f32[9,1536]{1,0:T(8,128)}, f32[1536]{0:T(1024)}, /*index=5*/f32[384]...) custom-call(bf16[8,160,128]{2,1,0:T(8,128)(2,1)S(1)} %get-tuple-elem, ...), custom_call_target="tpu_custom_call" | custom-call | flops 1 | bytes 1 | tf_op jit(solution)/shard_map/conv_all/pallas_call | solution.py:775
  (106 shorter events, 15.7 us)
Async XLA Ops:
  0.7 9.7 %copy-start.6 = (bf16[1536,384]{1,0:T(8,128)(2,1)S(1)}, bf16[1536,384]{1,0:T(8,128)(2,1)}, u32[]{:S(2)}) copy-start(bf16[1536,384]{1,0:T(8,128)(2,1)} %refs_3_.9) | copy-start | bytes 3538948
  15.5 2.9 %collective-permute-start = (bf16[4,4,288,128]{3,2,1,0:T(8,128)(2,1)S(1)}, bf16[4,4,288,128]{3,2,1,0:T(8,128)(2,1)S(1)}, u32[]{:S(2)}, u32[]{:S(2)}) collective-permute-start(bf16[4,4,288,128]{3,2,1,0:T(8,128)(2,1)S(1)} %get-tuple-element.155), channel_id=1, source_target_pairs={{0,1},{1,0},{2,3},{3,2},{4,5},{5,4},{6,7},{7,6},{8,9},{9,8},{10,11... | collective-permute-start | bytes 3538952 | tf_op jit(solution)/shard_map/ppermute | solution.py:829
  18.7 10.2 %collective-permute-start.2 = (bf16[8,288,128]{2,1,0:T(8,128)(2,1)S(1)}, bf16[8,288,128]{2,1,0:T(8,128)(2,1)S(1)}, u32[]{:S(2)}, u32[]{:S(2)}) collective-permute-start(bf16[8,288,128]{2,1,0:T(8,128)(2,1)S(1)} %get-tuple-element.172), channel_id=1, source_target_pairs={{0,16},{1,3},{2,18},{3,1},{4,20},{5,7},{6,22},{7,5},{8,24},{9,11},... | collective-permute-start | bytes 1769480 | tf_op jit(solution)/shard_map/ppermute | solution.py:829
  24.8 5.8 %collective-permute-start.1 = (bf16[4,4,288,128]{3,2,1,0:T(8,128)(2,1)S(1)}, bf16[4,4,288,128]{3,2,1,0:T(8,128)(2,1)S(1)}, u32[]{:S(2)}, u32[]{:S(2)}) collective-permute-start(bf16[4,4,288,128]{3,2,1,0:T(8,128)(2,1)S(1)} %get-tuple-element.170), channel_id=1, source_target_pairs={{0,1},{1,0},{2,3},{3,2},{4,5},{5,4},{6,7},{7,6},{8,9},{9,8},{10,11... | collective-permute-start | bytes 3538952 | tf_op jit(solution)/shard_map/ppermute | solution.py:829
  29.0 8.4 %collective-permute-start.4 = (bf16[4,288,128]{2,1,0:T(8,128)(2,1)S(1)}, bf16[4,288,128]{2,1,0:T(8,128)(2,1)S(1)}, u32[]{:S(2)}, u32[]{:S(2)}) collective-permute-start(bf16[4,288,128]{2,1,0:T(8,128)(2,1)S(1)} %get-tuple-element.180), channel_id=1, source_target_pairs={{0,2},{1,17},{2,0},{3,19},{4,6},{5,21},{6,4},{7,23},{8,10},{9,25},... | collective-permute-start | bytes 884744 | tf_op jit(solution)/shard_map/ppermute | solution.py:829
  30.8 11.5 %collective-permute-start.7 = (bf16[8,288,128]{2,1,0:T(8,128)(2,1)S(1)}, bf16[8,288,128]{2,1,0:T(8,128)(2,1)S(1)}, u32[]{:S(2)}, u32[]{:S(2)}) collective-permute-start(bf16[8,288,128]{2,1,0:T(8,128)(2,1)S(1)} %get-tuple-element.188), channel_id=1, source_target_pairs={{0,16},{1,3},{2,18},{3,1},{4,20},{5,7},{6,22},{7,5},{8,24},{9,11},... | collective-permute-start | bytes 1769480 | tf_op jit(solution)/shard_map/ppermute | solution.py:829
  35.6 3.5 %collective-permute-start.3 = (bf16[4,4,160,128]{3,2,1,0:T(8,128)(2,1)S(1)}, bf16[4,4,160,128]{3,2,1,0:T(8,128)(2,1)S(1)}, u32[]{:S(2)}, u32[]{:S(2)}) collective-permute-start(bf16[4,4,160,128]{3,2,1,0:T(8,128)(2,1)S(1)} %get-tuple-element.178), channel_id=1, source_target_pairs={{0,1},{1,0},{2,3},{3,2},{4,5},{5,4},{6,7},{7,6},{8,9},{9,8},{10,11... | collective-permute-start | bytes 1966088 | tf_op jit(solution)/shard_map/ppermute | solution.py:829
  37.5 5.0 %collective-permute-start.6 = (bf16[2,288,128]{2,1,0:T(8,128)(2,1)S(1)}, bf16[2,288,128]{2,1,0:T(8,128)(2,1)S(1)}, u32[]{:S(2)}, u32[]{:S(2)}) collective-permute-start(bf16[2,288,128]{2,1,0:T(8,128)(2,1)S(1)} %get-tuple-element.186), channel_id=1, source_target_pairs={{0,4},{1,5},{2,6},{3,7},{4,0},{5,1},{6,2},{7,3},{8,12},{9,13},{10,... | collective-permute-start | bytes 442376 | tf_op jit(solution)/shard_map/ppermute | solution.py:829
  39.3 6.8 %collective-permute-start.5 = (bf16[8,160,128]{2,1,0:T(8,128)(2,1)S(1)}, bf16[8,160,128]{2,1,0:T(8,128)(2,1)S(1)}, u32[]{:S(2)}, u32[]{:S(2)}) collective-permute-start(bf16[8,160,128]{2,1,0:T(8,128)(2,1)S(1)} %get-tuple-element.184), channel_id=1, source_target_pairs={{0,16},{1,3},{2,18},{3,1},{4,20},{5,7},{6,22},{7,5},{8,24},{9,11},... | collective-permute-start | bytes 983048 | tf_op jit(solution)/shard_map/ppermute | solution.py:829
  42.5 12.6 %collective-permute-start.9 = (bf16[2,288,128]{2,1,0:T(8,128)(2,1)S(1)}, bf16[2,288,128]{2,1,0:T(8,128)(2,1)S(1)}, u32[]{:S(2)}, u32[]{:S(2)}) collective-permute-start(bf16[2,288,128]{2,1,0:T(8,128)(2,1)S(1)} %get-tuple-element.195.refs_0_), channel_id=1, source_target_pairs={{0,8},{1,9},{2,10},{3,11},{4,12},{5,13},{6,14},{7,15},{8,0},{9,1},... | collective-permute-start | bytes 442376 | tf_op jit(solution)/shard_map/ppermute | solution.py:829
  45.3 6.8 %collective-permute-start.11 = (bf16[4,288,128]{2,1,0:T(8,128)(2,1)S(1)}, bf16[4,288,128]{2,1,0:T(8,128)(2,1)S(1)}, u32[]{:S(2)}, u32[]{:S(2)}) collective-permute-start(bf16[4,288,128]{2,1,0:T(8,128)(2,1)S(1)} %get-tuple-element.199), channel_id=1, source_target_pairs={{0,2},{1,17},{2,0},{3,19},{4,6},{5,21},{6,4},{7,23},{8,10},{9,25},... | collective-permute-start | bytes 884744 | tf_op jit(solution)/shard_map/ppermute | solution.py:829
  46.2 7.6 %collective-permute-start.10 = (bf16[4,160,128]{2,1,0:T(8,128)(2,1)S(1)}, bf16[4,160,128]{2,1,0:T(8,128)(2,1)S(1)}, u32[]{:S(2)}, u32[]{:S(2)}) collective-permute-start(bf16[4,160,128]{2,1,0:T(8,128)(2,1)S(1)} %get-tuple-element.197), channel_id=1, source_target_pairs={{0,2},{1,17},{2,0},{3,19},{4,6},{5,21},{6,4},{7,23},{8,10},{9,25},... | collective-permute-start | bytes 491528 | tf_op jit(solution)/shard_map/ppermute | solution.py:829
  52.2 4.2 %collective-permute-start.14 = (bf16[2,288,128]{2,1,0:T(8,128)(2,1)S(1)}, bf16[2,288,128]{2,1,0:T(8,128)(2,1)S(1)}, u32[]{:S(2)}, u32[]{:S(2)}) collective-permute-start(bf16[2,288,128]{2,1,0:T(8,128)(2,1)S(1)} %get-tuple-element.207), channel_id=1, source_target_pairs={{0,4},{1,5},{2,6},{3,7},{4,0},{5,1},{6,2},{7,3},{8,12},{9,13},{10,... | collective-permute-start | bytes 442376 | tf_op jit(solution)/shard_map/ppermute | solution.py:829
  52.6 9.0 %collective-permute-start.8 = (bf16[512,384]{1,0:T(8,128)(2,1)S(1)}, bf16[512,384]{1,0:T(8,128)(2,1)S(1)}, u32[]{:S(2)}, u32[]{:S(2)}) collective-permute-start(bf16[512,384]{1,0:T(8,128)(2,1)S(1)} %get-tuple-element.194), channel_id=1, source_target_pairs={{0,16},{16,0},{1,17},{17,1},{2,18},{18,2},{3,19},{19,3},{4,20},{20... | collective-permute-start | bytes 1179656 | tf_op jit(solution)/shard_map/ppermute | solution.py:1020
  53.9 5.0 %collective-permute-start.13 = (bf16[2,160,128]{2,1,0:T(8,128)(2,1)S(1)}, bf16[2,160,128]{2,1,0:T(8,128)(2,1)S(1)}, u32[]{:S(2)}, u32[]{:S(2)}) collective-permute-start(bf16[2,160,128]{2,1,0:T(8,128)(2,1)S(1)} %get-tuple-element.205), channel_id=1, source_target_pairs={{0,4},{1,5},{2,6},{3,7},{4,0},{5,1},{6,2},{7,3},{8,12},{9,13},{10,... | collective-permute-start | bytes 245768 | tf_op jit(solution)/shard_map/ppermute | solution.py:829
  55.1 6.5 %collective-permute-start.12 = (bf16[2,288,128]{2,1,0:T(8,128)(2,1)S(1)}, bf16[2,288,128]{2,1,0:T(8,128)(2,1)S(1)}, u32[]{:S(2)}, u32[]{:S(2)}) collective-permute-start(bf16[2,288,128]{2,1,0:T(8,128)(2,1)S(1)} %get-tuple-element.203.refs_0_), channel_id=1, source_target_pairs={{0,4},{1,5},{2,6},{3,7},{4,0},{5,1},{6,2},{7,3},{8,12},{9,13},{10,... | collective-permute-start | bytes 442376 | tf_op jit(solution)/shard_map/ppermute | solution.py:829
  56.4 6.7 %collective-permute-start.16 = (bf16[2,288,128]{2,1,0:T(8,128)(2,1)S(1)}, bf16[2,288,128]{2,1,0:T(8,128)(2,1)S(1)}, u32[]{:S(2)}, u32[]{:S(2)}) collective-permute-start(bf16[2,288,128]{2,1,0:T(8,128)(2,1)S(1)} %get-tuple-element.215.refs_0_), channel_id=1, source_target_pairs={{0,8},{1,9},{2,10},{3,11},{4,12},{5,13},{6,14},{7,15},{8,0},{9,1},... | collective-permute-start | bytes 442376 | tf_op jit(solution)/shard_map/ppermute | solution.py:829
  58.9 5.7 %collective-permute-start.15 = (bf16[2,160,128]{2,1,0:T(8,128)(2,1)S(1)}, bf16[2,160,128]{2,1,0:T(8,128)(2,1)S(1)}, u32[]{:S(2)}, u32[]{:S(2)}) collective-permute-start(bf16[2,160,128]{2,1,0:T(8,128)(2,1)S(1)} %get-tuple-element.214.refs_0_), channel_id=1, source_target_pairs={{0,8},{1,9},{2,10},{3,11},{4,12},{5,13},{6,14},{7,15},{8,0},{9,1},... | collective-permute-start | bytes 245768 | tf_op jit(solution)/shard_map/ppermute | solution.py:829
  61.6 9.8 %collective-permute-start.18 = (bf16[4,288,128]{2,1,0:T(8,128)(2,1)S(1)}, bf16[4,288,128]{2,1,0:T(8,128)(2,1)S(1)}, u32[]{:S(2)}, u32[]{:S(2)}) collective-permute-start(bf16[4,288,128]{2,1,0:T(8,128)(2,1)S(1)} %get-tuple-element.219.refs_0_), channel_id=1, source_target_pairs={{0,2},{1,17},{2,0},{3,19},{4,6},{5,21},{6,4},{7,23},{8,10},{9,25},... | collective-permute-start | bytes 884744 | tf_op jit(solution)/shard_map/ppermute | solution.py:829
  63.2 5.0 %collective-permute-start.19 = (bf16[2,288,128]{2,1,0:T(8,128)(2,1)S(1)}, bf16[2,288,128]{2,1,0:T(8,128)(2,1)S(1)}, u32[]{:S(2)}, u32[]{:S(2)}) collective-permute-start(bf16[2,288,128]{2,1,0:T(8,128)(2,1)S(1)} %get-tuple-element.220.refs_0_), channel_id=1, source_target_pairs={{0,4},{1,5},{2,6},{3,7},{4,0},{5,1},{6,2},{7,3},{8,12},{9,13},{10,... | collective-permute-start | bytes 442376 | tf_op jit(solution)/shard_map/ppermute | solution.py:829
  64.6 8.2 %collective-permute-start.17 = (bf16[2,160,128]{2,1,0:T(8,128)(2,1)S(1)}, bf16[2,160,128]{2,1,0:T(8,128)(2,1)S(1)}, u32[]{:S(2)}, u32[]{:S(2)}) collective-permute-start(bf16[2,160,128]{2,1,0:T(8,128)(2,1)S(1)} %get-tuple-element.218.refs_0_), channel_id=1, source_target_pairs={{0,4},{1,5},{2,6},{3,7},{4,0},{5,1},{6,2},{7,3},{8,12},{9,13},{10,... | collective-permute-start | bytes 245768 | tf_op jit(solution)/shard_map/ppermute | solution.py:829
  68.2 10.7 %collective-permute-start.21 = (bf16[4,288,128]{2,1,0:T(8,128)(2,1)S(1)}, bf16[4,288,128]{2,1,0:T(8,128)(2,1)S(1)}, u32[]{:S(2)}, u32[]{:S(2)}) collective-permute-start(bf16[4,288,128]{2,1,0:T(8,128)(2,1)S(1)} %get-tuple-element.225.refs_0_), channel_id=1, source_target_pairs={{0,2},{1,17},{2,0},{3,19},{4,6},{5,21},{6,4},{7,23},{8,10},{9,25},... | collective-permute-start | bytes 884744 | tf_op jit(solution)/shard_map/ppermute | solution.py:829
  71.4 14.1 %collective-permute-start.22 = (bf16[8,288,128]{2,1,0:T(8,128)(2,1)S(1)}, bf16[8,288,128]{2,1,0:T(8,128)(2,1)S(1)}, u32[]{:S(2)}, u32[]{:S(2)}) collective-permute-start(bf16[8,288,128]{2,1,0:T(8,128)(2,1)S(1)} %get-tuple-element.228.refs_0_), channel_id=1, source_target_pairs={{0,16},{1,3},{2,18},{3,1},{4,20},{5,7},{6,22},{7,5},{8,24},{9,11},... | collective-permute-start | bytes 1769480 | tf_op jit(solution)/shard_map/ppermute | solution.py:829
  72.8 14.4 %collective-permute-start.20 = (bf16[4,160,128]{2,1,0:T(8,128)(2,1)S(1)}, bf16[4,160,128]{2,1,0:T(8,128)(2,1)S(1)}, u32[]{:S(2)}, u32[]{:S(2)}) collective-permute-start(bf16[4,160,128]{2,1,0:T(8,128)(2,1)S(1)} %get-tuple-element.224.refs_0_), channel_id=1, source_target_pairs={{0,2},{1,17},{2,0},{3,19},{4,6},{5,21},{6,4},{7,23},{8,10},{9,25},... | collective-permute-start | bytes 491528 | tf_op jit(solution)/shard_map/ppermute | solution.py:829
  73.0 14.3 %collective-permute-start.23 = (bf16[8,288,128]{2,1,0:T(8,128)(2,1)S(1)}, bf16[8,288,128]{2,1,0:T(8,128)(2,1)S(1)}, u32[]{:S(2)}, u32[]{:S(2)}) collective-permute-start(bf16[8,288,128]{2,1,0:T(8,128)(2,1)S(1)} %get-tuple-element.228.refs_0_), channel_id=1, source_target_pairs={{0,1},{1,0},{2,3},{3,2},{4,5},{5,4},{6,7},{7,6},{8,9},{9,8},{10,11... | collective-permute-start | bytes 1769480 | tf_op jit(solution)/shard_map/ppermute | solution.py:829
  78.9 18.8 %collective-permute-start.29 = (bf16[8,288,128]{2,1,0:T(8,128)(2,1)S(1)}, bf16[8,288,128]{2,1,0:T(8,128)(2,1)S(1)}, u32[]{:S(2)}, u32[]{:S(2)}) collective-permute-start(bf16[8,288,128]{2,1,0:T(8,128)(2,1)S(1)} %get-tuple-element.234.refs_0_), channel_id=1, source_target_pairs={{0,1},{1,0},{2,3},{3,2},{4,5},{5,4},{6,7},{7,6},{8,9},{9,8},{10,11... | collective-permute-start | bytes 1769480 | tf_op jit(solution)/shard_map/ppermute | solution.py:829
  84.2 9.0 %collective-permute-start.25 = (bf16[8,288,128]{2,1,0:T(8,128)(2,1)S(1)}, bf16[8,288,128]{2,1,0:T(8,128)(2,1)S(1)}, u32[]{:S(2)}, u32[]{:S(2)}) collective-permute-start(bf16[8,288,128]{2,1,0:T(8,128)(2,1)S(1)} %get-tuple-element.234.refs_0_), channel_id=1, source_target_pairs={{0,16},{1,3},{2,18},{3,1},{4,20},{5,7},{6,22},{7,5},{8,24},{9,11},... | collective-permute-start | bytes 1769480 | tf_op jit(solution)/shard_map/ppermute | solution.py:829
  85.5 3.3 %collective-permute-start.24 = (bf16[8,288,128]{2,1,0:T(8,128)(2,1)S(1)}, bf16[8,288,128]{2,1,0:T(8,128)(2,1)S(1)}, u32[]{:S(2)}, u32[]{:S(2)}) collective-permute-start(bf16[8,288,128]{2,1,0:T(8,128)(2,1)S(1)} %get-tuple-element.231.refs_1_), channel_id=1, source_target_pairs={{0,1},{1,0},{2,3},{3,2},{4,5},{5,4},{6,7},{7,6},{8,9},{9,8},{10,11... | collective-permute-start | bytes 1769480 | tf_op jit(solution)/shard_map/ppermute | solution.py:829
  87.2 13.3 %collective-permute-start.27 = (bf16[8,160,128]{2,1,0:T(8,128)(2,1)S(1)}, bf16[8,160,128]{2,1,0:T(8,128)(2,1)S(1)}, u32[]{:S(2)}, u32[]{:S(2)}) collective-permute-start(bf16[8,160,128]{2,1,0:T(8,128)(2,1)S(1)} %get-tuple-element.230.refs_0_), channel_id=1, source_target_pairs={{0,1},{1,0},{2,3},{3,2},{4,5},{5,4},{6,7},{7,6},{8,9},{9,8},{10,11... | collective-permute-start | bytes 983048 | tf_op jit(solution)/shard_map/ppermute | solution.py:829
  87.3 9.4 %collective-permute-start.26 = (bf16[8,160,128]{2,1,0:T(8,128)(2,1)S(1)}, bf16[8,160,128]{2,1,0:T(8,128)(2,1)S(1)}, u32[]{:S(2)}, u32[]{:S(2)}) collective-permute-start(bf16[8,160,128]{2,1,0:T(8,128)(2,1)S(1)} %get-tuple-element.230.refs_0_), channel_id=1, source_target_pairs={{0,16},{1,3},{2,18},{3,1},{4,20},{5,7},{6,22},{7,5},{8,24},{9,11},... | collective-permute-start | bytes 983048 | tf_op jit(solution)/shard_map/ppermute | solution.py:829
  93.2 4.5 %collective-permute-start.30 = (bf16[8,288,128]{2,1,0:T(8,128)(2,1)S(1)}, bf16[8,288,128]{2,1,0:T(8,128)(2,1)S(1)}, u32[]{:S(2)}, u32[]{:S(2)}) collective-permute-start(bf16[8,288,128]{2,1,0:T(8,128)(2,1)S(1)} %get-tuple-element.237.refs_1_), channel_id=1, source_target_pairs={{0,1},{1,0},{2,3},{3,2},{4,5},{5,4},{6,7},{7,6},{8,9},{9,8},{10,11... | collective-permute-start | bytes 1769480 | tf_op jit(solution)/shard_map/ppermute | solution.py:829
  96.7 3.8 %collective-permute-start.28 = (bf16[8,160,128]{2,1,0:T(8,128)(2,1)S(1)}, bf16[8,160,128]{2,1,0:T(8,128)(2,1)S(1)}, u32[]{:S(2)}, u32[]{:S(2)}) collective-permute-start(bf16[8,160,128]{2,1,0:T(8,128)(2,1)S(1)} %get-tuple-element.236.refs_1_), channel_id=1, source_target_pairs={{0,1},{1,0},{2,3},{3,2},{4,5},{5,4},{6,7},{7,6},{8,9},{9,8},{10,11... | collective-permute-start | bytes 983048 | tf_op jit(solution)/shard_map/ppermute | solution.py:829
  (19 other events, 82.5 us)

commit v3 on v2

--- a/solution.py
+++ b/solution.py
@@ -729,7 +729,6 @@
 WHOLE = pl.BlockSpec(memory_space=pltpu.VMEM)
 ANYWHERE = pl.BlockSpec(memory_space=pl.ANY)
 REMOTE = pl.BlockSpec(memory_space=pltpu.HBM)
-SCALARS = pl.BlockSpec(memory_space=pltpu.SMEM)
 COST = 30
 ORDER = (
     "mlp.near", "conv.first", "inner.second", "mlp.far", "conv.second", "swap_ends", "inner.near",
@@ -739,9 +738,9 @@
     "put_inner", "put_conv",
 )
 COSTS = {
-    "conv_first": 0, "conv_second": 30, "conv_far": 0, "conv_join_square": 30, "give": 30,
+    "conv_first": 0, "conv_second": 30, "conv_far": 0, "conv_join_square": 30, "give": 0,
     "mlp_cores": 0, "conv_cores": 30, "conv_all": 0, "inner_cores": 30, "conv_total": 30,
-    "inner_join_square": 0, "mlp_end": 0, "mlp_far": 0, "conv_near": 0,
+    "inner_join_square": 0, "mlp_end": 0, "mlp_far": 0, "conv_near": 30, "mlp_total": 0,
 }
 BOTH = ("section", "dp")
 
@@ -754,10 +753,9 @@
     def __init__(self):
         self.last = None
 
-    def __call__(self, kernel, name, ins, outs, scratch=(), mb=8, us=0, smem=(), hbm=(), hbm_outs=(), aliases={}):
+    def __call__(self, kernel, name, ins, outs, scratch=(), mb=8, us=0, hbm=(), hbm_outs=()):
         count = len(ins)
         after = () if self.last is None else (self.last,)
-
 
         def body(*refs):
             token = refs[count + len(after)]
@@ -776,14 +774,13 @@
             body,
             out_shape=[shape((8, LANES), F32)] + outs,
             in_specs=[
-                SCALARS if place in smem else REMOTE if place in hbm else WHOLE
+                REMOTE if place in hbm else WHOLE
                 for place in range(count)
             ]
             + [ANYWHERE] * len(after),
             out_specs=[WHOLE]
             + [REMOTE if place in hbm_outs else WHOLE for place in range(len(outs))],
             scratch_shapes=list(scratch),
-            input_output_aliases={place: out + 1 for place, out in aliases.items()},
             cost_estimate=pl.CostEstimate(
                 flops=1 + int(COSTS.get(name, us) * 1e9), bytes_accessed=1, transcendentals=0
             ),

time: 103 us -> 103 us (level)
  no operation moved by 1% of the time
where the time goes in v3:
time: 103 us
  starting transfers between devices  42.2 us (41%)
  Pallas kernels  40.1 us (39%)
  waiting for transfers between devices  18.3 us (18%)
  between operations  1.28 us (1%)
  local copies, waits for them, and re-layouts  1.04 us (1%)
    ppermute x30, starting transfers between devices, swapped(): return lax.ppermute(value, BOTH, pairs)  41.2 us
    pallas_call x33, Pallas kernels, __call__(): pl.pallas_call(body, out_shape=[shape((8, LANES), F32)] + outs, in_specs=...  40.1 us
    ppermute x30, waiting for transfers between devices, swapped(): return lax.ppermute(value, BOTH, pairs)  18.3 us
  transfers between devices with their start and end apart: 31, of which 14 were waited for; matrix products, arithmetic and copies ran while one was open for 0% of the time, Pallas kernels for 22%

profile of v3, /device:TPU:1, one launch (start us, length us, event | category | flops | bytes accessed | tf_op | source)
XLA Modules:
  0.0 103.0 jit_solution(9830104510477648816)
XLA Ops:
  0.7 6.5 %conv_ahead.1 = (f32[8,128]{1,0:T(8,128)S(1)}, bf16[512,384]{1,0:T(8,128)(2,1)S(1)}, bf16[512,1536]{1,0:T(8,128)(2,1)S(1)}, bf16[512,1536]{1,0:T(8,128)(2,1)S(1)...) custom-call(s32[1,2,4]{2,1,0:T(2,128)} %bitcast.5, ...), custom_call_target="tpu_custom_call" | custom-call | flops 1 | bytes 1 | tf_op jit(solution)/shard_map/conv_ahead/pallas_call | solution.py:773
  7.3 3.1 %attend_ahead.1 = (f32[8,128]{1,0:T(8,128)S(1)}, bf16[512,1152]{1,0:T(8,128)(2,1)S(1)}, bf16[12,256,256]{2,1,0:T(8,128)(2,1)S(1)}, bf16[512,384]{1,0:T(8,128)(2,1)S(1)}, f32[512,384]{1,0:T(8,128)S(1)}) custom-call(f32[512,1]{1,0:T(8,128)S(1)} %get-tuple-element.140.refs_0_, bf16[512,384]{1,0:T(8,128)(2,1)S(1)} %get-tuple-element.141.refs_1_.refs_0_, ...), custom_call_target="tpu_custom_call" | custom-call | flops 1 | bytes 1 | tf_op jit(solution)/shard_map/attend_ahead/pallas_call | solution.py:773
  10.5 5.0 %mlp.1 = (f32[8,128]{1,0:T(8,128)S(1)}, bf16[512,1536]{1,0:T(8,128)(2,1)S(1)}, f32[512,384]{1,0:T(8,128)S(1)}, bf16[2,4,4,288,128]{4,3,2,1,0:T(8,128)(2,1)S(1)},...) custom-call(f32[512,1]{1,0:T(8,128)S(1)} %get-tuple-element.140.refs_0_, ...), custom_call_target="tpu_custom_call" | custom-call | flops 1 | bytes 1 | tf_op jit(solution)/shard_map/mlp/pallas_call | solution.py:773
  15.7 2.5 %heads_back.1 = (f32[8,128]{1,0:T(8,128)S(1)}, bf16[512,1152]{1,0:T(8,128)(2,1)S(1)}) custom-call(f32[512,384]{1,0:T(8,128)S(1)} %get-tuple-element.146.refs_0_.refs_1_, bf16[512,1152]{1,0:T(8,128)(2,1)S(1)} %get-tuple-element.147.refs_1_, bf16[12,256,256]{2,1,0:T(8,128)(2,1)S(1)} %get-tuple-element.148.refs_2_, bf16[384,384]{1,0:T(8,128)(2,1)S(1)} %copy-done.8, ...), custom_call_target="tpu_custom_call" | custom-call | flops 1 | bytes 1 | tf_op jit(solution)/shard_map/heads_back/pallas_call | solution.py:773
  18.7 2.6 %collective-permute-start.2 = (bf16[8,288,128]{2,1,0:T(8,128)(2,1)S(1)}, bf16[8,288,128]{2,1,0:T(8,128)(2,1)S(1)}, u32[]{:S(2)}, u32[]{:S(2)}) collective-permute-start(bf16[8,288,128]{2,1,0:T(8,128)(2,1)S(1)} %get-tuple-element.172), channel_id=1, source_target_pairs={{0,16},{1,3},{2,18},{3,1},{4,20},{5,7},{6,22},{7,5},{8,24},{9,11},... | collective-permute-start | bytes 1769480 | tf_op jit(solution)/shard_map/ppermute | solution.py:826
  21.3 3.4 %sent_back.1 = (f32[8,128]{1,0:T(8,128)S(1)}, bf16[512,384]{1,0:T(8,128)(2,1)S(1)}, bf16[512,384]{1,0:T(8,128)(2,1)S(1)}, bf16[2,4,4,288,128]{4,3,2,1,0:T(8,128)...) custom-call(bf16[512,384]{1,0:T(8,128)(2,1)S(1)} %get-tuple-element.141.refs_1_.refs_0_, ...), custom_call_target="tpu_custom_call" | custom-call | flops 1 | bytes 1 | tf_op jit(solution)/shard_map/sent_back/pallas_call | solution.py:773
  25.4 3.1 %conv_back.1 = (f32[8,128]{1,0:T(8,128)S(1)}, bf16[512,768]{1,0:T(8,128)(2,1)S(1)}, bf16[2,4,2,144,128]{4,3,2,1,0:T(8,128)(2,1)S(1)}, f32[16,1536]{1,0:T(8,128)S(1)}) custom-call(f32[512,1]{1,0:T(8,128)S(1)} %get-tuple-element.140.refs_0_, bf16[4,1,256,384]{3,2,1,0:T(8,128)(2,1)S(1)} %copy-done.1, bf16[512,384]{1,0:T(8,128)(2,1)S(1)} %get-tuple-element.159.refs_2_, ...), custom_call_target="tpu_custom_call" | custom-call | flops 1 | bytes 1 | tf_op jit(solution)/shard_map/conv_back/pallas_call | solution.py:773
  29.0 1.5 %collective-permute-start.4 = (bf16[4,288,128]{2,1,0:T(8,128)(2,1)S(1)}, bf16[4,288,128]{2,1,0:T(8,128)(2,1)S(1)}, u32[]{:S(2)}, u32[]{:S(2)}) collective-permute-start(bf16[4,288,128]{2,1,0:T(8,128)(2,1)S(1)} %get-tuple-element.180), channel_id=1, source_target_pairs={{0,2},{1,17},{2,0},{3,19},{4,6},{5,21},{6,4},{7,23},{8,10},{9,25},... | collective-permute-start | bytes 884744 | tf_op jit(solution)/shard_map/ppermute | solution.py:826
  30.8 1.3 %collective-permute-start.7 = (bf16[8,288,128]{2,1,0:T(8,128)(2,1)S(1)}, bf16[8,288,128]{2,1,0:T(8,128)(2,1)S(1)}, u32[]{:S(2)}, u32[]{:S(2)}) collective-permute-start(bf16[8,288,128]{2,1,0:T(8,128)(2,1)S(1)} %get-tuple-element.188), channel_id=1, source_target_pairs={{0,16},{1,3},{2,18},{3,1},{4,20},{5,7},{6,22},{7,5},{8,24},{9,11},... | collective-permute-start | bytes 1769480 | tf_op jit(solution)/shard_map/ppermute | solution.py:826
  32.1 3.5 %conv_end.1 = (f32[8,128]{1,0:T(8,128)S(1)}, bf16[512,768]{1,0:T(8,128)(2,1)S(1)}, bf16[2,4,4,160,128]{4,3,2,1,0:T(8,128)(2,1)S(1)}, bf16[4,4,160,128]{3,2,1,0:T(8,128)(2,1)S(1)}) custom-call(f32[512,1]{1,0:T(8,128)S(1)} %get-tuple-element.140.refs_0_, bf16[4,1,256,384]{3,2,1,0:T(8,128)(2,1)S(1)} %copy-done.1, ...), custom_call_target="tpu_custom_call" | custom-call | flops 1 | bytes 1 | tf_op jit(solution)/shard_map/conv_end/pallas_call | solution.py:773
  35.6 1.8 %collective-permute-start.3 = (bf16[4,4,160,128]{3,2,1,0:T(8,128)(2,1)S(1)}, bf16[4,4,160,128]{3,2,1,0:T(8,128)(2,1)S(1)}, u32[]{:S(2)}, u32[]{:S(2)}) collective-permute-start(bf16[4,4,160,128]{3,2,1,0:T(8,128)(2,1)S(1)} %get-tuple-element.178), channel_id=1, source_target_pairs={{0,1},{1,0},{2,3},{3,2},{4,5},{5,4},{6,7},{7,6},{8,9},{9,8},{10,11... | collective-permute-start | bytes 1966088 | tf_op jit(solution)/shard_map/ppermute | solution.py:826
  37.5 1.4 %collective-permute-start.6 = (bf16[2,288,128]{2,1,0:T(8,128)(2,1)S(1)}, bf16[2,288,128]{2,1,0:T(8,128)(2,1)S(1)}, u32[]{:S(2)}, u32[]{:S(2)}) collective-permute-start(bf16[2,288,128]{2,1,0:T(8,128)(2,1)S(1)} %get-tuple-element.186), channel_id=1, source_target_pairs={{0,4},{1,5},{2,6},{3,7},{4,0},{5,1},{6,2},{7,3},{8,12},{9,13},{10,... | collective-permute-start | bytes 442376 | tf_op jit(solution)/shard_map/ppermute | solution.py:826
  39.6 2.7 %collective-permute-done.7.refs_1_ = bf16[8,288,128]{2,1,0:T(8,128)(2,1)S(1)} collective-permute-done((bf16[8,288,128]{2,1,0:T(8,128)(2,1)S(1)}, bf16[8,288,128]{2,1,0:T(8,128)(2,1)S(1)}, u32[]{:S(2)}, u32[]{:S(2)}) %collective-permute-start.7) | collective-permute-done | bytes 589856 | tf_op jit(solution)/shard_map/ppermute | solution.py:826
  42.5 2.8 %collective-permute-start.9 = (bf16[2,288,128]{2,1,0:T(8,128)(2,1)S(1)}, bf16[2,288,128]{2,1,0:T(8,128)(2,1)S(1)}, u32[]{:S(2)}, u32[]{:S(2)}) collective-permute-start(bf16[2,288,128]{2,1,0:T(8,128)(2,1)S(1)} %get-tuple-element.195.refs_0_), channel_id=1, source_target_pairs={{0,8},{1,9},{2,10},{3,11},{4,12},{5,13},{6,14},{7,15},{8,0},{9,1},... | collective-permute-start | bytes 442376 | tf_op jit(solution)/shard_map/ppermute | solution.py:826
  47.9 1.8 %give.1 = (f32[8,128]{1,0:T(8,128)S(1)}, bf16[512,384]{1,0:T(8,128)(2,1)S(1)}, bf16[512,384]{1,0:T(8,128)(2,1)S(1)}) custom-call(f32[512,1]{1,0:T(8,128)S(1)} %get-tuple-element.140.refs_0_, f32[512,384]{1,0:T(8,128)S(1)} %copy-done.7, bf16[512,1536]{1,0:T(8,128)(2,1)S(1)} %get-tuple-element.145.refs_2_, bf16[1536,384]{1,0:T(8,128)(2,1)S(1)} %copy-done.4, ...), custom_call_target="tpu_custom_call" | custom-call | flops 1 | bytes 1 | tf_op jit(solution)/shard_map/give/pallas_call | solution.py:773
  49.7 2.4 %collective-permute-done.11.refs_1_ = bf16[4,288,128]{2,1,0:T(8,128)(2,1)S(1)} collective-permute-done((bf16[4,288,128]{2,1,0:T(8,128)(2,1)S(1)}, bf16[4,288,128]{2,1,0:T(8,128)(2,1)S(1)}, u32[]{:S(2)}, u32[]{:S(2)}) %collective-permute-start.11) | collective-permute-done | bytes 294944 | tf_op jit(solution)/shard_map/ppermute | solution.py:826
  56.4 2.4 %collective-permute-start.16 = (bf16[2,288,128]{2,1,0:T(8,128)(2,1)S(1)}, bf16[2,288,128]{2,1,0:T(8,128)(2,1)S(1)}, u32[]{:S(2)}, u32[]{:S(2)}) collective-permute-start(bf16[2,288,128]{2,1,0:T(8,128)(2,1)S(1)} %get-tuple-element.215.refs_0_), channel_id=1, source_target_pairs={{0,8},{1,9},{2,10},{3,11},{4,12},{5,13},{6,14},{7,15},{8,0},{9,1},... | collective-permute-start | bytes 442376 | tf_op jit(solution)/shard_map/ppermute | solution.py:826
  59.7 1.8 %collective-permute-done.12.refs_1_ = bf16[2,288,128]{2,1,0:T(8,128)(2,1)S(1)} collective-permute-done((bf16[2,288,128]{2,1,0:T(8,128)(2,1)S(1)}, bf16[2,288,128]{2,1,0:T(8,128)(2,1)S(1)}, u32[]{:S(2)}, u32[]{:S(2)}) %collective-permute-start.12) | collective-permute-done | bytes 147488 | tf_op jit(solution)/shard_map/ppermute | solution.py:826
  61.6 1.5 %ends.1 = (f32[8,128]{1,0:T(8,128)S(1)}, bf16[4,1,256,384]{3,2,1,0:T(8,128)(2,1)}, f32[1,1,4]{2,1,0:T(1,128)}) custom-call(f32[4,128]{1,0:T(4,128)S(1)} %get-tuple-element.139.refs_0_, bf16[512,384]{1,0:T(8,128)(2,1)S(1)} %get-tuple-element.193.refs_1_, bf16[512,384]{1,0:T(8,128)(2,1)S(1)} %collective-permute-done.8.refs_2_, ...), custom_call_target="tpu_custom_call" | custom-call | flops 30000001024 | bytes 1 | tf_op jit(solution)/shard_map/ends/pallas_call | solution.py:773
  65.2 2.9 %collective-permute-done.19.refs_1_ = bf16[2,288,128]{2,1,0:T(8,128)(2,1)S(1)} collective-permute-done((bf16[2,288,128]{2,1,0:T(8,128)(2,1)S(1)}, bf16[2,288,128]{2,1,0:T(8,128)(2,1)S(1)}, u32[]{:S(2)}, u32[]{:S(2)}) %collective-permute-start.19) | collective-permute-done | bytes 147488 | tf_op jit(solution)/shard_map/ppermute | solution.py:826
  68.1 3.2 %collective-permute-start.21 = (bf16[4,288,128]{2,1,0:T(8,128)(2,1)S(1)}, bf16[4,288,128]{2,1,0:T(8,128)(2,1)S(1)}, u32[]{:S(2)}, u32[]{:S(2)}) collective-permute-start(bf16[4,288,128]{2,1,0:T(8,128)(2,1)S(1)} %get-tuple-element.225.refs_0_), channel_id=1, source_target_pairs={{0,2},{1,17},{2,0},{3,19},{4,6},{5,21},{6,4},{7,23},{8,10},{9,25},... | collective-permute-start | bytes 884744 | tf_op jit(solution)/shard_map/ppermute | solution.py:826
  71.3 1.3 %collective-permute-start.22 = (bf16[8,288,128]{2,1,0:T(8,128)(2,1)S(1)}, bf16[8,288,128]{2,1,0:T(8,128)(2,1)S(1)}, u32[]{:S(2)}, u32[]{:S(2)}) collective-permute-start(bf16[8,288,128]{2,1,0:T(8,128)(2,1)S(1)} %get-tuple-element.228.refs_0_), channel_id=1, source_target_pairs={{0,16},{1,3},{2,18},{3,1},{4,20},{5,7},{6,22},{7,5},{8,24},{9,11},... | collective-permute-start | bytes 1769480 | tf_op jit(solution)/shard_map/ppermute | solution.py:826
  73.0 5.8 %collective-permute-start.23 = (bf16[8,288,128]{2,1,0:T(8,128)(2,1)S(1)}, bf16[8,288,128]{2,1,0:T(8,128)(2,1)S(1)}, u32[]{:S(2)}, u32[]{:S(2)}) collective-permute-start(bf16[8,288,128]{2,1,0:T(8,128)(2,1)S(1)} %get-tuple-element.228.refs_0_), channel_id=1, source_target_pairs={{0,1},{1,0},{2,3},{3,2},{4,5},{5,4},{6,7},{7,6},{8,9},{9,8},{10,11... | collective-permute-start | bytes 1769480 | tf_op jit(solution)/shard_map/ppermute | solution.py:826
  78.9 5.2 %collective-permute-start.29 = (bf16[8,288,128]{2,1,0:T(8,128)(2,1)S(1)}, bf16[8,288,128]{2,1,0:T(8,128)(2,1)S(1)}, u32[]{:S(2)}, u32[]{:S(2)}) collective-permute-start(bf16[8,288,128]{2,1,0:T(8,128)(2,1)S(1)} %get-tuple-element.234.refs_0_), channel_id=1, source_target_pairs={{0,1},{1,0},{2,3},{3,2},{4,5},{5,4},{6,7},{7,6},{8,9},{9,8},{10,11... | collective-permute-start | bytes 1769480 | tf_op jit(solution)/shard_map/ppermute | solution.py:826
  84.1 1.2 %collective-permute-start.25 = (bf16[8,288,128]{2,1,0:T(8,128)(2,1)S(1)}, bf16[8,288,128]{2,1,0:T(8,128)(2,1)S(1)}, u32[]{:S(2)}, u32[]{:S(2)}) collective-permute-start(bf16[8,288,128]{2,1,0:T(8,128)(2,1)S(1)} %get-tuple-element.234.refs_0_), channel_id=1, source_target_pairs={{0,16},{1,3},{2,18},{3,1},{4,20},{5,7},{6,22},{7,5},{8,24},{9,11},... | collective-permute-start | bytes 1769480 | tf_op jit(solution)/shard_map/ppermute | solution.py:826
  85.3 2.0 %collective-permute-start.24 = (bf16[8,288,128]{2,1,0:T(8,128)(2,1)S(1)}, bf16[8,288,128]{2,1,0:T(8,128)(2,1)S(1)}, u32[]{:S(2)}, u32[]{:S(2)}) collective-permute-start(bf16[8,288,128]{2,1,0:T(8,128)(2,1)S(1)} %get-tuple-element.231.refs_1_), channel_id=1, source_target_pairs={{0,1},{1,0},{2,3},{3,2},{4,5},{5,4},{6,7},{7,6},{8,9},{9,8},{10,11... | collective-permute-start | bytes 1769480 | tf_op jit(solution)/shard_map/ppermute | solution.py:826
  87.8 1.2 %collective-permute-done.24.refs_3_ = bf16[8,288,128]{2,1,0:T(8,128)(2,1)S(1)} collective-permute-done((bf16[8,288,128]{2,1,0:T(8,128)(2,1)S(1)}, bf16[8,288,128]{2,1,0:T(8,128)(2,1)S(1)}, u32[]{:S(2)}, u32[]{:S(2)}) %collective-permute-start.24) | collective-permute-done | bytes 589856 | tf_op jit(solution)/shard_map/ppermute | solution.py:826
  89.0 2.8 %mlp_end.1 = (f32[8,128]{1,0:T(8,128)S(1)}, f32[1536,384]{1,0:T(8,128)}, f32[384,1536]{1,0:T(8,128)}) custom-call(bf16[8,288,128]{2,1,0:T(8,128)(2,1)S(1)} %get-tuple-element.228.refs_0_, bf16[8,288,128]{2,1,0:T(8,128)(2,1)S(1)} %get-tuple-element.231.refs_1_, bf16[8,288,128]{2,1,0:T(8,128)(2,1)S(1)} %collective-permute-done.23.refs_2_, ...), custom_call_target="tpu_custom_call" | custom-call | flops 1 | bytes 1 | tf_op jit(solution)/shard_map/mlp_end/pallas_call | solution.py:773
  91.8 1.3 %collective-permute-done.25.value = bf16[8,288,128]{2,1,0:T(8,128)(2,1)S(1)} collective-permute-done((bf16[8,288,128]{2,1,0:T(8,128)(2,1)S(1)}, bf16[8,288,128]{2,1,0:T(8,128)(2,1)S(1)}, u32[]{:S(2)}, u32[]{:S(2)}) %collective-permute-start.25) | collective-permute-done | bytes 589856 | tf_op jit(solution)/shard_map/ppermute | solution.py:826
  94.0 2.6 %collective-permute-done.26.value = bf16[8,160,128]{2,1,0:T(8,128)(2,1)S(1)} collective-permute-done((bf16[8,160,128]{2,1,0:T(8,128)(2,1)S(1)}, bf16[8,160,128]{2,1,0:T(8,128)(2,1)S(1)}, u32[]{:S(2)}, u32[]{:S(2)}) %collective-permute-start.26) | collective-permute-done | bytes 327712 | tf_op jit(solution)/shard_map/ppermute | solution.py:826
  97.6 2.8 %sent_end.1 = (f32[8,128]{1,0:T(8,128)S(1)}, f32[384,1152]{1,0:T(8,128)}, f32[384,384]{1,0:T(8,128)}, f32[1536,384]{1,0:T(8,128)}) custom-call(bf16[8,288,128]{2,1,0:T(8,128)(2,1)S(1)} %get-tuple-element.234.refs_0_, bf16[8,288,128]{2,1,0:T(8,128)(2,1)S(1)} %get-tuple-element.237.refs_1_, bf16[8,288,128]{2,1,0:T(8,128)(2,1)S(1)} %collective-permute-done.29.refs_2_, ...), custom_call_target="tpu_custom_call" | custom-call | flops 30000001024 | bytes 1 | tf_op jit(solution)/shard_map/sent_end/pallas_call | solution.py:773
  100.4 2.4 %conv_all.1 = (f32[8,128]{1,0:T(8,128)}, f32[384,1536]{1,0:T(8,128)}, f32[1536]{0:T(1024)}, f32[9,1536]{1,0:T(8,128)}, f32[1536]{0:T(1024)}, /*index=5*/f32[384]...) custom-call(bf16[8,160,128]{2,1,0:T(8,128)(2,1)S(1)} %get-tuple-elem, ...), custom_call_target="tpu_custom_call" | custom-call | flops 1 | bytes 1 | tf_op jit(solution)/shard_map/conv_all/pallas_call | solution.py:773
  (106 shorter events, 15.7 us)
Async XLA Ops:
  0.7 9.7 %copy-start.9 = (bf16[384,1536]{1,0:T(8,128)(2,1)S(1)}, bf16[384,1536]{1,0:T(8,128)(2,1)}, u32[]{:S(2)}) copy-start(bf16[384,1536]{1,0:T(8,128)(2,1)} %refs_5_.7) | copy-start | bytes 3538948
  15.5 2.9 %collective-permute-start = (bf16[4,4,288,128]{3,2,1,0:T(8,128)(2,1)S(1)}, bf16[4,4,288,128]{3,2,1,0:T(8,128)(2,1)S(1)}, u32[]{:S(2)}, u32[]{:S(2)}) collective-permute-start(bf16[4,4,288,128]{3,2,1,0:T(8,128)(2,1)S(1)} %get-tuple-element.155), channel_id=1, source_target_pairs={{0,1},{1,0},{2,3},{3,2},{4,5},{5,4},{6,7},{7,6},{8,9},{9,8},{10,11... | collective-permute-start | bytes 3538952 | tf_op jit(solution)/shard_map/ppermute | solution.py:826
  18.7 10.2 %collective-permute-start.2 = (bf16[8,288,128]{2,1,0:T(8,128)(2,1)S(1)}, bf16[8,288,128]{2,1,0:T(8,128)(2,1)S(1)}, u32[]{:S(2)}, u32[]{:S(2)}) collective-permute-start(bf16[8,288,128]{2,1,0:T(8,128)(2,1)S(1)} %get-tuple-element.172), channel_id=1, source_target_pairs={{0,16},{1,3},{2,18},{3,1},{4,20},{5,7},{6,22},{7,5},{8,24},{9,11},... | collective-permute-start | bytes 1769480 | tf_op jit(solution)/shard_map/ppermute | solution.py:826
  24.7 5.7 %collective-permute-start.1 = (bf16[4,4,288,128]{3,2,1,0:T(8,128)(2,1)S(1)}, bf16[4,4,288,128]{3,2,1,0:T(8,128)(2,1)S(1)}, u32[]{:S(2)}, u32[]{:S(2)}) collective-permute-start(bf16[4,4,288,128]{3,2,1,0:T(8,128)(2,1)S(1)} %get-tuple-element.170), channel_id=1, source_target_pairs={{0,1},{1,0},{2,3},{3,2},{4,5},{5,4},{6,7},{7,6},{8,9},{9,8},{10,11... | collective-permute-start | bytes 3538952 | tf_op jit(solution)/shard_map/ppermute | solution.py:826
  29.0 8.4 %collective-permute-start.4 = (bf16[4,288,128]{2,1,0:T(8,128)(2,1)S(1)}, bf16[4,288,128]{2,1,0:T(8,128)(2,1)S(1)}, u32[]{:S(2)}, u32[]{:S(2)}) collective-permute-start(bf16[4,288,128]{2,1,0:T(8,128)(2,1)S(1)} %get-tuple-element.180), channel_id=1, source_target_pairs={{0,2},{1,17},{2,0},{3,19},{4,6},{5,21},{6,4},{7,23},{8,10},{9,25},... | collective-permute-start | bytes 884744 | tf_op jit(solution)/shard_map/ppermute | solution.py:826
  30.8 11.5 %collective-permute-start.7 = (bf16[8,288,128]{2,1,0:T(8,128)(2,1)S(1)}, bf16[8,288,128]{2,1,0:T(8,128)(2,1)S(1)}, u32[]{:S(2)}, u32[]{:S(2)}) collective-permute-start(bf16[8,288,128]{2,1,0:T(8,128)(2,1)S(1)} %get-tuple-element.188), channel_id=1, source_target_pairs={{0,16},{1,3},{2,18},{3,1},{4,20},{5,7},{6,22},{7,5},{8,24},{9,11},... | collective-permute-start | bytes 1769480 | tf_op jit(solution)/shard_map/ppermute | solution.py:826
  35.6 3.5 %collective-permute-start.3 = (bf16[4,4,160,128]{3,2,1,0:T(8,128)(2,1)S(1)}, bf16[4,4,160,128]{3,2,1,0:T(8,128)(2,1)S(1)}, u32[]{:S(2)}, u32[]{:S(2)}) collective-permute-start(bf16[4,4,160,128]{3,2,1,0:T(8,128)(2,1)S(1)} %get-tuple-element.178), channel_id=1, source_target_pairs={{0,1},{1,0},{2,3},{3,2},{4,5},{5,4},{6,7},{7,6},{8,9},{9,8},{10,11... | collective-permute-start | bytes 1966088 | tf_op jit(solution)/shard_map/ppermute | solution.py:826
  37.5 4.9 %collective-permute-start.6 = (bf16[2,288,128]{2,1,0:T(8,128)(2,1)S(1)}, bf16[2,288,128]{2,1,0:T(8,128)(2,1)S(1)}, u32[]{:S(2)}, u32[]{:S(2)}) collective-permute-start(bf16[2,288,128]{2,1,0:T(8,128)(2,1)S(1)} %get-tuple-element.186), channel_id=1, source_target_pairs={{0,4},{1,5},{2,6},{3,7},{4,0},{5,1},{6,2},{7,3},{8,12},{9,13},{10,... | collective-permute-start | bytes 442376 | tf_op jit(solution)/shard_map/ppermute | solution.py:826
  39.3 6.8 %collective-permute-start.5 = (bf16[8,160,128]{2,1,0:T(8,128)(2,1)S(1)}, bf16[8,160,128]{2,1,0:T(8,128)(2,1)S(1)}, u32[]{:S(2)}, u32[]{:S(2)}) collective-permute-start(bf16[8,160,128]{2,1,0:T(8,128)(2,1)S(1)} %get-tuple-element.184), channel_id=1, source_target_pairs={{0,16},{1,3},{2,18},{3,1},{4,20},{5,7},{6,22},{7,5},{8,24},{9,11},... | collective-permute-start | bytes 983048 | tf_op jit(solution)/shard_map/ppermute | solution.py:826
  42.5 12.5 %collective-permute-start.9 = (bf16[2,288,128]{2,1,0:T(8,128)(2,1)S(1)}, bf16[2,288,128]{2,1,0:T(8,128)(2,1)S(1)}, u32[]{:S(2)}, u32[]{:S(2)}) collective-permute-start(bf16[2,288,128]{2,1,0:T(8,128)(2,1)S(1)} %get-tuple-element.195.refs_0_), channel_id=1, source_target_pairs={{0,8},{1,9},{2,10},{3,11},{4,12},{5,13},{6,14},{7,15},{8,0},{9,1},... | collective-permute-start | bytes 442376 | tf_op jit(solution)/shard_map/ppermute | solution.py:826
  45.3 6.8 %collective-permute-start.11 = (bf16[4,288,128]{2,1,0:T(8,128)(2,1)S(1)}, bf16[4,288,128]{2,1,0:T(8,128)(2,1)S(1)}, u32[]{:S(2)}, u32[]{:S(2)}) collective-permute-start(bf16[4,288,128]{2,1,0:T(8,128)(2,1)S(1)} %get-tuple-element.199), channel_id=1, source_target_pairs={{0,2},{1,17},{2,0},{3,19},{4,6},{5,21},{6,4},{7,23},{8,10},{9,25},... | collective-permute-start | bytes 884744 | tf_op jit(solution)/shard_map/ppermute | solution.py:826
  46.2 7.7 %collective-permute-start.10 = (bf16[4,160,128]{2,1,0:T(8,128)(2,1)S(1)}, bf16[4,160,128]{2,1,0:T(8,128)(2,1)S(1)}, u32[]{:S(2)}, u32[]{:S(2)}) collective-permute-start(bf16[4,160,128]{2,1,0:T(8,128)(2,1)S(1)} %get-tuple-element.197), channel_id=1, source_target_pairs={{0,2},{1,17},{2,0},{3,19},{4,6},{5,21},{6,4},{7,23},{8,10},{9,25},... | collective-permute-start | bytes 491528 | tf_op jit(solution)/shard_map/ppermute | solution.py:826
  52.2 4.2 %collective-permute-start.14 = (bf16[2,288,128]{2,1,0:T(8,128)(2,1)S(1)}, bf16[2,288,128]{2,1,0:T(8,128)(2,1)S(1)}, u32[]{:S(2)}, u32[]{:S(2)}) collective-permute-start(bf16[2,288,128]{2,1,0:T(8,128)(2,1)S(1)} %get-tuple-element.207), channel_id=1, source_target_pairs={{0,4},{1,5},{2,6},{3,7},{4,0},{5,1},{6,2},{7,3},{8,12},{9,13},{10,... | collective-permute-start | bytes 442376 | tf_op jit(solution)/shard_map/ppermute | solution.py:826
  52.6 9.0 %collective-permute-start.8 = (bf16[512,384]{1,0:T(8,128)(2,1)S(1)}, bf16[512,384]{1,0:T(8,128)(2,1)S(1)}, u32[]{:S(2)}, u32[]{:S(2)}) collective-permute-start(bf16[512,384]{1,0:T(8,128)(2,1)S(1)} %get-tuple-element.194), channel_id=1, source_target_pairs={{0,16},{16,0},{1,17},{17,1},{2,18},{18,2},{3,19},{19,3},{4,20},{20... | collective-permute-start | bytes 1179656 | tf_op jit(solution)/shard_map/ppermute | solution.py:1017
  53.9 5.0 %collective-permute-start.13 = (bf16[2,160,128]{2,1,0:T(8,128)(2,1)S(1)}, bf16[2,160,128]{2,1,0:T(8,128)(2,1)S(1)}, u32[]{:S(2)}, u32[]{:S(2)}) collective-permute-start(bf16[2,160,128]{2,1,0:T(8,128)(2,1)S(1)} %get-tuple-element.205), channel_id=1, source_target_pairs={{0,4},{1,5},{2,6},{3,7},{4,0},{5,1},{6,2},{7,3},{8,12},{9,13},{10,... | collective-permute-start | bytes 245768 | tf_op jit(solution)/shard_map/ppermute | solution.py:826
  55.0 6.5 %collective-permute-start.12 = (bf16[2,288,128]{2,1,0:T(8,128)(2,1)S(1)}, bf16[2,288,128]{2,1,0:T(8,128)(2,1)S(1)}, u32[]{:S(2)}, u32[]{:S(2)}) collective-permute-start(bf16[2,288,128]{2,1,0:T(8,128)(2,1)S(1)} %get-tuple-element.203.refs_0_), channel_id=1, source_target_pairs={{0,4},{1,5},{2,6},{3,7},{4,0},{5,1},{6,2},{7,3},{8,12},{9,13},{10,... | collective-permute-start | bytes 442376 | tf_op jit(solution)/shard_map/ppermute | solution.py:826
  56.4 6.7 %collective-permute-start.16 = (bf16[2,288,128]{2,1,0:T(8,128)(2,1)S(1)}, bf16[2,288,128]{2,1,0:T(8,128)(2,1)S(1)}, u32[]{:S(2)}, u32[]{:S(2)}) collective-permute-start(bf16[2,288,128]{2,1,0:T(8,128)(2,1)S(1)} %get-tuple-element.215.refs_0_), channel_id=1, source_target_pairs={{0,8},{1,9},{2,10},{3,11},{4,12},{5,13},{6,14},{7,15},{8,0},{9,1},... | collective-permute-start | bytes 442376 | tf_op jit(solution)/shard_map/ppermute | solution.py:826
  58.9 5.7 %collective-permute-start.15 = (bf16[2,160,128]{2,1,0:T(8,128)(2,1)S(1)}, bf16[2,160,128]{2,1,0:T(8,128)(2,1)S(1)}, u32[]{:S(2)}, u32[]{:S(2)}) collective-permute-start(bf16[2,160,128]{2,1,0:T(8,128)(2,1)S(1)} %get-tuple-element.214.refs_0_), channel_id=1, source_target_pairs={{0,8},{1,9},{2,10},{3,11},{4,12},{5,13},{6,14},{7,15},{8,0},{9,1},... | collective-permute-start | bytes 245768 | tf_op jit(solution)/shard_map/ppermute | solution.py:826
  61.5 9.7 %collective-permute-start.18 = (bf16[4,288,128]{2,1,0:T(8,128)(2,1)S(1)}, bf16[4,288,128]{2,1,0:T(8,128)(2,1)S(1)}, u32[]{:S(2)}, u32[]{:S(2)}) collective-permute-start(bf16[4,288,128]{2,1,0:T(8,128)(2,1)S(1)} %get-tuple-element.219.refs_0_), channel_id=1, source_target_pairs={{0,2},{1,17},{2,0},{3,19},{4,6},{5,21},{6,4},{7,23},{8,10},{9,25},... | collective-permute-start | bytes 884744 | tf_op jit(solution)/shard_map/ppermute | solution.py:826
  63.1 4.9 %collective-permute-start.19 = (bf16[2,288,128]{2,1,0:T(8,128)(2,1)S(1)}, bf16[2,288,128]{2,1,0:T(8,128)(2,1)S(1)}, u32[]{:S(2)}, u32[]{:S(2)}) collective-permute-start(bf16[2,288,128]{2,1,0:T(8,128)(2,1)S(1)} %get-tuple-element.220.refs_0_), channel_id=1, source_target_pairs={{0,4},{1,5},{2,6},{3,7},{4,0},{5,1},{6,2},{7,3},{8,12},{9,13},{10,... | collective-permute-start | bytes 442376 | tf_op jit(solution)/shard_map/ppermute | solution.py:826
  64.6 8.0 %collective-permute-start.17 = (bf16[2,160,128]{2,1,0:T(8,128)(2,1)S(1)}, bf16[2,160,128]{2,1,0:T(8,128)(2,1)S(1)}, u32[]{:S(2)}, u32[]{:S(2)}) collective-permute-start(bf16[2,160,128]{2,1,0:T(8,128)(2,1)S(1)} %get-tuple-element.218.refs_0_), channel_id=1, source_target_pairs={{0,4},{1,5},{2,6},{3,7},{4,0},{5,1},{6,2},{7,3},{8,12},{9,13},{10,... | collective-permute-start | bytes 245768 | tf_op jit(solution)/shard_map/ppermute | solution.py:826
  68.1 10.7 %collective-permute-start.21 = (bf16[4,288,128]{2,1,0:T(8,128)(2,1)S(1)}, bf16[4,288,128]{2,1,0:T(8,128)(2,1)S(1)}, u32[]{:S(2)}, u32[]{:S(2)}) collective-permute-start(bf16[4,288,128]{2,1,0:T(8,128)(2,1)S(1)} %get-tuple-element.225.refs_0_), channel_id=1, source_target_pairs={{0,2},{1,17},{2,0},{3,19},{4,6},{5,21},{6,4},{7,23},{8,10},{9,25},... | collective-permute-start | bytes 884744 | tf_op jit(solution)/shard_map/ppermute | solution.py:826
  71.3 14.0 %collective-permute-start.22 = (bf16[8,288,128]{2,1,0:T(8,128)(2,1)S(1)}, bf16[8,288,128]{2,1,0:T(8,128)(2,1)S(1)}, u32[]{:S(2)}, u32[]{:S(2)}) collective-permute-start(bf16[8,288,128]{2,1,0:T(8,128)(2,1)S(1)} %get-tuple-element.228.refs_0_), channel_id=1, source_target_pairs={{0,16},{1,3},{2,18},{3,1},{4,20},{5,7},{6,22},{7,5},{8,24},{9,11},... | collective-permute-start | bytes 1769480 | tf_op jit(solution)/shard_map/ppermute | solution.py:826
  72.6 14.7 %collective-permute-start.20 = (bf16[4,160,128]{2,1,0:T(8,128)(2,1)S(1)}, bf16[4,160,128]{2,1,0:T(8,128)(2,1)S(1)}, u32[]{:S(2)}, u32[]{:S(2)}) collective-permute-start(bf16[4,160,128]{2,1,0:T(8,128)(2,1)S(1)} %get-tuple-element.224.refs_0_), channel_id=1, source_target_pairs={{0,2},{1,17},{2,0},{3,19},{4,6},{5,21},{6,4},{7,23},{8,10},{9,25},... | collective-permute-start | bytes 491528 | tf_op jit(solution)/shard_map/ppermute | solution.py:826
  73.0 14.5 %collective-permute-start.23 = (bf16[8,288,128]{2,1,0:T(8,128)(2,1)S(1)}, bf16[8,288,128]{2,1,0:T(8,128)(2,1)S(1)}, u32[]{:S(2)}, u32[]{:S(2)}) collective-permute-start(bf16[8,288,128]{2,1,0:T(8,128)(2,1)S(1)} %get-tuple-element.228.refs_0_), channel_id=1, source_target_pairs={{0,1},{1,0},{2,3},{3,2},{4,5},{5,4},{6,7},{7,6},{8,9},{9,8},{10,11... | collective-permute-start | bytes 1769480 | tf_op jit(solution)/shard_map/ppermute | solution.py:826
  78.9 18.7 %collective-permute-start.29 = (bf16[8,288,128]{2,1,0:T(8,128)(2,1)S(1)}, bf16[8,288,128]{2,1,0:T(8,128)(2,1)S(1)}, u32[]{:S(2)}, u32[]{:S(2)}) collective-permute-start(bf16[8,288,128]{2,1,0:T(8,128)(2,1)S(1)} %get-tuple-element.234.refs_0_), channel_id=1, source_target_pairs={{0,1},{1,0},{2,3},{3,2},{4,5},{5,4},{6,7},{7,6},{8,9},{9,8},{10,11... | collective-permute-start | bytes 1769480 | tf_op jit(solution)/shard_map/ppermute | solution.py:826
  84.1 9.0 %collective-permute-start.25 = (bf16[8,288,128]{2,1,0:T(8,128)(2,1)S(1)}, bf16[8,288,128]{2,1,0:T(8,128)(2,1)S(1)}, u32[]{:S(2)}, u32[]{:S(2)}) collective-permute-start(bf16[8,288,128]{2,1,0:T(8,128)(2,1)S(1)} %get-tuple-element.234.refs_0_), channel_id=1, source_target_pairs={{0,16},{1,3},{2,18},{3,1},{4,20},{5,7},{6,22},{7,5},{8,24},{9,11},... | collective-permute-start | bytes 1769480 | tf_op jit(solution)/shard_map/ppermute | solution.py:826
  85.3 3.7 %collective-permute-start.24 = (bf16[8,288,128]{2,1,0:T(8,128)(2,1)S(1)}, bf16[8,288,128]{2,1,0:T(8,128)(2,1)S(1)}, u32[]{:S(2)}, u32[]{:S(2)}) collective-permute-start(bf16[8,288,128]{2,1,0:T(8,128)(2,1)S(1)} %get-tuple-element.231.refs_1_), channel_id=1, source_target_pairs={{0,1},{1,0},{2,3},{3,2},{4,5},{5,4},{6,7},{7,6},{8,9},{9,8},{10,11... | collective-permute-start | bytes 1769480 | tf_op jit(solution)/shard_map/ppermute | solution.py:826
  87.4 13.0 %collective-permute-start.27 = (bf16[8,160,128]{2,1,0:T(8,128)(2,1)S(1)}, bf16[8,160,128]{2,1,0:T(8,128)(2,1)S(1)}, u32[]{:S(2)}, u32[]{:S(2)}) collective-permute-start(bf16[8,160,128]{2,1,0:T(8,128)(2,1)S(1)} %get-tuple-element.230.refs_0_), channel_id=1, source_target_pairs={{0,1},{1,0},{2,3},{3,2},{4,5},{5,4},{6,7},{7,6},{8,9},{9,8},{10,11... | collective-permute-start | bytes 983048 | tf_op jit(solution)/shard_map/ppermute | solution.py:826
  87.5 9.2 %collective-permute-start.26 = (bf16[8,160,128]{2,1,0:T(8,128)(2,1)S(1)}, bf16[8,160,128]{2,1,0:T(8,128)(2,1)S(1)}, u32[]{:S(2)}, u32[]{:S(2)}) collective-permute-start(bf16[8,160,128]{2,1,0:T(8,128)(2,1)S(1)} %get-tuple-element.230.refs_0_), channel_id=1, source_target_pairs={{0,16},{1,3},{2,18},{3,1},{4,20},{5,7},{6,22},{7,5},{8,24},{9,11},... | collective-permute-start | bytes 983048 | tf_op jit(solution)/shard_map/ppermute | solution.py:826
  93.1 4.5 %collective-permute-start.30 = (bf16[8,288,128]{2,1,0:T(8,128)(2,1)S(1)}, bf16[8,288,128]{2,1,0:T(8,128)(2,1)S(1)}, u32[]{:S(2)}, u32[]{:S(2)}) collective-permute-start(bf16[8,288,128]{2,1,0:T(8,128)(2,1)S(1)} %get-tuple-element.237.refs_1_), channel_id=1, source_target_pairs={{0,1},{1,0},{2,3},{3,2},{4,5},{5,4},{6,7},{7,6},{8,9},{9,8},{10,11... | collective-permute-start | bytes 1769480 | tf_op jit(solution)/shard_map/ppermute | solution.py:826
  96.6 3.8 %collective-permute-start.28 = (bf16[8,160,128]{2,1,0:T(8,128)(2,1)S(1)}, bf16[8,160,128]{2,1,0:T(8,128)(2,1)S(1)}, u32[]{:S(2)}, u32[]{:S(2)}) collective-permute-start(bf16[8,160,128]{2,1,0:T(8,128)(2,1)S(1)} %get-tuple-element.236.refs_1_), channel_id=1, source_target_pairs={{0,1},{1,0},{2,3},{3,2},{4,5},{5,4},{6,7},{7,6},{8,9},{9,8},{10,11... | collective-permute-start | bytes 983048 | tf_op jit(solution)/shard_map/ppermute | solution.py:826
  (19 other events, 82.6 us)
